TPU v7x, 32 devices: a whole 2x2x4 slice. The times are simulated.
32 devices in a mesh: dp: 8 (over z, x), seq: 4 (over y, core).
Axes of the slice: x: 2, y: 2, z: 4, core: 2. Of those that a mesh axis runs over, the one named last changes fastest.
Arguments:
- block_in: bfloat16 [16, 768, 768], P('dp', 'seq'), may hold values from -6 to 6
- cotangent: bfloat16 [16, 768, 768], P('dp', 'seq'), may hold values from -6 to 6
- labels: int32 [16], P('dp'), may hold values 0 or 1
- master: float32 [2, 768, 9216], P(None, 'dp', 'seq'), may hold values from -8 to 8
- small_params: float32 [2, 9984], replicated, may hold values from -2 to 3
- row_state: float32 [2, 4, 768], P(None, None, 'dp')
- col_state: float32 [2, 9216], P(None, 'seq')
- small_state: float32 [2, 9984], replicated
Outputs:
- block_out: bfloat16 [16, 768, 768], P('dp', 'seq')
- input_grad: float32 [16, 768, 768], P('dp', 'seq')
- example_norms: float32 [16], P('dp')
- influence: float32 [16], P('dp')
- weight_grads: float32 [2, 768, 9216], P(None, 'dp', 'seq')
- fresh_row_moments: float32 [2, 4, 768], P(None, None, 'dp')
- col_stats: float32 [2, 9216], P(None, 'seq')
- new_master: float32 [2, 768, 9216], P(None, 'dp', 'seq')
- new_low: bfloat16 [2, 768, 9216], P(None, 'dp', 'seq')
- small_grads: float32 [2, 9984], replicated
- small_moments: float32 [2, 9984], replicated
- small_new: float32 [2, 9984], replicated
All inputs are finite; a program needn't handle non-finite values. No bound on the sum of `labels` on one device may be relied on, other than what follows from the above.
Results may differ from a plain program's by a relative error of at most 0.022.
Values may be sent and summed in bfloat16 or wider, within the bound.
No kernel may reach another device: no remote copies, remote signals or barrier semaphores. Data moves between devices by JAX's collectives and lax.ppermute only.
A program may use at most 256 MiB of HBM per device.

v0:
```python
import jax
import jax.numpy as jnp
from jax import lax
from jax.sharding import PartitionSpec as P

D = 768
HEADS = 12
FF = 3072
L = 768
LAYERS = 2
HEAD_DIM = 64
ROT = 16
SMALL = 9984


EPS_NORM = 1e-05
EPS_SQUARE = 1e-30
RATE = 0.5
DECAY = 0.5
NEG_LARGE = -1e30
HIGH_ACCURACY = lax.Precision.HIGHEST
CONTRACT_LAST = (((1,), (1,)), ((), ()))
CONTRACT_FIRST = (((0,), (0,)), ((), ()))


def unpack(vector):
    return jnp.split(vector, [D, 2 * D, 3 * D, 4 * D, 7 * D, 8 * D, 8 * D + FF], axis=-1)


def apply_layer_norm(inputs):
    centred = inputs - jnp.mean(inputs, axis=-1, keepdims=True)
    variance = jnp.mean(centred * centred, axis=-1, keepdims=True)
    inverse = lax.rsqrt(variance + EPS_NORM)
    return (centred * inverse, inverse)


def norm_back(grad_normed, scaled, inverse, gain_vec):
    grad_scaled = grad_normed * gain_vec
    mean_grad = jnp.mean(grad_scaled, axis=-1, keepdims=True)
    mean_cross = jnp.mean(grad_scaled * scaled, axis=-1, keepdims=True)
    return (grad_scaled - mean_grad - scaled * mean_cross) * inverse


def rotary_tables(positions):
    halfway = ROT // 2
    frequency = 10000.0 ** (-2.0 * jnp.arange(halfway, dtype=jnp.float32) / ROT)
    angles = positions.astype(jnp.float32)[:, None] * frequency[None, :]
    angles = jnp.concatenate([angles, angles], axis=-1)
    return (jnp.cos(angles), jnp.sin(angles))


def rotate(values, cosine_table, sine_table):
    turned = values[..., :ROT]
    passed = values[..., ROT:]
    front_half = turned[..., : ROT // 2]
    back_half = turned[..., ROT // 2 :]
    swapped = jnp.concatenate([-back_half, front_half], axis=-1)
    turned = turned * cosine_table[:, None, :] + swapped * sine_table[:, None, :]
    return jnp.concatenate([turned, passed], axis=-1)


def rotate_back(values, cosine_table, sine_table):
    turned = values[..., :ROT]
    passed = values[..., ROT:]
    scaled = turned * sine_table[:, None, :]
    front_half = scaled[..., : ROT // 2]
    back_half = scaled[..., ROT // 2 :]
    swapped = jnp.concatenate([back_half, -front_half], axis=-1)
    return jnp.concatenate([turned * cosine_table[:, None, :] + swapped, passed], axis=-1)


def gelu_slope(hidden_pre):
    normal_cdf = 0.5 * (1.0 + lax.erf(hidden_pre * 0.7071067811865476))
    density = jnp.exp(-0.5 * hidden_pre * hidden_pre) * 0.3989422804014327
    return normal_cdf + hidden_pre * density


def per_sequence(values, sequence_count):
    return jnp.sum(values.reshape(sequence_count, -1, values.shape[-1]), axis=1, dtype=jnp.float32)


def gather_weight(master_layer, column_cuts):
    low_weight = master_layer.astype(jnp.bfloat16)
    pieces = jnp.split(low_weight, column_cuts, axis=1)
    widened = (
        lax.all_gather(pieces[0], "seq", axis=1, tiled=True),
        lax.all_gather(pieces[1], "seq", axis=1, tiled=True),
        lax.all_gather(pieces[2], "seq", axis=1, tiled=True),
        lax.all_gather(pieces[3], "seq", axis=1, tiled=True),
    )
    return (
        lax.all_gather(widened[0], "dp", axis=0, tiled=True),
        lax.all_gather(widened[1], "dp", axis=0, tiled=True),
        lax.all_gather(widened[2], "dp", axis=0, tiled=True),
        lax.all_gather(widened[3], "dp", axis=0, tiled=True),
    )


def reduce_rows(values):
    return (
        lax.psum_scatter(
            values[0].astype(jnp.bfloat16), "dp", scatter_dimension=0, tiled=True
        ).astype(jnp.float32),
        lax.psum_scatter(
            values[1].astype(jnp.bfloat16), "dp", scatter_dimension=0, tiled=True
        ).astype(jnp.float32),
        lax.psum_scatter(
            values[2].astype(jnp.bfloat16), "dp", scatter_dimension=0, tiled=True
        ).astype(jnp.float32),
        lax.psum_scatter(
            values[3].astype(jnp.bfloat16), "dp", scatter_dimension=0, tiled=True
        ).astype(jnp.float32),
    )


def reduce_cols(values):
    return (
        lax.psum_scatter(
            values[0].astype(jnp.bfloat16), "seq", scatter_dimension=1, tiled=True
        ).astype(jnp.float32),
        lax.psum_scatter(
            values[1].astype(jnp.bfloat16), "seq", scatter_dimension=1, tiled=True
        ).astype(jnp.float32),
        lax.psum_scatter(
            values[2].astype(jnp.bfloat16), "seq", scatter_dimension=1, tiled=True
        ).astype(jnp.float32),
        lax.psum_scatter(
            values[3].astype(jnp.bfloat16), "seq", scatter_dimension=1, tiled=True
        ).astype(jnp.float32),
    )


def masked_scores(queries, all_keys, positions):
    raw_scores = jnp.einsum(
        "sqhd,skhd->shqk", queries, all_keys, preferred_element_type=jnp.float32
    ) * HEAD_DIM ** (-0.5)
    visible = jnp.arange(all_keys.shape[1])[None, :] <= positions[:, None]
    return jnp.where(visible[None, None], raw_scores, NEG_LARGE)


def matrix_sums(values, label_indicator):
    return jnp.einsum("lrc,mc->lm", values, label_indicator, precision=HIGH_ACCURACY)


def layer_forward(stream, full_weight, small_layer, cosine_table, sine_table, positions):
    gain_one, shift_one, gain_two, shift_two, bias_qkv, bias_out, bias_up, bias_down = unpack(
        small_layer
    )
    w_qkv, w_out, w_up, w_down = full_weight
    sequence_count, local_len = (stream.shape[0], stream.shape[1])
    token_count = sequence_count * local_len
    flat_state = stream.reshape(token_count, D)
    scaled, inverse = apply_layer_norm(flat_state)
    normed_one = (scaled * gain_one + shift_one).astype(jnp.bfloat16)
    normed_two = (scaled * gain_two + shift_two).astype(jnp.bfloat16)
    joined_proj = jnp.dot(normed_one, w_qkv, preferred_element_type=jnp.float32) + bias_qkv
    shaped = joined_proj.reshape(sequence_count, local_len, HEADS, 3, HEAD_DIM)
    queries = rotate(shaped[:, :, :, 0], cosine_table, sine_table).astype(jnp.bfloat16)
    keys_low = rotate(shaped[:, :, :, 1], cosine_table, sine_table).astype(jnp.bfloat16)
    values_low = shaped[:, :, :, 2].astype(jnp.bfloat16)
    all_keys, all_values = (
        lax.all_gather(keys_low, "seq", axis=1, tiled=True),
        lax.all_gather(values_low, "seq", axis=1, tiled=True),
    )
    scores = masked_scores(queries, all_keys, positions)
    largest = jnp.max(scores, axis=-1, keepdims=True)
    exponent = jnp.exp(scores - largest)
    exp_total = jnp.sum(exponent, axis=-1, keepdims=True)
    attention = (exponent / exp_total).astype(jnp.bfloat16)
    log_total = (largest + jnp.log(exp_total))[..., 0]
    mixed_heads = jnp.einsum(
        "shqk,skhd->sqhd", attention, all_values, preferred_element_type=jnp.float32
    )
    attended = mixed_heads.reshape(token_count, D).astype(jnp.bfloat16)
    branch_attn = jnp.dot(attended, w_out, preferred_element_type=jnp.float32) + bias_out
    hidden_pre = jnp.dot(normed_two, w_up, preferred_element_type=jnp.float32) + bias_up
    hidden = jax.nn.gelu(hidden_pre, approximate=False).astype(jnp.bfloat16)
    branch_mlp = (
        lax.dot_general(hidden, w_down, CONTRACT_LAST, preferred_element_type=jnp.float32)
        + bias_down
    )
    output = flat_state + branch_attn + branch_mlp
    saved_layer = (
        scaled,
        inverse,
        normed_one,
        normed_two,
        queries,
        all_keys,
        all_values,
        log_total,
        attended,
        hidden_pre,
        hidden,
    )
    return (output.reshape(sequence_count, local_len, D), saved_layer)


def layer_backward(
    saved_layer,
    full_weight,
    small_layer,
    grad_stream,
    train_rows,
    cosine_table,
    sine_table,
    positions,
):
    (
        scaled,
        inverse,
        normed_one,
        normed_two,
        queries,
        all_keys,
        all_values,
        log_total,
        attended,
        hidden_pre,
        hidden,
    ) = saved_layer
    gain_one, shift_one, gain_two, shift_two, bias_qkv, bias_out, bias_up, bias_down = unpack(
        small_layer
    )
    w_qkv, w_out, w_up, w_down = full_weight
    sequence_count, local_len = (grad_stream.shape[0], grad_stream.shape[1])
    token_count = sequence_count * local_len
    score_scale = HEAD_DIM ** (-0.5)
    grad_low = grad_stream.reshape(token_count, D).astype(jnp.bfloat16)
    kept_out = grad_low * train_rows
    grad_hidden = jnp.dot(grad_low, w_down, preferred_element_type=jnp.float32)
    grad_pre = (grad_hidden * gelu_slope(hidden_pre)).astype(jnp.bfloat16)
    grad_normed_two = lax.dot_general(
        grad_pre, w_up, CONTRACT_LAST, preferred_element_type=jnp.float32
    )
    grad_attended = lax.dot_general(
        grad_low, w_out, CONTRACT_LAST, preferred_element_type=jnp.float32
    )
    grad_attended = grad_attended.astype(jnp.bfloat16).reshape(
        sequence_count, local_len, HEADS, HEAD_DIM
    )
    scores = masked_scores(queries, all_keys, positions)
    attention = jnp.exp(scores - log_total[..., None])
    grad_attention = jnp.einsum(
        "sqhd,skhd->shqk", grad_attended, all_values, preferred_element_type=jnp.float32
    )
    grad_scores = attention * (
        grad_attention - jnp.sum(attention * grad_attention, axis=-1, keepdims=True)
    )
    grad_scores = grad_scores.astype(jnp.bfloat16)
    grad_queries = (
        jnp.einsum("shqk,skhd->sqhd", grad_scores, all_keys, preferred_element_type=jnp.float32)
        * score_scale
    )
    keys_term = (
        jnp.einsum("shqk,sqhd->skhd", grad_scores, queries, preferred_element_type=jnp.float32)
        * score_scale
    )
    values_term = jnp.einsum(
        "shqk,sqhd->skhd",
        attention.astype(jnp.bfloat16),
        grad_attended,
        preferred_element_type=jnp.float32,
    )
    grad_keys, grad_values = (
        lax.psum_scatter(keys_term, "seq", scatter_dimension=1, tiled=True),
        lax.psum_scatter(values_term, "seq", scatter_dimension=1, tiled=True),
    )
    grad_joined = jnp.stack(
        [
            rotate_back(grad_queries, cosine_table, sine_table),
            rotate_back(grad_keys, cosine_table, sine_table),
            grad_values,
        ],
        axis=3,
    )
    grad_joined = grad_joined.reshape(token_count, 3 * D).astype(jnp.bfloat16)
    grad_normed_one = lax.dot_general(
        grad_joined, w_qkv, CONTRACT_LAST, preferred_element_type=jnp.float32
    )
    grad_input = (
        grad_stream.reshape(token_count, D)
        + norm_back(grad_normed_one, scaled, inverse, gain_one)
        + norm_back(grad_normed_two, scaled, inverse, gain_two)
    )
    masked_joined = grad_joined * train_rows
    masked_pre = grad_pre * train_rows
    grad_weight = (
        lax.dot_general(
            normed_one, masked_joined, CONTRACT_FIRST, preferred_element_type=jnp.float32
        ),
        lax.dot_general(attended, kept_out, CONTRACT_FIRST, preferred_element_type=jnp.float32),
        lax.dot_general(normed_two, masked_pre, CONTRACT_FIRST, preferred_element_type=jnp.float32),
        lax.dot_general(kept_out, hidden, CONTRACT_FIRST, preferred_element_type=jnp.float32),
    )
    out_sum = per_sequence(grad_low, sequence_count)
    example_part = jnp.concatenate(
        [
            per_sequence(grad_normed_one * scaled, sequence_count),
            per_sequence(grad_normed_one, sequence_count),
            per_sequence(grad_normed_two * scaled, sequence_count),
            per_sequence(grad_normed_two, sequence_count),
            per_sequence(grad_joined, sequence_count),
            out_sum,
            per_sequence(grad_pre, sequence_count),
            out_sum,
        ],
        axis=1,
    )
    return (grad_input.reshape(sequence_count, local_len, D), example_part, grad_weight)


def on_device(block_in, cotangent, labels, master, small_params, row_state, col_state, small_state):
    sequence_count, local_len = (block_in.shape[0], block_in.shape[1])
    positions = lax.axis_index("seq") * local_len + jnp.arange(local_len)
    cosine_table, sine_table = rotary_tables(positions)
    train_flag = (labels == 0).astype(jnp.float32)
    query_flag = 1.0 - train_flag
    train_rows = jnp.repeat(train_flag.astype(jnp.bfloat16), local_len)[:, None]
    width_local = master.shape[2]
    group_count = lax.axis_size("seq")
    column_cuts = [3 * D // group_count, 4 * D // group_count, (4 * D + FF) // group_count]
    local_column = jnp.arange(width_local)
    bounds = jnp.array([0] + column_cuts + [width_local], jnp.int32)
    label_indicator = (
        (local_column[None, :] >= bounds[:4, None]) & (local_column[None, :] < bounds[1:, None])
    ).astype(jnp.float32)
    stream = block_in.astype(jnp.float32)
    kept_weights = []
    saved_all = []
    for layer_index in range(LAYERS):
        full_weight = gather_weight(master[layer_index], column_cuts)
        kept_weights.append(full_weight)
        stream, saved_layer = layer_forward(
            stream, full_weight, small_params[layer_index], cosine_table, sine_table, positions
        )
        saved_all.append(saved_layer)
    block_out = stream.astype(jnp.bfloat16)
    grad_stream = cotangent.astype(jnp.float32)
    example_parts = [None] * LAYERS
    grad_list = [None] * LAYERS
    for layer_index in reversed(range(LAYERS)):
        full_weight = gather_weight(master[layer_index], column_cuts)
        grad_stream, example_part, grad_weight = layer_backward(
            saved_all[layer_index],
            full_weight,
            small_params[layer_index],
            grad_stream,
            train_rows,
            cosine_table,
            sine_table,
            positions,
        )
        reduced = reduce_cols(reduce_rows(grad_weight))
        example_parts[layer_index] = example_part
        grad_list[layer_index] = jnp.concatenate(
            [reduced[0], reduced[1], reduced[2], reduced[3]], axis=1
        )
    examples = lax.psum(jnp.concatenate(example_parts, axis=1).astype(jnp.bfloat16), "seq").astype(
        jnp.float32
    )
    train_part = jnp.dot(train_flag, examples, precision=HIGH_ACCURACY)
    query_part = jnp.dot(query_flag, examples, precision=HIGH_ACCURACY)
    small_flat, query_total = (
        lax.psum(train_part.astype(jnp.bfloat16), "dp").astype(jnp.float32),
        lax.psum(query_part.astype(jnp.bfloat16), "dp").astype(jnp.float32),
    )
    example_norms = jnp.sum(examples * examples, axis=1) / (LAYERS * SMALL * L)
    influence = jnp.dot(examples, query_total, precision=HIGH_ACCURACY) / jnp.sqrt(
        L * LAYERS * SMALL * (jnp.mean(query_total * query_total) + 1e-06)
    )
    reduced_all = jnp.stack(grad_list, axis=0)
    squared_entries = reduced_all * reduced_all + EPS_SQUARE
    matrix_width = jnp.array([3 * D, D, FF, FF], jnp.float32)
    row_portion = jnp.einsum(
        "qvk,ak->qav", squared_entries, label_indicator, precision=HIGH_ACCURACY
    )
    row_total = lax.psum(row_portion, "seq")
    fresh_row_moments = DECAY * row_state + (1.0 - DECAY) * (
        row_total / matrix_width[None, :, None]
    )
    col_total, row_sum_all = lax.psum(
        (jnp.sum(squared_entries, axis=1), jnp.sum(fresh_row_moments, axis=2)), "dp"
    )
    col_stats = DECAY * col_state + (1.0 - DECAY) * (col_total / D)
    row_mean = row_sum_all / D
    row_selected = jnp.einsum(
        "eqd,qh->edh", fresh_row_moments, label_indicator, precision=HIGH_ACCURACY
    )
    mean_pick = jnp.einsum("lm,mc->lc", row_mean, label_indicator, precision=HIGH_ACCURACY)
    second = row_selected * col_stats[:, None, :] / mean_pick[:, None, :]
    update = reduced_all * lax.rsqrt(second)
    update_total, weight_total = lax.psum(
        (
            matrix_sums(update * update, label_indicator),
            matrix_sums(master * master, label_indicator),
        ),
        ("dp", "seq"),
    )
    entry_count = D * matrix_width
    update_rms = jnp.sqrt(update_total / entry_count[None, :])
    weight_rms = jnp.sqrt(weight_total / entry_count[None, :])
    clip_pick = jnp.einsum(
        "lm,mc->lc", jnp.maximum(1.0, update_rms), label_indicator, precision=HIGH_ACCURACY
    )
    rate_pick = jnp.einsum("lm,mc->lc", weight_rms, label_indicator, precision=HIGH_ACCURACY)
    new_master = master - RATE * rate_pick[:, None, :] * (update / clip_pick[:, None, :])
    small_grads = small_flat.reshape(LAYERS, SMALL)
    small_moments = DECAY * small_state + (1.0 - DECAY) * (small_grads * small_grads + EPS_SQUARE)
    small_update = small_grads * lax.rsqrt(small_moments)
    new_pieces = []
    for update_piece, param_piece in zip(unpack(small_update), unpack(small_params)):
        piece_rms = jnp.sqrt(jnp.mean(update_piece * update_piece, axis=-1, keepdims=True))
        param_rms = jnp.sqrt(jnp.mean(param_piece * param_piece, axis=-1, keepdims=True))
        new_pieces.append(
            param_piece - RATE * param_rms * (update_piece / jnp.maximum(1.0, piece_rms))
        )
    small_new = jnp.concatenate(new_pieces, axis=-1)
    return (
        block_out,
        grad_stream,
        example_norms,
        influence,
        reduced_all,
        fresh_row_moments,
        col_stats,
        new_master,
        new_master.astype(jnp.bfloat16),
        small_grads,
        small_moments,
        small_new,
    )


def solution(mesh):
    placed = (
        P("dp", "seq", None),
        P("dp", "seq", None),
        P("dp"),
        P(None, "dp", "seq"),
        P(),
        P(None, None, "dp"),
        P(None, "seq"),
        P(),
    )
    return jax.shard_map(
        on_device,
        mesh=mesh,
        in_specs=placed,
        out_specs=(
            P("dp", "seq", None),
            P("dp", "seq", None),
            P("dp"),
            P("dp"),
            P(None, "dp", "seq"),
            P(None, None, "dp"),
            P(None, "seq"),
            P(None, "dp", "seq"),
            P(None, "dp", "seq"),
            P(),
            P(),
            P(),
        ),
        check_vma=False,
    )
```

profile of v0, /device:TPU:0, one launch (start us, length us, event | category | flops | bytes accessed | tf_op | source)
XLA Modules:
  0.0 2080.9 jit_solution(12985455557382141610)
XLA Ops:
  10.9 8.5 all-gather.2
  20.9 8.1 all_gather.82
  29.1 8.1 all_gather.84
  41.1 45.9 %all-gather.17.cloned.1.call-done = bf16[768,2304]{1,0:T(8,128)(2,1)} async-done(((bf16[96,2304]{1,0:T(8,128)(2,1)}), bf16[768,2304]{1,0:T(8,128)(2,1)}) %all-gather.17.cloned.1.call-update) | async-done | bytes 3538960 | tf_op jit(solution)/shard_map/all_gather | solution.py:92
  97.6 7.1 reshape.518
  124.6 7.1 all-gather.3
  142.7 24.9 %all-gather.23.cloned.1.call-done = bf16[768,3072]{1,0:T(8,128)(2,1)} async-done(((bf16[96,3072]{1,0:T(8,128)(2,1)}), bf16[768,3072]{1,0:T(8,128)(2,1)}) %all-gather.23.cloned.1.call-update) | async-done | bytes 4718608 | tf_op jit(solution)/shard_map/all_gather | solution.py:94
  167.6 14.4 fusion.14
  182.0 65.9 %all-gather.25.cloned.1.call-done = bf16[768,3072]{1,0:T(8,128)(2,1)} async-done(((bf16[96,3072]{1,0:T(8,128)(2,1)}), bf16[768,3072]{1,0:T(8,128)(2,1)}) %all-gather.25.cloned.1.call-update) | async-done | bytes 4718608 | tf_op jit(solution)/shard_map/all_gather | solution.py:95
  253.2 32.2 %all-gather.19.cloned.1.call-done = bf16[2,768,12,64]{3,0,2,1:T(2,128)(2,1)} async-done(((bf16[2,192,12,64]{3,0,2,1:T(2,128)(2,1)}), bf16[2,768,12,64]{3,0,2,1:T(2,128)(2,1)}) %all-gather.19.cloned.1.call-update) | async-done | bytes 2359312 | tf_op jit(solution)/shard_map/all_gather | solution.py:162
  285.5 10.3 copy.125
  308.2 16.7 all-gather.37.cloned.1.call-done
  324.9 10.2 copy.121
  335.2 8.3 fusion.75
  347.6 20.4 all-gather.21.cloned.1.call-done
  370.8 63.4 %all-gather.27.cloned.1.call-done = bf16[768,2304]{1,0:T(8,128)(2,1)} async-done(((bf16[96,2304]{1,0:T(8,128)(2,1)}), bf16[768,2304]{1,0:T(8,128)(2,1)}) %all-gather.27.cloned.1.call-update) | async-done | bytes 3538960 | tf_op jit(solution)/shard_map/all_gather | solution.py:92
  444.9 7.1 reshape.519
  464.9 8.1 all_gather.92
  473.1 8.1 all_gather.94
  487.2 27.1 %all-gather.29.cloned.1.call-done = bf16[2,768,12,64]{3,0,2,1:T(2,128)(2,1)} async-done(((bf16[2,192,12,64]{3,0,2,1:T(2,128)(2,1)}), bf16[2,768,12,64]{3,0,2,1:T(2,128)(2,1)}) %all-gather.29.cloned.1.call-update) | async-done | bytes 2359312 | tf_op jit(solution)/shard_map/all_gather | solution.py:162
  514.4 11.9 copy.136
  540.3 12.0 copy.155
  552.3 10.2 reshape.549
  562.7 12.1 copy.132
  574.7 13.3 multiply_reduce_fusion.1
  588.6 7.1 multiply_convert_fusion.1
  602.5 12.0 copy.153
  614.5 10.1 reshape.547
  626.0 10.0 all-gather.33.cloned.1.call-done
  636.0 15.5 fusion.17
  651.5 64.6 %all-gather.35.cloned.1.call-done = bf16[768,3072]{1,0:T(8,128)(2,1)} async-done(((bf16[96,3072]{1,0:T(8,128)(2,1)}), bf16[768,3072]{1,0:T(8,128)(2,1)}) %all-gather.35.cloned.1.call-update) | async-done | bytes 4718608 | tf_op jit(solution)/shard_map/all_gather | solution.py:95
  716.1 7.3 fusion.23
  735.1 29.5 %reduce-scatter.63.cloned.1.call-done = f32[192,1536]{1,0:T(8,128)} async-done(((f32[768,1536]{1,0:T(8,128)}), f32[192,1536]{1,0:T(8,128)}) %reduce-scatter.63.cloned.1.call-update) | async-done | bytes 1179664
  769.9 45.1 %reduce-scatter.61.cloned.1.call-done = f32[192,1536]{1,0:T(8,128)} async-done(((f32[768,1536]{1,0:T(8,128)}), f32[192,1536]{1,0:T(8,128)}) %reduce-scatter.61.cloned.1.call-update) | async-done | bytes 1179664
  856.0 9.6 fusion.58
  865.6 12.0 copy.159
  877.6 10.1 reshape.553
  887.7 8.3 multiply_reduce_fusion
  896.0 7.8 multiply_convert_fusion
  910.3 12.0 copy.157
  922.3 10.3 reshape.551
  934.7 8.0 fusion.78
  955.9 6.2 convolution_convert_fusion
  962.8 6.2 convolution_convert_fusion.1
  983.1 7.6 fusion.29
  1087.3 32.5 %reduce-scatter.39.cloned.1.call-done = bf16[96,768]{1,0:T(8,128)(2,1)} async-done(((bf16[768,768]{1,0:T(8,128)(2,1)}), bf16[96,768]{1,0:T(8,128)(2,1)}) %reduce-scatter.39.cloned.1.call-update) | async-done | bytes 147472 | tf_op jit(solution)/shard_map/reduce_scatter | solution.py:104
  1121.6 80.0 %reduce-scatter.49.cloned.1.call-done = bf16[96,2304]{1,0:T(8,128)(2,1)} async-done(((bf16[768,2304]{1,0:T(8,128)(2,1)}), bf16[96,2304]{1,0:T(8,128)(2,1)}) %reduce-scatter.49.cloned.1.call-update) | async-done | bytes 442384 | tf_op jit(solution)/shard_map/reduce_scatter | solution.py:101
  1203.7 96.4 %reduce-scatter.57.cloned.1.call-done = bf16[96,3072]{1,0:T(8,128)(2,1)} async-done(((bf16[768,3072]{1,0:T(8,128)(2,1)}), bf16[96,3072]{1,0:T(8,128)(2,1)}) %reduce-scatter.57.cloned.1.call-update) | async-done | bytes 589840 | tf_op jit(solution)/shard_map/reduce_scatter | solution.py:110
  1300.2 98.8 %reduce-scatter.53.cloned.1.call-done = bf16[96,3072]{1,0:T(8,128)(2,1)} async-done(((bf16[768,3072]{1,0:T(8,128)(2,1)}), bf16[96,3072]{1,0:T(8,128)(2,1)}) %reduce-scatter.53.cloned.1.call-update) | async-done | bytes 589840 | tf_op jit(solution)/shard_map/reduce_scatter | solution.py:107
  1406.6 24.3 %all-reduce.6.cloned.1.call-done = bf16[2,19968]{1,0:T(2,128)(2,1)} async-done(((bf16[2,19968]{1,0:T(2,128)(2,1)}), bf16[2,19968]{1,0:T(2,128)(2,1)}) %all-reduce.6.cloned.1.call-update) | async-done | bytes 79888 | tf_op jit(solution)/shard_map/psum | solution.py:359
  1435.6 80.5 %reduce-scatter.37.cloned.1.call-done = bf16[96,2304]{1,0:T(8,128)(2,1)} async-done(((bf16[768,2304]{1,0:T(8,128)(2,1)}), bf16[96,2304]{1,0:T(8,128)(2,1)}) %reduce-scatter.37.cloned.1.call-update) | async-done | bytes 442384 | tf_op jit(solution)/shard_map/reduce_scatter | solution.py:101
  1519.1 96.0 %reduce-scatter.41.cloned.1.call-done = bf16[96,3072]{1,0:T(8,128)(2,1)} async-done(((bf16[768,3072]{1,0:T(8,128)(2,1)}), bf16[96,3072]{1,0:T(8,128)(2,1)}) %reduce-scatter.41.cloned.1.call-update) | async-done | bytes 589840 | tf_op jit(solution)/shard_map/reduce_scatter | solution.py:107
  1622.1 15.6 reduce-scatter.75.cloned.1.call-done
  1638.6 21.3 %reduce-scatter.71.cloned.1.call-done = bf16[192,96]{1,0:T(8,128)(2,1)} async-done(((bf16[768,96]{1,0:T(8,128)(2,1)}), bf16[192,96]{1,0:T(8,128)(2,1)}) %reduce-scatter.71.cloned.1.call-update) | async-done | bytes 36880
  1660.8 24.3 %reduce-scatter.73.cloned.1.call-done = bf16[576,96]{1,0:T(8,128)(2,1)} async-done(((bf16[2304,96]{1,0:T(8,128)(2,1)}), bf16[576,96]{1,0:T(8,128)(2,1)}) %reduce-scatter.73.cloned.1.call-update) | async-done | bytes 110608
  1686.2 23.7 %reduce-scatter.59.cloned.1.call-done = bf16[96,768]{1,0:T(8,128)(2,1)} async-done(((bf16[96,3072]{1,0:T(8,128)(2,1)}), bf16[96,768]{1,0:T(8,128)(2,1)}) %reduce-scatter.59.cloned.1.call-update) | async-done | bytes 147472 | tf_op jit(solution)/shard_map/reduce_scatter | solution.py:127
  1709.9 24.8 %reduce-scatter.55.cloned.1.call-done = bf16[96,768]{1,0:T(8,128)(2,1)} async-done(((bf16[96,3072]{1,0:T(8,128)(2,1)}), bf16[96,768]{1,0:T(8,128)(2,1)}) %reduce-scatter.55.cloned.1.call-update) | async-done | bytes 147472 | tf_op jit(solution)/shard_map/reduce_scatter | solution.py:124
  1735.7 98.3 %reduce-scatter.45.cloned.1.call-done = bf16[96,3072]{1,0:T(8,128)(2,1)} async-done(((bf16[768,3072]{1,0:T(8,128)(2,1)}), bf16[96,3072]{1,0:T(8,128)(2,1)}) %reduce-scatter.45.cloned.1.call-update) | async-done | bytes 589840 | tf_op jit(solution)/shard_map/reduce_scatter | solution.py:110
  1834.8 72.5 %all-reduce.8.cloned.1.call-done = (bf16[19968]{0:T(1024)(128)(2,1)}, bf16[2,9984]{1,0:T(2,128)(2,1)}) async-done(((bf16[19968]{0:T(1024)(128)(2,1)}, bf16[2,9984]{1,0:T(2,128)(2,1)}), (bf16[19968]{0:T(1024)(128)(2,1)}, bf16[2,9984]{1,0:T(2,128)(2,1)})) %all-reduce.8.cloned.1.call-update) | async-done | bytes 79888 | tf_op jit(solution)/shard_map/psum | solution.py:366
  1918.4 14.0 reduce-scatter.69.cloned.1.call-done
  1933.4 23.5 %reduce-scatter.43.cloned.1.call-done = bf16[96,768]{1,0:T(8,128)(2,1)} async-done(((bf16[96,3072]{1,0:T(8,128)(2,1)}), bf16[96,768]{1,0:T(8,128)(2,1)}) %reduce-scatter.43.cloned.1.call-update) | async-done | bytes 147472 | tf_op jit(solution)/shard_map/reduce_scatter | solution.py:124
  1957.0 24.8 %reduce-scatter.47.cloned.1.call-done = bf16[96,768]{1,0:T(8,128)(2,1)} async-done(((bf16[96,3072]{1,0:T(8,128)(2,1)}), bf16[96,768]{1,0:T(8,128)(2,1)}) %reduce-scatter.47.cloned.1.call-update) | async-done | bytes 147472 | tf_op jit(solution)/shard_map/reduce_scatter | solution.py:127
  1990.2 37.2 %all-reduce.1 = (f32[2,2304]{1,0:T(2,128)S(1)}, f32[2,4]{1,0:T(2,128)S(1)}) all-reduce(f32[2,2304]{1,0:T(2,128)S(1)} %get-tuple-element.59, f32[2,4]{1,0:T(2,128)S(1)} %get-tuple-element.57), channel_id=1, replica_groups=mesh['dp'=8,'seq'=4] {'dp'}, use_global_device_ids=true, to_apply=%region_58.59 | all-reduce | flops 4616 | bytes 36928 | tf_op jit(solution)/shard_map/psum | solution.py:382
  2031.7 37.0 %all-reduce = (f32[2,4]{1,0:T(2,128)S(1)}, f32[2,4]{1,0:T(2,128)S(1)}) all-reduce(f32[2,4]{1,0:T(2,128)S(1)} %fusion.161, f32[2,4]{1,0:T(2,128)} %fusion.160), channel_id=1, replica_groups=mesh['dp'=8,'seq'=4] {'dp','seq'}, use_global_device_ids=true, to_apply=%region_64.65 | all-reduce | flops 16 | bytes 128 | tf_op jit(solution)/shard_map/psum | solution.py:393
  (584 shorter events, 377.0 us)
Async XLA Ops:
  7.2 79.8 %all-gather.17.cloned.1.call-start = ((), (), s32[]{:S(2)}) async-start(), calls=%async_computation.20 | async-start | bytes 3981312 | tf_op jit(solution)/shard_map/all_gather | solution.py:92
  20.8 146.8 %all-gather.23.cloned.1.call-start = ((), (), s32[]{:S(2)}) async-start(), calls=%async_computation.23 | async-start | bytes 5308416 | tf_op jit(solution)/shard_map/all_gather | solution.py:94
  29.0 218.8 %all-gather.25.cloned.1.call-start = ((), (), s32[]{:S(2)}) async-start(), calls=%async_computation.24 | async-start | bytes 5308416 | tf_op jit(solution)/shard_map/all_gather | solution.py:95
  37.2 248.2 %all-gather.19.cloned.1.call-start = ((), (), s32[]{:S(2)}) async-start(), calls=%async_computation.21 | async-start | bytes 5898240 | tf_op jit(solution)/shard_map/all_gather | solution.py:162
  37.6 54.8 %copy-start.91 = (f32[384]{0:T(512)}, f32[384]{0:T(512)S(1)}, u32[]{:S(2)}) copy-start(f32[384]{0:T(512)S(1)} %div.227) | copy-start | bytes 4612
  38.0 54.4 %copy-start.93 = (f32[384]{0:T(512)}, f32[384]{0:T(512)S(1)}, u32[]{:S(2)}) copy-start(f32[384]{0:T(512)S(1)} %rsqrt.27) | copy-start | bytes 4612
  38.6 417.5 %copy-start.54 = (f32[192,16]{0,1:T(8,128)}, f32[192,16]{0,1:T(8,128)S(1)}, u32[]{:S(2)}) copy-start(f32[192,16]{0,1:T(8,128)S(1)} %get-tuple-element.121) | copy-start | bytes 36868
  39.9 52.5 %copy-start.76 = (f32[768]{0:T(1024)}, f32[768]{0:T(1024)S(1)}, u32[]{:S(2)}) copy-start(f32[768]{0:T(1024)S(1)} %get-tuple-element.43) | copy-start | bytes 9220
  39.9 52.5 %copy-start.81 = (f32[768]{0:T(1024)}, f32[768]{0:T(1024)S(1)}, u32[]{:S(2)}) copy-start(f32[768]{0:T(1024)S(1)} %get-tuple-element.40) | copy-start | bytes 9220
  39.9 52.5 %copy-start.83 = (f32[768]{0:T(1024)}, f32[768]{0:T(1024)S(1)}, u32[]{:S(2)}) copy-start(f32[768]{0:T(1024)S(1)} %get-tuple-element.42) | copy-start | bytes 9220
  109.0 186.8 %copy-start.40 = (bf16[2,192,12,16]{1,3,2,0:T(8,128)(2,1)}, bf16[2,192,12,16]{1,3,2,0:T(8,128)(2,1)S(1)}, u32[]{:S(2)}) copy-start(bf16[2,192,12,16]{1,3,2,0:T(8,128)(2,1)S(1)} %get-tuple-element.110) | copy-start | bytes 442372
  111.2 213.7 %all-gather.37.cloned.1.call-start = ((), (), s32[]{:S(2)}) async-start(), calls=%async_computation.43 | async-start | bytes 5898240 | tf_op jit(solution)/shard_map/all_gather | solution.py:163
  116.0 252.0 %all-gather.21.cloned.1.call-start = ((), (), s32[]{:S(2)}) async-start(), calls=%async_computation.22 | async-start | bytes 1327104 | tf_op jit(solution)/shard_map/all_gather | solution.py:93
  123.6 310.6 %all-gather.27.cloned.1.call-start = ((), (), s32[]{:S(2)}) async-start(), calls=%async_computation.25 | async-start | bytes 3981312 | tf_op jit(solution)/shard_map/all_gather | solution.py:92
  133.2 348.1 %all-gather.31.cloned.1.call-start = ((), (), s32[]{:S(2)}) async-start(), calls=%async_computation.27 | async-start | bytes 1327104 | tf_op jit(solution)/shard_map/all_gather | solution.py:93
  140.8 373.6 %all-gather.29.cloned.1.call-start = ((), (), s32[]{:S(2)}) async-start(), calls=%async_computation.26 | async-start | bytes 5898240 | tf_op jit(solution)/shard_map/all_gather | solution.py:162
  141.7 40.3 %copy-start.106 = (f32[1,3072]{1,0:T(1,128)}, f32[1,3072]{1,0:T(1,128)S(1)}, u32[]{:S(2)}) copy-start(f32[1,3072]{1,0:T(1,128)S(1)} %get-tuple-element.107) | copy-start | bytes 36868
  141.8 154.0 %copy-start.20 = (pred[192,768]{1,0:T(8,128)(4,1)}, pred[192,768]{1,0:T(8,128)(4,1)S(1)}, u32[]{:S(2)}) copy-start(pred[192,768]{1,0:T(8,128)(4,1)S(1)} %iota_compare_fusion) | copy-start | bytes 442372
  167.6 80.2 %copy-start.117 = (f32[768]{0:T(1024)S(1)}, f32[768]{0:T(1024)}, u32[]{:S(2)}) copy-start(f32[768]{0:T(1024)} %get-tuple-element.38) | copy-start | bytes 9220
  182.0 71.2 %copy-start.130 = (bf16[384,3072]{1,0:T(8,128)(2,1)}, bf16[384,3072]{1,0:T(8,128)(2,1)S(1)}, u32[]{:S(2)}) copy-start(bf16[384,3072]{1,0:T(8,128)(2,1)S(1)} %get-tuple-element.122) | copy-start | bytes 7077892
  368.1 66.2 %copy-start.71 = (f32[768]{0:T(1024)S(1)}, f32[768]{0:T(1024)}, u32[]{:S(2)}) copy-start(f32[768]{0:T(1024)} %get-tuple-element.37) | copy-start | bytes 9220
  368.1 66.2 %copy-start.109 = (f32[2304]{0:T(1024)S(1)}, f32[2304]{0:T(1024)}, u32[]{:S(2)}) copy-start(f32[2304]{0:T(1024)} %get-tuple-element.44) | copy-start | bytes 27652
  368.1 66.2 %copy-start.115 = (f32[768]{0:T(1024)S(1)}, f32[768]{0:T(1024)}, u32[]{:S(2)}) copy-start(f32[768]{0:T(1024)} %get-tuple-element.36) | copy-start | bytes 9220
  370.5 69.2 %copy-start.59 = (f32[384]{0:T(512)}, f32[384]{0:T(512)S(1)}, u32[]{:S(2)}) copy-start(f32[384]{0:T(512)S(1)} %broadcast_multiply_fusion.13) | copy-start | bytes 4612
  370.8 68.9 %copy-start.62 = (f32[384]{0:T(512)}, f32[384]{0:T(512)S(1)}, u32[]{:S(2)}) copy-start(f32[384]{0:T(512)S(1)} %add_rsqrt_fusion) | copy-start | bytes 4612
  459.9 102.7 %all-gather.39.cloned.1.call-start = ((), (), s32[]{:S(2)}) async-start(), calls=%async_computation.44 | async-start | bytes 5898240 | tf_op jit(solution)/shard_map/all_gather | solution.py:163
  464.8 171.2 %all-gather.33.cloned.1.call-start = ((), (), s32[]{:S(2)}) async-start(), calls=%async_computation.28 | async-start | bytes 5308416 | tf_op jit(solution)/shard_map/all_gather | solution.py:94
  473.0 243.0 %all-gather.35.cloned.1.call-start = ((), (), s32[]{:S(2)}) async-start(), calls=%async_computation.29 | async-start | bytes 5308416 | tf_op jit(solution)/shard_map/all_gather | solution.py:95
  481.2 283.4 %reduce-scatter.63.cloned.1.call-start = ((), (), s32[]{:S(2)}) async-start(), calls=%async_computation.46 | async-start | bytes 5898240
  562.6 252.5 %reduce-scatter.61.cloned.1.call-start = ((), (), s32[]{:S(2)}) async-start(), calls=%async_computation.45 | async-start | bytes 5898240
  624.7 385.0 %reduce-scatter.67.cloned.1.call-start = ((), (), s32[]{:S(2)}) async-start(), calls=%async_computation.48 | async-start | bytes 5898240
  636.0 80.1 %copy-start.23 = (bf16[2,192,768]{2,1,0:T(8,128)(2,1)S(1)}, bf16[2,192,768]{2,1,0:T(8,128)(2,1)}, u32[]{:S(2)}) copy-start(bf16[2,192,768]{2,1,0:T(8,128)(2,1)} %param.11) | copy-start | bytes 1769476
  727.1 121.4 %copy-start.8 = (f32[384,768]{1,0:T(8,128)}, f32[384,768]{1,0:T(8,128)S(1)}, u32[]{:S(2)}) copy-start(f32[384,768]{1,0:T(8,128)S(1)} %fusion.158) | copy-start | bytes 3538948
  887.7 127.3 %reduce-scatter.65.cloned.1.call-start = ((), (), s32[]{:S(2)}) async-start(), calls=%async_computation.47 | async-start | bytes 5898240
  932.6 152.9 %reduce-scatter.51.cloned.1.call-start = ((), (), s32[]{:S(2)}) async-start(), calls=%async_computation.38 | async-start | bytes 1327104 | tf_op jit(solution)/shard_map/reduce_scatter | solution.py:104
  947.0 172.8 %reduce-scatter.39.cloned.1.call-start = ((), (), s32[]{:S(2)}) async-start(), calls=%async_computation.32 | async-start | bytes 1327104 | tf_op jit(solution)/shard_map/reduce_scatter | solution.py:104
  949.1 252.4 %reduce-scatter.49.cloned.1.call-start = ((), (), s32[]{:S(2)}) async-start(), calls=%async_computation.37 | async-start | bytes 3981312 | tf_op jit(solution)/shard_map/reduce_scatter | solution.py:101
  954.9 345.2 %reduce-scatter.57.cloned.1.call-start = ((), (), s32[]{:S(2)}) async-start(), calls=%async_computation.41 | async-start | bytes 5308416 | tf_op jit(solution)/shard_map/reduce_scatter | solution.py:110
  962.2 436.8 %reduce-scatter.53.cloned.1.call-start = ((), (), s32[]{:S(2)}) async-start(), calls=%async_computation.39 | async-start | bytes 5308416 | tf_op jit(solution)/shard_map/reduce_scatter | solution.py:107
  969.1 461.9 %all-reduce.6.cloned.1.call-start = ((), (), s32[]{:S(2)}) async-start(), calls=%async_computation.30 | async-start | bytes 159744 | tf_op jit(solution)/shard_map/psum | solution.py:359
  1072.9 443.2 %reduce-scatter.37.cloned.1.call-start = ((), (), s32[]{:S(2)}) async-start(), calls=%async_computation.31 | async-start | bytes 3981312 | tf_op jit(solution)/shard_map/reduce_scatter | solution.py:101
  1078.2 536.8 %reduce-scatter.41.cloned.1.call-start = ((), (), s32[]{:S(2)}) async-start(), calls=%async_computation.33 | async-start | bytes 5308416 | tf_op jit(solution)/shard_map/reduce_scatter | solution.py:107
  1085.4 313.7 %copy-start.29 = (bf16[384,768]{1,0:T(8,128)(2,1)S(1)}, bf16[384,768]{1,0:T(8,128)(2,1)}, u32[]{:S(2)}) copy-start(bf16[384,768]{1,0:T(8,128)(2,1)} %copy-done.26) | copy-start | bytes 1769476
  1085.4 552.4 %reduce-scatter.75.cloned.1.call-start = ((), (), s32[]{:S(2)}) async-start(), calls=%async_computation.52 | async-start | bytes 245760
  1087.2 572.7 %reduce-scatter.71.cloned.1.call-start = ((), (), s32[]{:S(2)}) async-start(), calls=%async_computation.50 | async-start | bytes 245760
  1121.5 563.6 %reduce-scatter.73.cloned.1.call-start = ((), (), s32[]{:S(2)}) async-start(), calls=%async_computation.51 | async-start | bytes 737280
  1203.7 506.2 %reduce-scatter.59.cloned.1.call-start = ((), (), s32[]{:S(2)}) async-start(), calls=%async_computation.42 | async-start | bytes 737280 | tf_op jit(solution)/shard_map/reduce_scatter | solution.py:127
  1300.1 434.5 %reduce-scatter.55.cloned.1.call-start = ((), (), s32[]{:S(2)}) async-start(), calls=%async_computation.40 | async-start | bytes 737280 | tf_op jit(solution)/shard_map/reduce_scatter | solution.py:124
  1399.0 435.0 %reduce-scatter.45.cloned.1.call-start = ((), (), s32[]{:S(2)}) async-start(), calls=%async_computation.35 | async-start | bytes 5308416 | tf_op jit(solution)/shard_map/reduce_scatter | solution.py:110
  1405.2 113.0 %copy-start.123 = (s32[4]{0:T(128)S(1)}, s32[4]{0:T(128)}, u32[]{:S(2)}) copy-start(s32[4]{0:T(128)} %constant.165) | copy-start | bytes 52
  1405.3 113.0 %copy-start.124 = (s32[4]{0:T(128)S(1)}, s32[4]{0:T(128)}, u32[]{:S(2)}) copy-start(s32[4]{0:T(128)} %constant.164) | copy-start | bytes 52
  1405.3 113.1 %copy-start.90 = (f32[2,2304]{1,0:T(2,128)S(1)}, f32[2,2304]{1,0:T(2,128)}, u32[]{:S(2)}) copy-start(f32[2,2304]{1,0:T(2,128)} %get-tuple-element.76) | copy-start | bytes 55300
  1405.3 210.1 %copy-start.112 = (f32[768]{0:T(1024)S(1)}, f32[768]{0:T(1024)}, u32[]{:S(2)}) copy-start(f32[768]{0:T(1024)} %get-tuple-element.33) | copy-start | bytes 9220
  1405.3 502.0 %all-reduce.8.cloned.1.call-start = ((), (), s32[]{:S(2)}) async-start(), calls=%async_computation.53 | async-start | bytes 161792 | tf_op jit(solution)/shard_map/psum | solution.py:366
  1434.9 497.4 %reduce-scatter.69.cloned.1.call-start = ((), (), s32[]{:S(2)}) async-start(), calls=%async_computation.49 | async-start | bytes 737280
  1518.2 438.8 %reduce-scatter.43.cloned.1.call-start = ((), (), s32[]{:S(2)}) async-start(), calls=%async_computation.34 | async-start | bytes 737280 | tf_op jit(solution)/shard_map/reduce_scatter | solution.py:124
  1615.1 366.7 %reduce-scatter.47.cloned.1.call-start = ((), (), s32[]{:S(2)}) async-start(), calls=%async_computation.36 | async-start | bytes 737280 | tf_op jit(solution)/shard_map/reduce_scatter | solution.py:127
  1620.6 213.4 %copy-start.75 = (bf16[2,19968]{1,0:T(2,128)(2,1)S(1)}, bf16[2,19968]{1,0:T(2,128)(2,1)}, u32[]{:S(2)}) copy-start(bf16[2,19968]{1,0:T(2,128)(2,1)} %all-reduce.6.cloned.1.call-done) | copy-start | bytes 239620
  1620.6 286.7 %copy-start.74 = (f32[2,9984]{1,0:T(2,128)S(1)}, f32[2,9984]{1,0:T(2,128)}, u32[]{:S(2)}) copy-start(f32[2,9984]{1,0:T(2,128)} %param.17) | copy-start | bytes 239620
  1908.8 48.2 %copy-start.46 = (f32[2,9984]{1,0:T(2,128)}, f32[2,9984]{1,0:T(2,128)S(1)}, u32[]{:S(2)}) copy-start(f32[2,9984]{1,0:T(2,128)S(1)} %get-tuple-element.52) | copy-start | bytes 239620
  1982.9 44.7 %copy-start.97 = (f32[2,2304]{1,0:T(2,128)S(1)}, f32[2,2304]{1,0:T(2,128)}, u32[]{:S(2)}) copy-start(f32[2,2304]{1,0:T(2,128)} %param.16) | copy-start | bytes 55300
  1983.1 46.9 %copy-start.13 = (f32[2,96,2304]{2,1,0:T(8,128)}, f32[2,96,2304]{2,1,0:T(8,128)S(1)}, u32[]{:S(2)}) copy-start(f32[2,96,2304]{2,1,0:T(8,128)S(1)} %get-tuple-element.60) | copy-start | bytes 5308420
  1990.2 39.9 %copy-start.111 = (f32[2,4,96]{2,1,0:T(4,128)}, f32[2,4,96]{2,1,0:T(4,128)S(1)}, u32[]{:S(2)}) copy-start(f32[2,4,96]{2,1,0:T(4,128)S(1)} %get-tuple-element.58) | copy-start | bytes 9220
  2027.6 42.7 %copy-start.12 = (f32[2,96,2304]{2,1,0:T(8,128)S(1)}, f32[2,96,2304]{2,1,0:T(8,128)}, u32[]{:S(2)}) copy-start(f32[2,96,2304]{2,1,0:T(8,128)} %param.13) | copy-start | bytes 5308420
  (105 other events, 784.3 us)
Sparse Core Ops, SparseCore 0:
  20.9 66.0 all-gather.16
  89.2 78.3 all-gather.22
  169.8 78.0 all-gather.24
  249.8 35.5 all-gather.18
  287.4 37.4 all-gather.36
  327.0 41.0 all-gather.20
  370.2 63.9 all-gather.26
  436.4 39.5 all-gather.30
  478.1 36.2 all-gather.28
  516.4 37.4 all-gather.38
  556.1 79.8 all-gather.32
  638.0 77.9 all-gather.34
  718.6 45.9 reduce-scatter.62
  767.2 47.8 reduce-scatter.60
  887.8 47.8 reduce-scatter.66
  938.2 47.9 reduce-scatter.64
  989.4 64.0 reduce-scatter.50
  1056.8 62.9 reduce-scatter.38
  1123.4 78.0 reduce-scatter.48
  1205.1 94.9 reduce-scatter.56
  1303.7 95.1 reduce-scatter.52
  1401.9 29.0 all-reduce.5
  1435.0 81.0 reduce-scatter.36
  1520.0 94.9 reduce-scatter.40
  1618.2 19.5 reduce-scatter.74
  1640.2 19.7 reduce-scatter.70
  1663.0 22.0 reduce-scatter.72
  1687.8 22.0 reduce-scatter.58
  1712.5 22.0 reduce-scatter.54
  1738.5 95.3 reduce-scatter.44
  1838.5 68.7 all-reduce.7
  1910.5 21.8 reduce-scatter.68
  1934.9 22.0 reduce-scatter.42
  1959.6 22.0 reduce-scatter.46
where the time goes:
time: 2100 us; the launch traced here: 2080 us
  waiting for transfers between devices  1300 us (62%)
  local copies, waits for them, and re-layouts  316 us (15%)
  matrix products  223 us (11%)
  blocking collectives  139 us (7%)
  other arithmetic  85.9 us (4%)
    reduce_scatter x2, waiting for transfers between devices, reduce_rows(): lax.psum_scatter(values[2].astype(jnp.bfloat16), 'dp', scatter_dimension=...  195 us
    reduce_scatter x2, waiting for transfers between devices, reduce_rows(): lax.psum_scatter(values[3].astype(jnp.bfloat16), 'dp', scatter_dimension=...  195 us
    reduce_scatter x2, waiting for transfers between devices, reduce_rows(): lax.psum_scatter(values[0].astype(jnp.bfloat16), 'dp', scatter_dimension=...  161 us
    unnamed x317, local copies, waits for them, and re-layouts  159 us
    unnamed x42, waiting for transfers between devices  150 us
    all_gather x2, waiting for transfers between devices, gather_weight(): lax.all_gather(widened[3], 'dp', axis=0, tiled=True)  130 us
    all_gather x2, waiting for transfers between devices, gather_weight(): lax.all_gather(widened[0], 'dp', axis=0, tiled=True)  109 us
    psum x1, waiting for transfers between devices, on_device(): lax.psum(query_part.astype(jnp.bfloat16), 'dp').astype(jnp.float32)  72.5 us
  transfers between devices with their start and end apart: 34, of which 29 were waited for; matrix products, arithmetic and copies ran while one was open for 24% of the time, Pallas kernels for 0%

commit v1 on v0

v1 whole, which is shorter than its diff:
```python
import functools

import jax
import jax.numpy as jnp
from jax import lax
from jax.experimental import pallas as pl
from jax.experimental.pallas import tpu as pltpu
from jax.sharding import PartitionSpec as P

D = 768
HEADS = 12
FF = 3072
LAYERS = 2
HEAD_DIM = 64
ROT = 16
SMALL = 9984

EPS_NORM = 1e-05
EPS_SQUARE = 1e-30
RATE = 0.5
DECAY = 0.5
NEG_LARGE = -1e30
SCORE_SCALE = HEAD_DIM ** (-0.5)
CONTRACT_LAST = (((1,), (1,)), ((), ()))
CONTRACT_FIRST = (((0,), (0,)), ((), ()))
VMEM_BYTES = 56 * 1024 * 1024
BF16 = jnp.bfloat16
F32 = jnp.float32


def unpack(vector):
    return jnp.split(vector, [D, 2 * D, 3 * D, 4 * D, 7 * D, 8 * D, 8 * D + FF], axis=-1)


def apply_layer_norm(inputs):
    centred = inputs - jnp.mean(inputs, axis=-1, keepdims=True)
    variance = jnp.mean(centred * centred, axis=-1, keepdims=True)
    inverse = lax.rsqrt(variance + EPS_NORM)
    return (centred * inverse, inverse)


def norm_back(grad_scaled, scaled, inverse):
    mean_grad = jnp.mean(grad_scaled, axis=-1, keepdims=True)
    mean_cross = jnp.mean(grad_scaled * scaled, axis=-1, keepdims=True)
    return (grad_scaled - mean_grad - scaled * mean_cross) * inverse


def rotary_tables(length):
    halfway = ROT // 2
    frequency = 10000.0 ** (-2.0 * jnp.arange(halfway, dtype=F32) / ROT)
    angles = jnp.arange(length).astype(F32)[:, None] * frequency[None, :]
    cosine, sine = jnp.cos(angles), jnp.sin(angles)
    rest = jnp.ones((length, HEAD_DIM - ROT), F32)
    none = jnp.zeros((length, halfway), F32)
    keep = jnp.concatenate([cosine, cosine, rest], axis=1)
    ahead = jnp.concatenate([-sine, none, 0.0 * rest], axis=1)
    behind = jnp.concatenate([none, sine, 0.0 * rest], axis=1)
    return tuple(jnp.concatenate([table, table], axis=1) for table in (keep, ahead, behind))


def swap(values, axis, bits):
    size = lax.axis_size(axis)
    return lax.ppermute(values, axis, [(i, i ^ bits) for i in range(size)])


def sum_pairwise(values, axis, wire=F32):
    bits = 1
    while bits < lax.axis_size(axis):
        sent = values.astype(wire)
        values = sent.astype(F32) + swap(sent, axis, bits).astype(F32)
        bits *= 2
    return values


def gather_tokens(own):
    far = swap(own, "seq", 2)
    near = swap(own, "seq", 1)
    return (own, near, far, swap(far, "seq", 1))


def scatter_tokens(keep, send):
    total = keep + swap(send, "seq", 1).astype(F32)
    return total[0] + swap(total[1].astype(BF16), "seq", 2).astype(F32)


def gather_rows(rows):
    size = lax.axis_size("dp")
    if size != 8:
        return [lax.all_gather(rows, "dp", axis=0, tiled=True)]
    even = [rows] + [swap(rows, "dp", 2 * k) for k in (1, 2, 3)]
    pieces = []
    for piece in even:
        pieces += [piece, swap(piece, "dp", 1)]
    return pieces


def scatter_rows(values):
    size = lax.axis_size("dp")
    if size != 8:
        return lax.psum_scatter(values.astype(BF16), "dp", scatter_dimension=0, tiled=True).astype(
            F32
        )
    own = lax.axis_index("dp")
    x_bit, z_place = own % 2, own // 2
    blocks = values.reshape(4, 2, D // 8, -1)
    keep = lax.dynamic_index_in_dim(blocks, x_bit, 1, keepdims=False)
    send = lax.dynamic_index_in_dim(blocks, 1 - x_bit, 1, keepdims=False)
    summed = keep.astype(F32) + swap(send.astype(BF16), "dp", 1).astype(F32)
    total = lax.dynamic_index_in_dim(summed, z_place, 0, keepdims=False)
    for k in (1, 2, 3):
        part = lax.dynamic_index_in_dim(summed, z_place ^ k, 0, keepdims=False)
        total = total + swap(part.astype(BF16), "dp", 2 * k).astype(F32)
    return total


def in_place_order(pieces, index):
    stacked = list(pieces)
    bits = 1
    while bits < len(stacked):
        flag = (index // bits) % 2 == 1
        stacked = [
            jnp.where(flag, stacked[i ^ bits], stacked[i]) for i in range(len(stacked))
        ]
        bits *= 2
    return stacked


def exchange_blocks(blocks, index):
    size = lax.axis_size("seq")
    received = []
    for k in range(size):
        block = lax.dynamic_index_in_dim(blocks, index ^ k, 0, keepdims=False)
        received.append(block if k == 0 else swap(block, "seq", k))
    return in_place_order(received, index)


def heads_together(values):
    heads = values.shape[-1] // (3 * HEAD_DIM)
    lead = values.shape[:-1]
    by_head = values.reshape(*lead, heads, 3 * HEAD_DIM)
    return jnp.concatenate(
        [
            by_head[..., : 2 * HEAD_DIM].reshape(*lead, heads * 2 * HEAD_DIM),
            by_head[..., 2 * HEAD_DIM :].reshape(*lead, heads * HEAD_DIM),
        ],
        axis=-1,
    )


def heads_apart(values):
    heads = values.shape[-1] // (3 * HEAD_DIM)
    lead = values.shape[:-1]
    pairs, last = jnp.split(values, [heads * 2 * HEAD_DIM], axis=-1)
    return jnp.concatenate(
        [
            pairs.reshape(*lead, heads, 2 * HEAD_DIM),
            last.reshape(*lead, heads, HEAD_DIM),
        ],
        axis=-1,
    ).reshape(values.shape)


def weight_copies(dp_place, pieces, whole, sems, base):
    rows = pieces[0].shape[0]
    copies = []
    for k, piece in enumerate(pieces):
        offset = 0 if len(pieces) == 1 else pl.multiple_of((k ^ dp_place) * rows, 16)
        copies.append(
            pltpu.make_async_copy(piece, whole.at[pl.ds(offset, rows), :], sems.at[base + k])
        )
    return copies


def place_tokens(dst, own, near, far, far_near, core_bit, y_here, chunk):
    for here, left, right in ((0, own, near), (1, far, far_near)):
        for bit in (0, 1):

            @pl.when((y_here == here) & (core_bit == bit))
            def _():
                first, second = (left, right) if bit == 0 else (right, left)
                dst[0, :chunk] = first[0]
                dst[0, chunk:] = second[0]


def spread_tokens(value, keep, send, core_bit, y_here, chunk):
    for bit in (0, 1):

        @pl.when(core_bit == bit)
        def _():
            mine = value[:chunk] if bit == 0 else value[chunk:]
            other = value[chunk:] if bit == 0 else value[:chunk]
            keep[pl.ds(y_here, 1), 0] = mine[None]
            send[pl.ds(y_here, 1), 0] = other.astype(send.dtype)[None]


def gelu_and_slope(v):
    magnitude = jnp.abs(v) * 0.7071067811865476
    t = 1.0 / (1.0 + 0.3275911 * magnitude)
    falling = jnp.exp(-0.5 * v * v)
    poly = t * (
        0.254829592
        + t * (-0.284496736 + t * (1.421413741 + t * (-1.453152027 + t * 1.061405429)))
    )
    tail = 0.5 * poly * falling
    cdf = jnp.where(v >= 0.0, 1.0 - tail, tail)
    return v * cdf, cdf + v * falling * 0.3989422804014327


def forward_kernel(n_pieces, place, *refs):
    (own, near, far, far_near, vec, keep_tab, ahead_tab, behind_tab, w_out) = refs[:9]
    pieces_a = refs[9 : 9 + n_pieces]
    pieces_b = refs[9 + n_pieces : 9 + 2 * n_pieces]
    (keep, send, xhat, qk, val, att, lse, hid, slope) = refs[9 + 2 * n_pieces : 18 + 2 * n_pieces]
    (whole_a, whole_b, k_all, v_all, sems) = refs[18 + 2 * n_pieces :]
    core_bit, y_bit, dp_place = place[0], place[1], place[2]
    step = pl.program_id(1)
    begin = (pl.program_id(0) == 0) & (step == 0)
    copies_a = weight_copies(dp_place, pieces_a, whole_a, sems, 0)
    copies_b = weight_copies(dp_place, pieces_b, whole_b, sems, n_pieces)

    @pl.when(begin)
    def _():
        for copy in copies_a + copies_b:
            copy.start()

    chunk = own.shape[1]
    block = 2 * chunk
    y_here = step ^ y_bit
    place_tokens(xhat, own, near, far, far_near, core_bit, y_here, chunk)
    scaled = xhat[0].astype(F32)
    normed_one = (scaled * vec[0:1] + vec[1:2]).astype(BF16)
    normed_two = (scaled * vec[2:3] + vec[3:4]).astype(BF16)

    @pl.when(begin)
    def _():
        for copy in copies_a:
            copy.wait()

    heads = val.shape[-1] // HEAD_DIM
    wide = 3 * heads * HEAD_DIM
    joined = jnp.dot(normed_one, whole_a[:, :wide], preferred_element_type=F32) + vec[5:6, :wide]
    for h in range(heads):
        pair = joined[:, 2 * HEAD_DIM * h : 2 * HEAD_DIM * (h + 1)]
        turned = (
            pair * keep_tab[...]
            + pltpu.roll(pair, 2 * HEAD_DIM - ROT // 2, 1) * ahead_tab[...]
            + pltpu.roll(pair, ROT // 2, 1) * behind_tab[...]
        )
        qk[0, :, 2 * HEAD_DIM * h : 2 * HEAD_DIM * (h + 1)] = turned.astype(BF16)
        k_all[h, pl.ds(step * block, block)] = turned[:, HEAD_DIM:].astype(BF16)
        first = 2 * HEAD_DIM * heads + HEAD_DIM * h
        v_all[h, pl.ds(step * block, block)] = joined[:, first : first + HEAD_DIM].astype(BF16)
    val[0] = joined[:, 2 * HEAD_DIM * heads :].astype(BF16)
    row = lax.broadcasted_iota(jnp.int32, (block, block), 0)
    column = lax.broadcasted_iota(jnp.int32, (block, block), 1)
    lane = lax.broadcasted_iota(jnp.int32, (block, 128), 1)
    for here in range(2):

        @pl.when(step == here)
        def _():
            log_sums = jnp.zeros((block, 128), F32)
            for h in range(heads):
                query = qk[0, :, 2 * HEAD_DIM * h : 2 * HEAD_DIM * h + HEAD_DIM] * jnp.asarray(
                    SCORE_SCALE, BF16
                )
                scores = []
                for j in range(here + 1):
                    part = lax.dot_general(
                        query,
                        k_all[h, block * j : block * (j + 1)],
                        CONTRACT_LAST,
                        preferred_element_type=F32,
                    )
                    if j == here:
                        part = jnp.where(column <= row, part, NEG_LARGE)
                    scores.append(part)
                largest = functools.reduce(
                    jnp.maximum, [jnp.max(part, axis=-1, keepdims=True) for part in scores]
                )
                total = 0.0
                mixed = 0.0
                for j, part in enumerate(scores):
                    exponent = jnp.exp(part - largest)
                    total = total + jnp.sum(exponent, axis=-1, keepdims=True)
                    mixed = mixed + jnp.dot(
                        exponent.astype(BF16),
                        v_all[h, block * j : block * (j + 1)],
                        preferred_element_type=F32,
                    )
                att[0, :, HEAD_DIM * h : HEAD_DIM * (h + 1)] = (mixed / total).astype(BF16)
                log_sums = jnp.where(lane == h, largest + jnp.log(total), log_sums)
            lse[0] = log_sums.T[:8]

    @pl.when(begin)
    def _():
        for copy in copies_b:
            copy.wait()

    quarter = hid.shape[-1]
    hidden_pre = (
        jnp.dot(normed_two, whole_b[:, :quarter], preferred_element_type=F32) + vec[4:5, :quarter]
    )
    hidden, gradient = gelu_and_slope(hidden_pre)
    hid[0] = hidden.astype(BF16)
    slope[0] = gradient
    partial = jnp.dot(att[0], w_out[...], preferred_element_type=F32) + lax.dot_general(
        hid[0], whole_b[:, quarter:], CONTRACT_LAST, preferred_element_type=F32
    )
    spread_tokens(partial, keep, send, core_bit, y_here, chunk)


def backward_kernel(n_pieces, place, *refs):
    (own, near, far, far_near, vec, keep_tab, ahead_tab, behind_tab, w_out) = refs[:9]
    pieces_a = refs[9 : 9 + n_pieces]
    pieces_b = refs[9 + n_pieces : 9 + 2 * n_pieces]
    (xhat, qk, val, lse, slope) = refs[9 + 2 * n_pieces : 14 + 2 * n_pieces]
    (keep, send, grad, grad_pre, grad_joined, sums) = refs[
        14 + 2 * n_pieces : 20 + 2 * n_pieces
    ]
    (whole_a, whole_b, dk_all, dv_all, dq_all, sems) = refs[20 + 2 * n_pieces :]
    core_bit, y_bit, dp_place = place[0], place[1], place[2]
    step = 1 - pl.program_id(1)
    begin = (pl.program_id(0) == 0) & (step == 1)
    copies_a = weight_copies(dp_place, pieces_a, whole_a, sems, 0)
    copies_b = weight_copies(dp_place, pieces_b, whole_b, sems, n_pieces)

    @pl.when(begin)
    def _():
        for copy in copies_a + copies_b:
            copy.start()

    chunk = own.shape[1]
    block = 2 * chunk
    y_here = step ^ y_bit
    place_tokens(grad, own, near, far, far_near, core_bit, y_here, chunk)
    low_grad = grad[0]

    @pl.when(begin)
    def _():
        for copy in copies_a + copies_b:
            copy.wait()

    quarter = slope.shape[-1]
    heads = val.shape[-1] // HEAD_DIM
    wide = 3 * heads * HEAD_DIM
    grad_hidden = jnp.dot(low_grad, whole_b[:, quarter:], preferred_element_type=F32)
    grad_pre[0] = (grad_hidden * slope[0]).astype(BF16)
    grad_two = lax.dot_general(
        grad_pre[0], whole_b[:, :quarter], CONTRACT_LAST, preferred_element_type=F32
    )
    grad_att = lax.dot_general(
        low_grad, w_out[...], CONTRACT_LAST, preferred_element_type=F32
    ).astype(BF16)
    row = lax.broadcasted_iota(jnp.int32, (block, block), 0)
    column = lax.broadcasted_iota(jnp.int32, (block, block), 1)
    for here in range(2):

        @pl.when(step == here)
        def _():
            for h in range(heads):
                at_q = 2 * HEAD_DIM * h
                query = qk[0, block * here : block * (here + 1), at_q : at_q + HEAD_DIM]
                query = query * jnp.asarray(SCORE_SCALE, BF16)
                near_grad = grad_att[:, HEAD_DIM * h : HEAD_DIM * (h + 1)]
                log_row = lse[0, h : h + 1]
                probs, grad_probs, keys = [], [], []
                delta = 0.0
                for j in range(here + 1):
                    key = qk[0, block * j : block * (j + 1), at_q + HEAD_DIM : at_q + 2 * HEAD_DIM]
                    value = val[0, block * j : block * (j + 1), HEAD_DIM * h : HEAD_DIM * (h + 1)]
                    scores = lax.dot_general(
                        key, query, CONTRACT_LAST, preferred_element_type=F32
                    )
                    prob = jnp.exp(scores - log_row)
                    if j == here:
                        prob = jnp.where(row <= column, prob, 0.0)
                    grad_prob = lax.dot_general(
                        value, near_grad, CONTRACT_LAST, preferred_element_type=F32
                    )
                    delta = delta + jnp.sum(prob * grad_prob, axis=0, keepdims=True)
                    probs.append(prob)
                    grad_probs.append(grad_prob)
                    keys.append(key)
                dq = 0.0
                for j in range(here + 1):
                    grad_score = (probs[j] * (grad_probs[j] - delta)).astype(BF16)
                    dk = jnp.dot(grad_score, query, preferred_element_type=F32)
                    dv = jnp.dot(probs[j].astype(BF16), near_grad, preferred_element_type=F32)
                    if here == 1:
                        dk_all[h, block * j : block * (j + 1)] = dk
                        dv_all[h, block * j : block * (j + 1)] = dv
                    else:
                        dk_all[h, block * j : block * (j + 1)] += dk
                        dv_all[h, block * j : block * (j + 1)] += dv
                    dq = dq + lax.dot_general(
                        grad_score, keys[j], CONTRACT_FIRST, preferred_element_type=F32
                    )
                dq_all[h] = dq * SCORE_SCALE

    for h in range(heads):
        pair = jnp.concatenate([dq_all[h], dk_all[h, pl.ds(step * block, block)]], axis=1)
        turned = (
            pair * keep_tab[...]
            - pltpu.roll(pair, 2 * HEAD_DIM - ROT // 2, 1) * ahead_tab[...]
            - pltpu.roll(pair, ROT // 2, 1) * behind_tab[...]
        )
        grad_joined[0, :, 2 * HEAD_DIM * h : 2 * HEAD_DIM * (h + 1)] = turned.astype(BF16)
        first = 2 * HEAD_DIM * heads + HEAD_DIM * h
        grad_joined[0, :, first : first + HEAD_DIM] = dv_all[
            h, pl.ds(step * block, block)
        ].astype(BF16)
    grad_one = lax.dot_general(
        grad_joined[0], whole_a[:, :wide], CONTRACT_LAST, preferred_element_type=F32
    )
    spread_tokens(
        grad_one * vec[0:1] + grad_two * vec[2:3], keep, send, core_bit, y_here, chunk
    )
    scaled = xhat[0].astype(F32)

    @pl.when(step == 1)
    def _():
        sums[...] = jnp.zeros_like(sums)

    def add_up(place_row, values):
        width = values.shape[-1]
        sums[0, place_row : place_row + 1, :width] += jnp.sum(
            values.astype(F32), axis=0, keepdims=True
        )

    add_up(0, grad_one * scaled)
    add_up(1, grad_one)
    add_up(2, grad_two * scaled)
    add_up(3, grad_two)
    add_up(4, grad_pre[0])
    add_up(5, low_grad)
    add_up(6, grad_joined[0])


def common_specs(count, chunk, quarter, heads, block_of):
    tokens = pl.BlockSpec((1, chunk, D), lambda s, t, place: (s, 0, 0))
    table = pl.BlockSpec((2 * chunk, 2 * HEAD_DIM), lambda s, t, place: (block_of(t), 0))
    return [
        tokens,
        tokens,
        tokens,
        tokens,
        pl.BlockSpec((8, D), lambda s, t, place: (0, 0)),
        table,
        table,
        table,
        pl.BlockSpec((heads * HEAD_DIM, D), lambda s, t, place: (0, 0)),
    ] + [pl.BlockSpec(memory_space=pl.ANY)] * (2 * count)


def block_spec(rows, width, block_of):
    return pl.BlockSpec((1, rows, width), lambda s, t, place: (s, block_of(t), 0))


def run_forward(place, chunks, vec, tables, w_out, pieces_a, pieces_b):
    sequences, chunk, _ = chunks[0].shape
    length = 4 * chunk
    count = len(pieces_a)
    heads = w_out.shape[0] // HEAD_DIM
    quarter = pieces_b[0].shape[1] // 2
    half = 2 * chunk

    def same(t):
        return t

    spread = pl.BlockSpec((2, 1, chunk, D), lambda s, t, place: (0, s, 0, 0))
    widths = [
        (D, BF16),
        (2 * heads * HEAD_DIM, BF16),
        (heads * HEAD_DIM, BF16),
        (heads * HEAD_DIM, BF16),
    ]
    out_shape = [
        jax.ShapeDtypeStruct((2, sequences, chunk, D), F32),
        jax.ShapeDtypeStruct((2, sequences, chunk, D), BF16),
        *[jax.ShapeDtypeStruct((sequences, length, width), kind) for width, kind in widths],
        jax.ShapeDtypeStruct((sequences, 8, length), F32),
        jax.ShapeDtypeStruct((sequences, length, quarter), BF16),
        jax.ShapeDtypeStruct((sequences, length, quarter), F32),
    ]
    out_specs = [
        spread,
        spread,
        *[block_spec(half, width, same) for width, _ in widths],
        pl.BlockSpec((1, 8, half), lambda s, t, place: (s, 0, t)),
        block_spec(half, quarter, same),
        block_spec(half, quarter, same),
    ]
    return pl.pallas_call(
        functools.partial(forward_kernel, count),
        grid_spec=pltpu.PrefetchScalarGridSpec(
            num_scalar_prefetch=1,
            grid=(sequences, 2),
            in_specs=common_specs(count, chunk, quarter, heads, same),
            out_specs=out_specs,
            scratch_shapes=[
                pltpu.VMEM((D, pieces_a[0].shape[1]), BF16),
                pltpu.VMEM((D, pieces_b[0].shape[1]), BF16),
                pltpu.VMEM((heads, length, HEAD_DIM), BF16),
                pltpu.VMEM((heads, length, HEAD_DIM), BF16),
                pltpu.SemaphoreType.DMA((2 * count,)),
            ],
        ),
        out_shape=out_shape,
        compiler_params=pltpu.CompilerParams(vmem_limit_bytes=VMEM_BYTES),
        cost_estimate=pl.CostEstimate(
            flops=8 * 10**9, bytes_accessed=2 * 10**7, transcendentals=10**7
        ),
        name="layer_forward",
    )(place, *chunks, vec, *tables, w_out, *pieces_a, *pieces_b)


def run_backward(place, chunks, vec, tables, w_out, pieces_a, pieces_b, saved):
    xhat, qk, val, lse, slope = saved
    sequences, chunk, _ = chunks[0].shape
    length = 4 * chunk
    count = len(pieces_a)
    heads = w_out.shape[0] // HEAD_DIM
    quarter = pieces_b[0].shape[1] // 2
    wide = 3 * heads * HEAD_DIM
    half = 2 * chunk

    def turned(t):
        return 1 - t

    spread = pl.BlockSpec((2, 1, chunk, D), lambda s, t, place: (0, s, 0, 0))
    return pl.pallas_call(
        functools.partial(backward_kernel, count),
        grid_spec=pltpu.PrefetchScalarGridSpec(
            num_scalar_prefetch=1,
            grid=(sequences, 2),
            in_specs=common_specs(count, chunk, quarter, heads, turned)
            + [
                block_spec(half, D, turned),
                pl.BlockSpec((1, length, qk.shape[-1]), lambda s, t, place: (s, 0, 0)),
                pl.BlockSpec((1, length, val.shape[-1]), lambda s, t, place: (s, 0, 0)),
                pl.BlockSpec((1, 8, half), lambda s, t, place: (s, 0, 1 - t)),
                block_spec(half, quarter, turned),
            ],
            out_specs=[
                spread,
                spread,
                block_spec(half, D, turned),
                block_spec(half, quarter, turned),
                block_spec(half, wide, turned),
                pl.BlockSpec((1, 8, D), lambda s, t, place: (s, 0, 0)),
            ],
            scratch_shapes=[
                pltpu.VMEM((D, pieces_a[0].shape[1]), BF16),
                pltpu.VMEM((D, pieces_b[0].shape[1]), BF16),
                pltpu.VMEM((heads, length, HEAD_DIM), F32),
                pltpu.VMEM((heads, length, HEAD_DIM), F32),
                pltpu.VMEM((heads, half, HEAD_DIM), F32),
                pltpu.SemaphoreType.DMA((2 * count,)),
            ],
        ),
        out_shape=[
            jax.ShapeDtypeStruct((2, sequences, chunk, D), F32),
            jax.ShapeDtypeStruct((2, sequences, chunk, D), BF16),
            jax.ShapeDtypeStruct((sequences, length, D), BF16),
            jax.ShapeDtypeStruct((sequences, length, quarter), BF16),
            jax.ShapeDtypeStruct((sequences, length, wide), BF16),
            jax.ShapeDtypeStruct((sequences, 8, D), F32),
        ],
        compiler_params=pltpu.CompilerParams(vmem_limit_bytes=VMEM_BYTES),
        cost_estimate=pl.CostEstimate(
            flops=16 * 10**9, bytes_accessed=3 * 10**7, transcendentals=10**7
        ),
        name="layer_backward",
    )(place, *chunks, vec, *tables, w_out, *pieces_a, *pieces_b, *saved)


def out_rows(pieces_a, wide, dp_place, seq_place):
    columns = [piece[:, wide:] for piece in pieces_a]
    stacked = jnp.concatenate(
        in_place_order(columns, dp_place) if len(columns) > 1 else columns, axis=0
    )
    size = lax.axis_size("seq")
    blocks = stacked.reshape(size, D // size, -1)
    return jnp.concatenate(exchange_blocks(blocks, seq_place), axis=1)


def on_device(block_in, cotangent, labels, master, small_params, row_state, col_state, small_state):
    sequences, chunk = block_in.shape[:2]
    group_count = lax.axis_size("seq")
    seq_place, dp_place = lax.axis_index("seq"), lax.axis_index("dp")
    place = jnp.stack([seq_place % 2, seq_place // 2, dp_place]).astype(jnp.int32)
    length = chunk * group_count
    train_flag = (labels == 0).astype(F32)
    query_flag = 1.0 - train_flag
    qkv_wide, out_wide, quarter = 3 * D // group_count, D // group_count, FF // group_count
    cuts = [0, qkv_wide, qkv_wide + out_wide, qkv_wide + out_wide + quarter, master.shape[2]]
    tables = rotary_tables(length)

    low = master.astype(BF16)
    weights, vectors, params = [], [], []
    for i in range(LAYERS):
        piece_a = jnp.concatenate(
            [heads_together(low[i, :, : cuts[1]]), low[i, :, cuts[1] : cuts[2]]], axis=1
        )
        pieces_a = gather_rows(piece_a)
        pieces_b = gather_rows(low[i, :, cuts[2] :])
        weights.append((out_rows(pieces_a, qkv_wide, dp_place, seq_place), pieces_a, pieces_b))
        param = unpack(small_params[i])
        params.append(param)
        bias_qkv = heads_together(
            lax.dynamic_slice_in_dim(param[4], seq_place * qkv_wide, qkv_wide)
        )
        bias_up = lax.dynamic_slice_in_dim(param[6], seq_place * quarter, quarter)
        vectors.append(
            jnp.stack(
                [
                    *param[:4],
                    jnp.pad(bias_up, (0, D - quarter)),
                    jnp.pad(bias_qkv, (0, D - qkv_wide)),
                    jnp.zeros((D,), F32),
                    jnp.zeros((D,), F32),
                ]
            )
        )

    stream = block_in.astype(F32)
    norms, saved_all = [], []
    for i in range(LAYERS):
        scaled, inverse = apply_layer_norm(stream)
        norms.append((scaled, inverse))
        chunks = gather_tokens(scaled.astype(BF16))
        keep, send, *saved = run_forward(place, chunks, vectors[i], tables, *weights[i])
        saved_all.append(saved)
        stream = (
            stream + scatter_tokens(keep, send) + (params[i][5] + params[i][7])
        )
    block_out = stream.astype(BF16)

    grad_stream = cotangent.astype(F32)
    row_flag = train_flag.astype(BF16)[:, None, None]
    example_parts, grad_list = [None] * LAYERS, [None] * LAYERS
    for i in reversed(range(LAYERS)):
        xhat, qk, val, att, lse, hid, slope = saved_all[i]
        chunks = gather_tokens(grad_stream.astype(BF16))
        keep, send, grad_low, grad_pre, grad_joined, sums = run_backward(
            place, chunks, vectors[i], tables, *weights[i], (xhat, qk, val, lse, slope)
        )
        grad_scaled = scatter_tokens(keep, send)
        grad_stream = grad_stream + norm_back(grad_scaled, *norms[i])
        wide_scaled = xhat.astype(F32)
        normed_one = (wide_scaled * params[i][0] + params[i][1]).astype(BF16)
        normed_two = (wide_scaled * params[i][2] + params[i][3]).astype(BF16)

        def tokens(values):
            return values.reshape(sequences * length, values.shape[-1])

        def outer(left, right):
            return lax.dot_general(
                tokens(left), tokens(right), CONTRACT_FIRST, preferred_element_type=F32
            )

        kept = grad_low * row_flag
        grad_up = outer(normed_two, grad_pre * row_flag)
        grad_down = outer(kept, hid)
        grad_out = outer(att, kept).astype(BF16)
        blocks = grad_out.reshape(out_wide, group_count, out_wide).transpose(1, 0, 2)
        grad_out = jnp.concatenate(exchange_blocks(blocks, seq_place), axis=0)
        grad_qkv = outer(normed_one, grad_joined * row_flag)
        part_b = scatter_rows(jnp.concatenate([grad_up, grad_down], axis=1))
        part_a = scatter_rows(jnp.concatenate([grad_qkv, grad_out.astype(F32)], axis=1))
        grad_list[i] = jnp.concatenate(
            [heads_apart(part_a[:, :qkv_wide]), part_a[:, qkv_wide:], part_b], axis=1
        )
        only_one = jnp.where(seq_place == 0, 1.0, 0.0)
        grad_sum = sums[:, 5] * only_one

        def spread(values, width):
            return lax.dynamic_update_slice(
                jnp.zeros((sequences, group_count * width), F32), values, (0, seq_place * width)
            )

        example_parts[i] = jnp.concatenate(
            [
                sums[:, 0],
                sums[:, 1],
                sums[:, 2],
                sums[:, 3],
                spread(heads_apart(sums[:, 6, :qkv_wide]), qkv_wide),
                grad_sum,
                spread(sums[:, 4, :quarter], quarter),
                grad_sum,
            ],
            axis=1,
        )

    examples = sum_pairwise(jnp.concatenate(example_parts, axis=1), "seq", BF16)
    totals = sum_pairwise(
        jnp.stack(
            [
                jnp.sum(train_flag[:, None] * examples, axis=0),
                jnp.sum(query_flag[:, None] * examples, axis=0),
            ]
        ),
        "dp",
        BF16,
    )
    small_flat, query_total = totals[0], totals[1]
    example_norms = jnp.sum(examples * examples, axis=1) / (LAYERS * SMALL * length)
    influence = jnp.sum(examples * query_total, axis=1) / jnp.sqrt(
        length * LAYERS * SMALL * (jnp.mean(query_total * query_total) + 1e-06)
    )

    def by_matrix(values):
        return [values[..., cuts[m] : cuts[m + 1]] for m in range(4)]

    def matrix_sums(values):
        return jnp.stack([jnp.sum(piece, axis=(1, 2)) for piece in by_matrix(values)], axis=1)

    reduced_all = jnp.stack(grad_list, axis=0)
    squared = reduced_all * reduced_all + EPS_SQUARE
    matrix_width = jnp.array([3 * D, D, FF, FF], F32)
    row_total = sum_pairwise(
        jnp.stack([jnp.sum(piece, axis=2) for piece in by_matrix(squared)], axis=1), "seq"
    )
    fresh_row_moments = DECAY * row_state + (1.0 - DECAY) * (
        row_total / matrix_width[None, :, None]
    )
    packed = sum_pairwise(
        jnp.concatenate(
            [jnp.sum(squared, axis=1), jnp.sum(fresh_row_moments, axis=2)], axis=1
        ),
        "dp",
    )
    col_stats = DECAY * col_state + (1.0 - DECAY) * (packed[:, : cuts[4]] / D)
    row_mean = packed[:, cuts[4] :] / D
    col_inverse = by_matrix(lax.rsqrt(col_stats))
    row_inverse = lax.rsqrt(fresh_row_moments / row_mean[:, :, None])
    update = jnp.concatenate(
        [
            piece * row_inverse[:, m, :, None] * col_inverse[m][:, None, :]
            for m, piece in enumerate(by_matrix(reduced_all))
        ],
        axis=2,
    )
    square_totals = jnp.stack([matrix_sums(update * update), matrix_sums(master * master)])
    square_totals = sum_pairwise(sum_pairwise(square_totals, "seq"), "dp")
    entry_count = D * matrix_width
    update_rms = jnp.sqrt(square_totals[0] / entry_count[None, :])
    weight_rms = jnp.sqrt(square_totals[1] / entry_count[None, :])
    factor = RATE * weight_rms / jnp.maximum(1.0, update_rms)
    new_master = jnp.concatenate(
        [
            old - factor[:, m, None, None] * piece
            for m, (old, piece) in enumerate(zip(by_matrix(master), by_matrix(update)))
        ],
        axis=2,
    )
    small_grads = small_flat.reshape(LAYERS, SMALL)
    small_moments = DECAY * small_state + (1.0 - DECAY) * (small_grads * small_grads + EPS_SQUARE)
    small_update = small_grads * lax.rsqrt(small_moments)
    new_pieces = []
    for update_piece, param_piece in zip(unpack(small_update), unpack(small_params)):
        piece_rms = jnp.sqrt(jnp.mean(update_piece * update_piece, axis=-1, keepdims=True))
        param_rms = jnp.sqrt(jnp.mean(param_piece * param_piece, axis=-1, keepdims=True))
        new_pieces.append(
            param_piece - RATE * param_rms * (update_piece / jnp.maximum(1.0, piece_rms))
        )
    small_new = jnp.concatenate(new_pieces, axis=-1)
    return (
        block_out,
        grad_stream,
        example_norms,
        influence,
        reduced_all,
        fresh_row_moments,
        col_stats,
        new_master,
        new_master.astype(BF16),
        small_grads,
        small_moments,
        small_new,
    )


def solution(mesh):
    placed = (
        P("dp", "seq", None),
        P("dp", "seq", None),
        P("dp"),
        P(None, "dp", "seq"),
        P(),
        P(None, None, "dp"),
        P(None, "seq"),
        P(),
    )
    return jax.shard_map(
        on_device,
        mesh=mesh,
        in_specs=placed,
        out_specs=(
            P("dp", "seq", None),
            P("dp", "seq", None),
            P("dp"),
            P("dp"),
            P(None, "dp", "seq"),
            P(None, None, "dp"),
            P(None, "seq"),
            P(None, "dp", "seq"),
            P(None, "dp", "seq"),
            P(),
            P(),
            P(),
        ),
        check_vma=False,
    )
```

time: 2100 us -> 647 us (0.31)
  waiting for transfers between devices: 1300 us -> 222 us
  local copies, waits for them, and re-layouts: 316 us -> 88.6 us
  matrix products: 223 us -> 28 us
  blocking collectives: 139 us -> 0 us
  Pallas kernels: 0 us -> 117 us
  starting transfers between devices: 1.87 us -> 90 us
    reduce_scatter x12 -> x0, waiting for transfers between devices: 679 us -> none  [the longest x2 195 us: reduce_rows(): lax.psum_scatter(values[2].astype(jnp.bfloat16), 'dp', scatter_dimension=...]
    all_gather x12 -> x0, waiting for transfers between devices: 371 us -> none  [the longest x2 130 us: gather_weight(): lax.all_gather(widened[3], 'dp', axis=0, tiled=True)]
    ppermute x0 -> x91, waiting for transfers between devices: none -> 222 us  [swap(): return lax.ppermute(values, axis, [(i, i ^ bits) for i in range(size)])]
    dot_general x46 -> x8, matrix products: 223 us -> 28 us  [outer(): lax.dot_general(tokens(left), tokens(right), CONTRACT_FIRST, preferred_el...]
    unnamed x42 -> x0, waiting for transfers between devices: 150 us -> none
    unnamed x317 -> x289, local copies, waits for them, and re-layouts: 159 us -> 10 us
    pallas_call x0 -> x4, Pallas kernels: none -> 117 us  [the longest x2 63 us: run_backward(): pl.pallas_call(functools.partial(backward_kernel, count), grid_spec=pltpu...]
    psum x2 -> x0, waiting for transfers between devices: 96.8 us -> none  [the longest x1 72.5 us: on_device(): lax.psum(query_part.astype(jnp.bfloat16), 'dp').astype(jnp.float32)]
  transfers between devices with their start and end apart: 34 -> 91, of which waited for: 29 -> 42; matrix products, arithmetic and copies ran while one was open for 24% -> 26% of each run, Pallas kernels for 0% -> 4%
where the time goes in v1:
time: 647 us; the launch traced here: 639 us
  waiting for transfers between devices  222 us (34%)
  Pallas kernels  117 us (18%)
  starting transfers between devices  90 us (14%)
  other arithmetic  89.7 us (14%)
  local copies, waits for them, and re-layouts  88.6 us (14%)
  matrix products  28 us (4%)
    ppermute x91, waiting for transfers between devices, swap(): return lax.ppermute(values, axis, [(i, i ^ bits) for i in range(size)])  222 us
    ppermute x91, starting transfers between devices, swap(): return lax.ppermute(values, axis, [(i, i ^ bits) for i in range(size)])  90 us
    pallas_call x2, Pallas kernels, run_backward(): pl.pallas_call(functools.partial(backward_kernel, count), grid_spec=pltpu...  63 us
    pallas_call x2, Pallas kernels, run_forward(): pl.pallas_call(functools.partial(forward_kernel, count), grid_spec=pltpu....  53.5 us
    dot_general x8, matrix products, outer(): lax.dot_general(tokens(left), tokens(right), CONTRACT_FIRST, preferred_el...  28 us
  transfers between devices with their start and end apart: 91, of which 42 were waited for; matrix products, arithmetic and copies ran while one was open for 26% of the time, Pallas kernels for 4%

profile of v1, /device:TPU:0, one launch (start us, length us, event | category | flops | bytes accessed | tf_op | source)
XLA Modules:
  0.0 639.1 jit_solution(11397852295496087431)
XLA Ops:
  10.2 2.9 collective-permute-start.9
  14.7 2.6 collective-permute-start.5
  27.7 3.1 multiply_sine_fusion
  30.9 2.5 concatenate.94.refs_7_
  33.3 2.4 concatenate.93.refs_6_
  40.0 3.5 collective-permute-start.27
  47.5 6.2 collective-permute-done.27.refs_13_
  57.5 2.5 collective-permute-start.18
  60.1 2.6 collective-permute-start.16
  72.1 8.8 %collective-permute-done.16.refs_21_ = bf16[96,1536]{1,0:T(8,128)(2,1)S(1)} collective-permute-done((bf16[96,1536]{1,0:T(8,128)(2,1)S(1)}, bf16[96,1536]{1,0:T(8,128)(2,1)S(1)}, u32[]{:S(2)}, u32[]{:S(2)}) %collective-permute-start.16) | collective-permute-done | bytes 294944 | tf_op jit(solution)/shard_map/ppermute | solution.py:63
  83.8 2.7 collective-permute-done.11
  96.3 3.3 collective-permute-done.19.refs_24_
  99.6 6.3 collective-permute-done.17.refs_22_
  105.9 5.6 collective-permute-done.15.refs_20_
  113.1 26.7 %layer_forward.2 = (f32[2,2,192,768]{3,2,1,0:T(8,128)}, bf16[2,2,192,768]{3,2,1,0:T(8,128)(2,1)}, bf16[2,768,768]{2,1,0:T(8,128)(2,1)}, bf16[2,768,384]{2,1,0:T(...) custom-call(s32[3]{0:T(128)} %pad_add_fusion.place, ...), custom_call_target="tpu_custom_call" | custom-call | flops 8000000000 | bytes 20000000 | tf_op jit(solution)/shard_map/layer_forward/pallas_call | solution.py:493
  158.2 13.9 %collective-permute-done.21 = bf16[2,192,768]{2,1,0:T(8,128)(2,1)S(1)} collective-permute-done((bf16[2,192,768]{2,1,0:T(8,128)(2,1)S(1)}, bf16[2,192,768]{2,1,0:T(8,128)(2,1)S(1)}, u32[]{:S(2)}, u32[]{:S(2)}) %collective-permute-start.21) | collective-permute-done | bytes 589856 | tf_op jit(solution)/shard_map/ppermute | solution.py:63
  179.6 9.8 %collective-permute-done.23.refs_2_ = bf16[2,192,768]{2,1,0:T(8,128)(2,1)S(1)} collective-permute-done((bf16[2,192,768]{2,1,0:T(8,128)(2,1)S(1)}, bf16[2,192,768]{2,1,0:T(8,128)(2,1)S(1)}, u32[]{:S(2)}, u32[]{:S(2)}) %collective-permute-start.23) | collective-permute-done | bytes 589856 | tf_op jit(solution)/shard_map/ppermute | solution.py:63
  196.3 5.1 collective-permute-done.41.refs_24_
  201.4 6.3 collective-permute-done.39.refs_22_
  207.7 5.9 collective-permute-done.37.refs_20_
  214.3 26.8 %layer_forward.3 = (f32[2,2,192,768]{3,2,1,0:T(8,128)}, bf16[2,2,192,768]{3,2,1,0:T(8,128)(2,1)}, bf16[2,768,768]{2,1,0:T(8,128)(2,1)}, bf16[2,768,384]{2,1,0:T(...) custom-call(s32[3]{0:T(128)} %pad_add_fusion.place, ...), custom_call_target="tpu_custom_call" | custom-call | flops 8000000000 | bytes 20000000 | tf_op jit(solution)/shard_map/layer_forward/pallas_call | solution.py:493
  242.1 31.7 %layer_backward.2 = (f32[2,2,192,768]{3,2,1,0:T(8,128)}, bf16[2,2,192,768]{3,2,1,0:T(8,128)(2,1)}, bf16[2,768,768]{2,1,0:T(8,128)(2,1)}, bf16[2,768,768]{2,1,0:T...) custom-call(s32[3]{0:T(128)} %pad_add_fusion.place, bf16[2,192,768]{2,1,0:T(8,128)(2,1)} %refs_0_, ...), custom_call_target="tpu_custom_call" | custom-call | flops 16000000000 | bytes 30000000 | tf_op jit(solution)/shard_map/layer_backward/pallas_call | solution.py:531
  277.6 2.4 fusion.73
  280.0 3.5 fusion.39
  289.6 4.1 fusion.47
  293.7 2.5 pad_maximum_fusion.1
  296.2 3.0 fusion.57
  299.6 3.1 pad_maximum_fusion.4
  302.8 3.1 copy.118
  309.5 6.1 copy.125
  318.4 4.3 collective-permute-done.73
  327.5 3.7 collective-permute-done.74
  334.5 5.1 collective-permute-done.75
  340.4 2.4 convert_add_fusion.1
  346.7 12.5 %collective-permute-done.48 = bf16[2,192,768]{2,1,0:T(8,128)(2,1)S(1)} collective-permute-done((bf16[2,192,768]{2,1,0:T(8,128)(2,1)S(1)}, bf16[2,192,768]{2,1,0:T(8,128)(2,1)S(1)}, u32[]{:S(2)}, u32[]{:S(2)}) %collective-permute-start.48) | collective-permute-done | bytes 589856 | tf_op jit(solution)/shard_map/ppermute | solution.py:63
  359.7 9.7 %collective-permute-done.43 = bf16[2,192,768]{2,1,0:T(8,128)(2,1)S(1)} collective-permute-done((bf16[2,192,768]{2,1,0:T(8,128)(2,1)S(1)}, bf16[2,192,768]{2,1,0:T(8,128)(2,1)S(1)}, u32[]{:S(2)}, u32[]{:S(2)}) %collective-permute-start.43) | collective-permute-done | bytes 589856 | tf_op jit(solution)/shard_map/ppermute | solution.py:63
  369.4 3.1 fusion.164
  380.5 5.2 collective-permute-done.50.refs_2_
  389.4 3.1 collective-permute-done.80
  392.5 10.2 %collective-permute-done.79 = bf16[96,1536]{1,0:T(8,128)(2,1)} collective-permute-done((bf16[96,1536]{1,0:T(8,128)(2,1)}, bf16[96,1536]{1,0:T(8,128)(2,1)}, u32[]{:S(2)}, u32[]{:S(2)}) %collective-permute-start.79) | collective-permute-done | bytes 294944 | tf_op jit(solution)/shard_map/ppermute | solution.py:63
  405.1 31.4 %layer_backward.3 = (f32[2,2,192,768]{3,2,1,0:T(8,128)}, bf16[2,2,192,768]{3,2,1,0:T(8,128)(2,1)}, bf16[2,768,768]{2,1,0:T(8,128)(2,1)}, bf16[2,768,768]{2,1,0:T...) custom-call(s32[3]{0:T(128)} %pad_add_fusion.place, bf16[2,192,768]{2,1,0:T(8,128)(2,1)} %get-tuple-element.130.refs_0_, ...), custom_call_target="tpu_custom_call" | custom-call | flops 16000000000 | bytes 30000000 | tf_op jit(solution)/shard_map/layer_backward/pallas_call | solution.py:531
  442.4 3.5 fusion.36
  451.1 4.1 fusion.42
  455.2 2.5 pad_maximum_fusion
  457.7 6.1 copy.109
  463.8 5.2 fusion.52
  469.0 2.8 fusion.85
  474.7 3.2 collective-permute-done.55
  479.7 22.0 %collective-permute-done.56 = bf16[2,19968]{1,0:T(2,128)(2,1)S(1)} collective-permute-done((bf16[2,19968]{1,0:T(2,128)(2,1)S(1)}, bf16[2,19968]{1,0:T(2,128)(2,1)S(1)}, u32[]{:S(2)}, u32[]{:S(2)}) %collective-permute-start.56) | collective-permute-done | bytes 79904 | tf_op jit(solution)/shard_map/ppermute | solution.py:63
  501.9 3.1 pad_maximum_fusion.3
  505.0 3.3 copy.103
  508.5 2.8 collective-permute-start.58
  516.7 10.0 %collective-permute-done.62 = bf16[4,96,768]{2,1,0:T(8,128)(2,1)S(1)} collective-permute-done((bf16[4,96,768]{2,1,0:T(8,128)(2,1)S(1)}, bf16[4,96,768]{2,1,0:T(8,128)(2,1)S(1)}, u32[]{:S(2)}, u32[]{:S(2)}) %collective-permute-start.62) | collective-permute-done | bytes 589856 | tf_op jit(solution)/shard_map/ppermute | solution.py:63
  531.8 2.6 collective-permute-done.63
  534.5 2.6 collective-permute-done.65
  537.1 5.4 collective-permute-done.64
  552.2 7.6 %collective-permute-done.67 = bf16[96,1536]{1,0:T(8,128)(2,1)S(1)} collective-permute-done((bf16[96,1536]{1,0:T(8,128)(2,1)}, bf16[96,1536]{1,0:T(8,128)(2,1)S(1)}, u32[]{:S(2)}, u32[]{:S(2)}) %collective-permute-start.67) | collective-permute-done | bytes 294944 | tf_op jit(solution)/shard_map/ppermute | solution.py:63
  559.8 3.7 collective-permute-done.69
  564.2 10.5 %collective-permute-done.68 = bf16[96,1536]{1,0:T(8,128)(2,1)} collective-permute-done((bf16[96,1536]{1,0:T(8,128)(2,1)}, bf16[96,1536]{1,0:T(8,128)(2,1)}, u32[]{:S(2)}, u32[]{:S(2)}) %collective-permute-start.68) | collective-permute-done | bytes 294944 | tf_op jit(solution)/shard_map/ppermute | solution.py:63
  588.4 3.2 collective-permute-done.84
  593.2 3.2 collective-permute-done.85
  622.9 3.1 collective-permute-done.90
  632.0 2.8 collective-permute-done.53
  636.4 2.5 fusion.82
  (691 shorter events, 219.6 us)
Async XLA Ops:
  10.2 28.8 %collective-permute-start.9 = (bf16[96,768]{1,0:T(8,128)(2,1)}, bf16[96,768]{1,0:T(8,128)(2,1)}, u32[]{:S(2)}, u32[]{:S(2)}) collective-permute-start(bf16[96,768]{1,0:T(8,128)(2,1)} %pad_maximum_fusion.9.refs_9_), channel_id=1, source_target_pairs={{0,4},{4,0},{8,12},{12,8},{16,20},{20,16},{24,28},{28,24},{1,5},{5... | collective-permute-start | bytes 442376 | tf_op jit(solution)/shard_map/ppermute | solution.py:63
  13.1 26.9 %collective-permute-start.7 = (bf16[96,768]{1,0:T(8,128)(2,1)}, bf16[96,768]{1,0:T(8,128)(2,1)}, u32[]{:S(2)}, u32[]{:S(2)}) collective-permute-start(bf16[96,768]{1,0:T(8,128)(2,1)} %pad_maximum_fusion.9.refs_9_), channel_id=1, source_target_pairs={{0,8},{4,12},{8,0},{12,4},{16,24},{20,28},{24,16},{28,20},{1,9},{5... | collective-permute-start | bytes 442376 | tf_op jit(solution)/shard_map/ppermute | solution.py:63
  14.7 28.8 %collective-permute-start.5 = (bf16[96,768]{1,0:T(8,128)(2,1)}, bf16[96,768]{1,0:T(8,128)(2,1)}, u32[]{:S(2)}, u32[]{:S(2)}) collective-permute-start(bf16[96,768]{1,0:T(8,128)(2,1)} %pad_maximum_fusion.9.refs_9_), channel_id=1, source_target_pairs={{0,16},{4,20},{8,24},{12,28},{16,0},{20,4},{24,8},{28,12},{1,17},{... | collective-permute-start | bytes 442376 | tf_op jit(solution)/shard_map/ppermute | solution.py:63
  17.3 26.2 %collective-permute-start.3 = (bf16[96,768]{1,0:T(8,128)(2,1)}, bf16[96,768]{1,0:T(8,128)(2,1)}, u32[]{:S(2)}, u32[]{:S(2)}) collective-permute-start(bf16[96,768]{1,0:T(8,128)(2,1)} %pad_maximum_fusion.9.refs_9_), channel_id=1, source_target_pairs={{0,24},{4,28},{8,16},{12,20},{16,8},{20,12},{24,0},{28,4},{1,25},{... | collective-permute-start | bytes 442376 | tf_op jit(solution)/shard_map/ppermute | solution.py:63
  22.5 22.7 %collective-permute-start.31 = (bf16[96,768]{1,0:T(8,128)(2,1)}, bf16[96,768]{1,0:T(8,128)(2,1)}, u32[]{:S(2)}, u32[]{:S(2)}) collective-permute-start(bf16[96,768]{1,0:T(8,128)(2,1)} %pad_maximum_fusion.10.refs_9_), channel_id=1, source_target_pairs={{0,4},{4,0},{8,12},{12,8},{16,20},{20,16},{24,28},{28,24},{1,5},{5... | collective-permute-start | bytes 442376 | tf_op jit(solution)/shard_map/ppermute | solution.py:63
  40.0 13.8 %collective-permute-start.27 = (bf16[96,768]{1,0:T(8,128)(2,1)}, bf16[96,768]{1,0:T(8,128)(2,1)S(1)}, u32[]{:S(2)}, u32[]{:S(2)}) collective-permute-start(bf16[96,768]{1,0:T(8,128)(2,1)} %pad_maximum_fusion.10.refs_9_), channel_id=1, source_target_pairs={{0,16},{4,20},{8,24},{12,28},{16,0},{20,4},{24,8},{28,12},{1,17},{... | collective-permute-start | bytes 442376 | tf_op jit(solution)/shard_map/ppermute | solution.py:63
  43.4 11.8 %collective-permute-start.25 = (bf16[96,768]{1,0:T(8,128)(2,1)}, bf16[96,768]{1,0:T(8,128)(2,1)S(1)}, u32[]{:S(2)}, u32[]{:S(2)}) collective-permute-start(bf16[96,768]{1,0:T(8,128)(2,1)} %pad_maximum_fusion.10.refs_9_), channel_id=1, source_target_pairs={{0,24},{4,28},{8,16},{12,20},{16,8},{20,12},{24,0},{28,4},{1,25},{... | collective-permute-start | bytes 442376 | tf_op jit(solution)/shard_map/ppermute | solution.py:63
  43.5 12.3 %collective-permute-start.8 = (bf16[96,768]{1,0:T(8,128)(2,1)}, bf16[96,768]{1,0:T(8,128)(2,1)S(1)}, u32[]{:S(2)}, u32[]{:S(2)}) collective-permute-start(bf16[96,768]{1,0:T(8,128)(2,1)} %collective-permute-done.7.refs_11_), channel_id=1, source_target_pairs={{0,4},{4,0},{8,12},{12,8},{16,20},{20,16},{24,28},{28,24},{1,5},{5... | collective-permute-start | bytes 442376 | tf_op jit(solution)/shard_map/ppermute | solution.py:63
  45.2 12.3 %collective-permute-start.6 = (bf16[96,768]{1,0:T(8,128)(2,1)}, bf16[96,768]{1,0:T(8,128)(2,1)S(1)}, u32[]{:S(2)}, u32[]{:S(2)}) collective-permute-start(bf16[96,768]{1,0:T(8,128)(2,1)} %collective-permute-done.5.refs_13_), channel_id=1, source_target_pairs={{0,4},{4,0},{8,12},{12,8},{16,20},{20,16},{24,28},{28,24},{1,5},{5... | collective-permute-start | bytes 442376 | tf_op jit(solution)/shard_map/ppermute | solution.py:63
  46.0 14.1 %collective-permute-start.4 = (bf16[96,768]{1,0:T(8,128)(2,1)}, bf16[96,768]{1,0:T(8,128)(2,1)S(1)}, u32[]{:S(2)}, u32[]{:S(2)}) collective-permute-start(bf16[96,768]{1,0:T(8,128)(2,1)} %collective-permute-done.3.refs_15_), channel_id=1, source_target_pairs={{0,4},{4,0},{8,12},{12,8},{16,20},{20,16},{24,28},{28,24},{1,5},{5... | collective-permute-start | bytes 442376 | tf_op jit(solution)/shard_map/ppermute | solution.py:63
  55.8 10.5 %collective-permute-start.26 = (bf16[96,768]{1,0:T(8,128)(2,1)S(1)}, bf16[96,768]{1,0:T(8,128)(2,1)S(1)}, u32[]{:S(2)}, u32[]{:S(2)}) collective-permute-start(bf16[96,768]{1,0:T(8,128)(2,1)S(1)} %collective-permute-done.25.refs_15_), channel_id=1, source_target_pairs={{0,4},{4,0},{8,12},{12,8},{16,20},{20,16},{24,28},{28,24},{1,5},{5... | collective-permute-start | bytes 442376 | tf_op jit(solution)/shard_map/ppermute | solution.py:63
  57.5 14.4 %collective-permute-start.18 = (bf16[96,1536]{1,0:T(8,128)(2,1)S(1)}, bf16[96,1536]{1,0:T(8,128)(2,1)S(1)}, u32[]{:S(2)}, u32[]{:S(2)}) collective-permute-start(bf16[96,1536]{1,0:T(8,128)(2,1)S(1)} %copy-done.29), channel_id=1, source_target_pairs={{0,24},{4,28},{8,16},{12,20},{16,8},{20,12},{24,0},{28,4},{1,25},{... | collective-permute-start | bytes 884744 | tf_op jit(solution)/shard_map/ppermute | solution.py:63
  60.1 20.7 %collective-permute-start.16 = (bf16[96,1536]{1,0:T(8,128)(2,1)S(1)}, bf16[96,1536]{1,0:T(8,128)(2,1)S(1)}, u32[]{:S(2)}, u32[]{:S(2)}) collective-permute-start(bf16[96,1536]{1,0:T(8,128)(2,1)S(1)} %copy-done.29), channel_id=1, source_target_pairs={{0,16},{4,20},{8,24},{12,28},{16,0},{20,4},{24,8},{28,12},{1,17},{... | collective-permute-start | bytes 884744 | tf_op jit(solution)/shard_map/ppermute | solution.py:63
  62.7 18.1 %collective-permute-start.14 = (bf16[96,1536]{1,0:T(8,128)(2,1)S(1)}, bf16[96,1536]{1,0:T(8,128)(2,1)S(1)}, u32[]{:S(2)}, u32[]{:S(2)}) collective-permute-start(bf16[96,1536]{1,0:T(8,128)(2,1)S(1)} %copy-done.29), channel_id=1, source_target_pairs={{0,8},{4,12},{8,0},{12,4},{16,24},{20,28},{24,16},{28,20},{1,9},{5... | collective-permute-start | bytes 884744 | tf_op jit(solution)/shard_map/ppermute | solution.py:63
  63.3 19.2 %collective-permute-start.13 = (bf16[96,1536]{1,0:T(8,128)(2,1)S(1)}, bf16[96,1536]{1,0:T(8,128)(2,1)S(1)}, u32[]{:S(2)}, u32[]{:S(2)}) collective-permute-start(bf16[96,1536]{1,0:T(8,128)(2,1)S(1)} %copy-done.29), channel_id=1, source_target_pairs={{0,4},{4,0},{8,12},{12,8},{16,20},{20,16},{24,28},{28,24},{1,5},{5... | collective-permute-start | bytes 884744 | tf_op jit(solution)/shard_map/ppermute | solution.py:63
  66.3 16.9 %collective-permute-start.1 = (bf16[2,192,768]{2,1,0:T(8,128)(2,1)S(1)}, bf16[2,192,768]{2,1,0:T(8,128)(2,1)S(1)}, u32[]{:S(2)}, u32[]{:S(2)}) collective-permute-start(bf16[2,192,768]{2,1,0:T(8,128)(2,1)S(1)} %fusion.66.refs_0_), channel_id=1, source_target_pairs={{0,2},{1,3},{2,0},{3,1},{4,6},{5,7},{6,4},{7,5},{8,10},{9,11},{10,... | collective-permute-start | bytes 1769480 | tf_op jit(solution)/shard_map/ppermute | solution.py:63
  72.0 24.3 %collective-permute-start = (bf16[2,192,768]{2,1,0:T(8,128)(2,1)S(1)}, bf16[2,192,768]{2,1,0:T(8,128)(2,1)S(1)}, u32[]{:S(2)}, u32[]{:S(2)}) collective-permute-start(bf16[2,192,768]{2,1,0:T(8,128)(2,1)S(1)} %fusion.66.refs_0_), channel_id=1, source_target_pairs={{0,1},{1,0},{2,3},{3,2},{4,5},{5,4},{6,7},{7,6},{8,9},{9,8},{10,11... | collective-permute-start | bytes 1769480 | tf_op jit(solution)/shard_map/ppermute | solution.py:63
  83.2 29.1 %collective-permute-start.2 = (bf16[2,192,768]{2,1,0:T(8,128)(2,1)S(1)}, bf16[2,192,768]{2,1,0:T(8,128)(2,1)S(1)}, u32[]{:S(2)}, u32[]{:S(2)}) collective-permute-start(bf16[2,192,768]{2,1,0:T(8,128)(2,1)S(1)} %collective-permute-done.1.refs_2_), channel_id=1, source_target_pairs={{0,1},{1,0},{2,3},{3,2},{4,5},{5,4},{6,7},{7,6},{8,9},{9,8},{10,11... | collective-permute-start | bytes 1769480 | tf_op jit(solution)/shard_map/ppermute | solution.py:63
  91.3 14.7 %collective-permute-start.17 = (bf16[96,1536]{1,0:T(8,128)(2,1)S(1)}, bf16[96,1536]{1,0:T(8,128)(2,1)S(1)}, u32[]{:S(2)}, u32[]{:S(2)}) collective-permute-start(bf16[96,1536]{1,0:T(8,128)(2,1)S(1)} %collective-permute-done.16.refs_21_), channel_id=1, source_target_pairs={{0,4},{4,0},{8,12},{12,8},{16,20},{20,16},{24,28},{28,24},{1,5},{5... | collective-permute-start | bytes 884744 | tf_op jit(solution)/shard_map/ppermute | solution.py:63
  93.1 18.4 %collective-permute-start.15 = (bf16[96,1536]{1,0:T(8,128)(2,1)S(1)}, bf16[96,1536]{1,0:T(8,128)(2,1)S(1)}, u32[]{:S(2)}, u32[]{:S(2)}) collective-permute-start(bf16[96,1536]{1,0:T(8,128)(2,1)S(1)} %collective-permute-done.14.refs_19_), channel_id=1, source_target_pairs={{0,4},{4,0},{8,12},{12,8},{16,20},{20,16},{24,28},{28,24},{1,5},{5... | collective-permute-start | bytes 884744 | tf_op jit(solution)/shard_map/ppermute | solution.py:63
  140.0 38.1 %collective-permute-start.40 = (bf16[96,1536]{1,0:T(8,128)(2,1)}, bf16[96,1536]{1,0:T(8,128)(2,1)}, u32[]{:S(2)}, u32[]{:S(2)}) collective-permute-start(bf16[96,1536]{1,0:T(8,128)(2,1)} %get-tuple-element.173.refs_17_), channel_id=1, source_target_pairs={{0,24},{4,28},{8,16},{12,20},{16,8},{20,12},{24,0},{28,4},{1,25},{... | collective-permute-start | bytes 884744 | tf_op jit(solution)/shard_map/ppermute | solution.py:63
  142.3 37.3 %collective-permute-start.38 = (bf16[96,1536]{1,0:T(8,128)(2,1)}, bf16[96,1536]{1,0:T(8,128)(2,1)}, u32[]{:S(2)}, u32[]{:S(2)}) collective-permute-start(bf16[96,1536]{1,0:T(8,128)(2,1)} %get-tuple-element.173.refs_17_), channel_id=1, source_target_pairs={{0,16},{4,20},{8,24},{12,28},{16,0},{20,4},{24,8},{28,12},{1,17},{... | collective-permute-start | bytes 884744 | tf_op jit(solution)/shard_map/ppermute | solution.py:63
  142.3 49.1 %collective-permute-start.36 = (bf16[96,1536]{1,0:T(8,128)(2,1)}, bf16[96,1536]{1,0:T(8,128)(2,1)}, u32[]{:S(2)}, u32[]{:S(2)}) collective-permute-start(bf16[96,1536]{1,0:T(8,128)(2,1)} %get-tuple-element.173.refs_17_), channel_id=1, source_target_pairs={{0,8},{4,12},{8,0},{12,4},{16,24},{20,28},{24,16},{28,20},{1,9},{5... | collective-permute-start | bytes 884744 | tf_op jit(solution)/shard_map/ppermute | solution.py:63
  144.4 49.0 %collective-permute-start.45 = (bf16[2,192,768]{2,1,0:T(8,128)(2,1)}, bf16[2,192,768]{2,1,0:T(8,128)(2,1)}, u32[]{:S(2)}, u32[]{:S(2)}) collective-permute-start(bf16[2,192,768]{2,1,0:T(8,128)(2,1)} %refs_0_), channel_id=1, source_target_pairs={{0,2},{1,3},{2,0},{3,1},{4,6},{5,7},{6,4},{7,5},{8,10},{9,11},{10,... | collective-permute-start | bytes 1769480 | tf_op jit(solution)/shard_map/ppermute | solution.py:63
  152.1 20.1 %collective-permute-start.21 = (bf16[2,192,768]{2,1,0:T(8,128)(2,1)S(1)}, bf16[2,192,768]{2,1,0:T(8,128)(2,1)S(1)}, u32[]{:S(2)}, u32[]{:S(2)}) collective-permute-start(bf16[2,192,768]{2,1,0:T(8,128)(2,1)S(1)} %fusion.105), channel_id=1, source_target_pairs={{0,2},{1,3},{2,0},{3,1},{4,6},{5,7},{6,4},{7,5},{8,10},{9,11},{10,... | collective-permute-start | bytes 1769480 | tf_op jit(solution)/shard_map/ppermute | solution.py:63
  175.4 14.0 %collective-permute-start.23 = (bf16[2,192,768]{2,1,0:T(8,128)(2,1)S(1)}, bf16[2,192,768]{2,1,0:T(8,128)(2,1)S(1)}, u32[]{:S(2)}, u32[]{:S(2)}) collective-permute-start(bf16[2,192,768]{2,1,0:T(8,128)(2,1)S(1)} %fusion.102.refs_0_), channel_id=1, source_target_pairs={{0,2},{1,3},{2,0},{3,1},{4,6},{5,7},{6,4},{7,5},{8,10},{9,11},{10,... | collective-permute-start | bytes 1769480 | tf_op jit(solution)/shard_map/ppermute | solution.py:63
  178.1 14.7 %collective-permute-start.35 = (bf16[96,1536]{1,0:T(8,128)(2,1)}, bf16[96,1536]{1,0:T(8,128)(2,1)}, u32[]{:S(2)}, u32[]{:S(2)}) collective-permute-start(bf16[96,1536]{1,0:T(8,128)(2,1)} %get-tuple-element.173.refs_17_), channel_id=1, source_target_pairs={{0,4},{4,0},{8,12},{12,8},{16,20},{20,16},{24,28},{28,24},{1,5},{5... | collective-permute-start | bytes 884744 | tf_op jit(solution)/shard_map/ppermute | solution.py:63
  179.6 34.0 %collective-permute-start.22 = (bf16[2,192,768]{2,1,0:T(8,128)(2,1)S(1)}, bf16[2,192,768]{2,1,0:T(8,128)(2,1)}, u32[]{:S(2)}, u32[]{:S(2)}) collective-permute-start(bf16[2,192,768]{2,1,0:T(8,128)(2,1)S(1)} %fusion.102.refs_0_), channel_id=1, source_target_pairs={{0,1},{1,0},{2,3},{3,2},{4,5},{5,4},{6,7},{7,6},{8,9},{9,8},{10,11... | collective-permute-start | bytes 1769480 | tf_op jit(solution)/shard_map/ppermute | solution.py:63
  189.4 24.2 %collective-permute-start.24 = (bf16[2,192,768]{2,1,0:T(8,128)(2,1)S(1)}, bf16[2,192,768]{2,1,0:T(8,128)(2,1)}, u32[]{:S(2)}, u32[]{:S(2)}) collective-permute-start(bf16[2,192,768]{2,1,0:T(8,128)(2,1)S(1)} %collective-permute-done.23.refs_2_), channel_id=1, source_target_pairs={{0,1},{1,0},{2,3},{3,2},{4,5},{5,4},{6,7},{7,6},{8,9},{9,8},{10,11... | collective-permute-start | bytes 1769480 | tf_op jit(solution)/shard_map/ppermute | solution.py:63
  191.4 10.0 %collective-permute-start.41 = (bf16[96,1536]{1,0:T(8,128)(2,1)}, bf16[96,1536]{1,0:T(8,128)(2,1)S(1)}, u32[]{:S(2)}, u32[]{:S(2)}) collective-permute-start(bf16[96,1536]{1,0:T(8,128)(2,1)} %collective-permute-done.40.refs_23_), channel_id=1, source_target_pairs={{0,4},{4,0},{8,12},{12,8},{16,20},{20,16},{24,28},{28,24},{1,5},{5... | collective-permute-start | bytes 884744 | tf_op jit(solution)/shard_map/ppermute | solution.py:63
  192.8 14.8 %collective-permute-start.39 = (bf16[96,1536]{1,0:T(8,128)(2,1)}, bf16[96,1536]{1,0:T(8,128)(2,1)S(1)}, u32[]{:S(2)}, u32[]{:S(2)}) collective-permute-start(bf16[96,1536]{1,0:T(8,128)(2,1)} %collective-permute-done.38.refs_21_), channel_id=1, source_target_pairs={{0,4},{4,0},{8,12},{12,8},{16,20},{20,16},{24,28},{28,24},{1,5},{5... | collective-permute-start | bytes 884744 | tf_op jit(solution)/shard_map/ppermute | solution.py:63
  193.4 20.2 %collective-permute-start.37 = (bf16[96,1536]{1,0:T(8,128)(2,1)}, bf16[96,1536]{1,0:T(8,128)(2,1)S(1)}, u32[]{:S(2)}, u32[]{:S(2)}) collective-permute-start(bf16[96,1536]{1,0:T(8,128)(2,1)} %collective-permute-done.36.refs_19_), channel_id=1, source_target_pairs={{0,4},{4,0},{8,12},{12,8},{16,20},{20,16},{24,28},{28,24},{1,5},{5... | collective-permute-start | bytes 884744 | tf_op jit(solution)/shard_map/ppermute | solution.py:63
  201.4 39.7 %collective-permute-start.44 = (bf16[2,192,768]{2,1,0:T(8,128)(2,1)}, bf16[2,192,768]{2,1,0:T(8,128)(2,1)S(1)}, u32[]{:S(2)}, u32[]{:S(2)}) collective-permute-start(bf16[2,192,768]{2,1,0:T(8,128)(2,1)} %refs_0_), channel_id=1, source_target_pairs={{0,1},{1,0},{2,3},{3,2},{4,5},{5,4},{6,7},{7,6},{8,9},{9,8},{10,11... | collective-permute-start | bytes 1769480 | tf_op jit(solution)/shard_map/ppermute | solution.py:63
  207.7 33.4 %collective-permute-start.46 = (bf16[2,192,768]{2,1,0:T(8,128)(2,1)}, bf16[2,192,768]{2,1,0:T(8,128)(2,1)S(1)}, u32[]{:S(2)}, u32[]{:S(2)}) collective-permute-start(bf16[2,192,768]{2,1,0:T(8,128)(2,1)} %collective-permute-done.45.refs_2_), channel_id=1, source_target_pairs={{0,1},{1,0},{2,3},{3,2},{4,5},{5,4},{6,7},{7,6},{8,9},{9,8},{10,11... | collective-permute-start | bytes 1769480 | tf_op jit(solution)/shard_map/ppermute | solution.py:63
  277.6 66.2 %collective-permute-start.42 = (bf16[2,2,192,768]{3,2,1,0:T(8,128)(2,1)}, bf16[2,2,192,768]{3,2,1,0:T(8,128)(2,1)}, u32[]{:S(2)}, u32[]{:S(2)}) collective-permute-start(bf16[2,2,192,768]{3,2,1,0:T(8,128)(2,1)} %get-tuple-element.45), channel_id=1, source_target_pairs={{0,1},{1,0},{2,3},{3,2},{4,5},{5,4},{6,7},{7,6},{8,9},{9,8},{10,11... | collective-permute-start | bytes 3538952 | tf_op jit(solution)/shard_map/ppermute | solution.py:63
  286.8 12.4 %collective-permute-start.70 = (bf16[192,192]{1,0:T(8,128)(2,1)S(1)}, bf16[192,192]{1,0:T(8,128)(2,1)S(1)}, u32[]{:S(2)}, u32[]{:S(2)}) collective-permute-start(bf16[192,192]{1,0:T(8,128)(2,1)S(1)} %bitcast.368), channel_id=1, source_target_pairs={{0,3},{1,2},{2,1},{3,0},{4,7},{5,6},{6,5},{7,4},{8,11},{9,10},{10,... | collective-permute-start | bytes 221192 | tf_op jit(solution)/shard_map/ppermute | solution.py:63
  287.9 11.4 %collective-permute-start.71 = (bf16[192,192]{1,0:T(8,128)(2,1)S(1)}, bf16[192,192]{1,0:T(8,128)(2,1)S(1)}, u32[]{:S(2)}, u32[]{:S(2)}) collective-permute-start(bf16[192,192]{1,0:T(8,128)(2,1)S(1)} %bitcast.366), channel_id=1, source_target_pairs={{0,2},{1,3},{2,0},{3,1},{4,6},{5,7},{6,4},{7,5},{8,10},{9,11},{10,... | collective-permute-start | bytes 221192 | tf_op jit(solution)/shard_map/ppermute | solution.py:63
  289.0 10.2 %collective-permute-start.72 = (bf16[192,192]{1,0:T(8,128)(2,1)S(1)}, bf16[192,192]{1,0:T(8,128)(2,1)S(1)}, u32[]{:S(2)}, u32[]{:S(2)}) collective-permute-start(bf16[192,192]{1,0:T(8,128)(2,1)S(1)} %bitcast.365), channel_id=1, source_target_pairs={{0,1},{1,0},{2,3},{3,2},{4,5},{5,4},{6,7},{7,6},{8,9},{9,8},{10,11... | collective-permute-start | bytes 221192 | tf_op jit(solution)/shard_map/ppermute | solution.py:63
  289.0 51.4 %collective-permute-start.47 = (bf16[2,2,192,768]{3,2,1,0:T(8,128)(2,1)}, bf16[2,2,192,768]{3,2,1,0:T(8,128)(2,1)}, u32[]{:S(2)}, u32[]{:S(2)}) collective-permute-start(bf16[2,2,192,768]{3,2,1,0:T(8,128)(2,1)} %get-tuple-element.52), channel_id=1, source_target_pairs={{0,1},{1,0},{2,3},{3,2},{4,5},{5,4},{6,7},{7,6},{8,9},{9,8},{10,11... | collective-permute-start | bytes 3538952 | tf_op jit(solution)/shard_map/ppermute | solution.py:63
  307.2 15.4 %collective-permute-start.73 = (bf16[4,96,768]{2,1,0:T(8,128)(2,1)S(1)}, bf16[4,96,768]{2,1,0:T(8,128)(2,1)}, u32[]{:S(2)}, u32[]{:S(2)}) collective-permute-start(bf16[4,96,768]{2,1,0:T(8,128)(2,1)S(1)} %fusion.104), channel_id=1, source_target_pairs={{0,4},{4,0},{8,12},{12,8},{16,20},{20,16},{24,28},{28,24},{1,5},{5... | collective-permute-start | bytes 1769480 | tf_op jit(solution)/shard_map/ppermute | solution.py:63
  324.6 9.9 %collective-permute-start.76 = (bf16[96,768]{1,0:T(8,128)(2,1)S(1)}, bf16[96,768]{1,0:T(8,128)(2,1)S(1)}, u32[]{:S(2)}, u32[]{:S(2)}) collective-permute-start(bf16[96,768]{1,0:T(8,128)(2,1)S(1)} %get-tuple-element.170), channel_id=1, source_target_pairs={{0,24},{4,28},{8,16},{12,20},{16,8},{20,12},{24,0},{28,4},{1,25},{... | collective-permute-start | bytes 442376 | tf_op jit(solution)/shard_map/ppermute | solution.py:63
  326.9 12.7 %collective-permute-start.75 = (bf16[96,768]{1,0:T(8,128)(2,1)S(1)}, bf16[96,768]{1,0:T(8,128)(2,1)S(1)}, u32[]{:S(2)}, u32[]{:S(2)}) collective-permute-start(bf16[96,768]{1,0:T(8,128)(2,1)S(1)} %get-tuple-element.171), channel_id=1, source_target_pairs={{0,16},{4,20},{8,24},{12,28},{16,0},{20,4},{24,8},{28,12},{1,17},{... | collective-permute-start | bytes 442376 | tf_op jit(solution)/shard_map/ppermute | solution.py:63
  331.2 42.1 %collective-permute-start.77 = (bf16[4,96,1536]{2,1,0:T(8,128)(2,1)S(1)}, bf16[4,96,1536]{2,1,0:T(8,128)(2,1)}, u32[]{:S(2)}, u32[]{:S(2)}) collective-permute-start(bf16[4,96,1536]{2,1,0:T(8,128)(2,1)S(1)} %fusion.86), channel_id=1, source_target_pairs={{0,4},{4,0},{8,12},{12,8},{16,20},{20,16},{24,28},{28,24},{1,5},{5... | collective-permute-start | bytes 3538952 | tf_op jit(solution)/shard_map/ppermute | solution.py:63
  342.9 16.3 %collective-permute-start.48 = (bf16[2,192,768]{2,1,0:T(8,128)(2,1)S(1)}, bf16[2,192,768]{2,1,0:T(8,128)(2,1)S(1)}, u32[]{:S(2)}, u32[]{:S(2)}) collective-permute-start(bf16[2,192,768]{2,1,0:T(8,128)(2,1)S(1)} %fusion.107), channel_id=1, source_target_pairs={{0,2},{1,3},{2,0},{3,1},{4,6},{5,7},{6,4},{7,5},{8,10},{9,11},{10,... | collective-permute-start | bytes 1769480 | tf_op jit(solution)/shard_map/ppermute | solution.py:63
  345.5 23.9 %collective-permute-start.43 = (bf16[2,192,768]{2,1,0:T(8,128)(2,1)S(1)}, bf16[2,192,768]{2,1,0:T(8,128)(2,1)S(1)}, u32[]{:S(2)}, u32[]{:S(2)}) collective-permute-start(bf16[2,192,768]{2,1,0:T(8,128)(2,1)S(1)} %fusion.106), channel_id=1, source_target_pairs={{0,2},{1,3},{2,0},{3,1},{4,6},{5,7},{6,4},{7,5},{8,10},{9,11},{10,... | collective-permute-start | bytes 1769480 | tf_op jit(solution)/shard_map/ppermute | solution.py:63
  372.5 13.2 %collective-permute-start.50 = (bf16[2,192,768]{2,1,0:T(8,128)(2,1)}, bf16[2,192,768]{2,1,0:T(8,128)(2,1)}, u32[]{:S(2)}, u32[]{:S(2)}) collective-permute-start(bf16[2,192,768]{2,1,0:T(8,128)(2,1)} %get-tuple-element.130.refs_0_), channel_id=1, source_target_pairs={{0,2},{1,3},{2,0},{3,1},{4,6},{5,7},{6,4},{7,5},{8,10},{9,11},{10,... | collective-permute-start | bytes 1769480 | tf_op jit(solution)/shard_map/ppermute | solution.py:63
  376.0 13.5 %collective-permute-start.78 = (bf16[96,1536]{1,0:T(8,128)(2,1)}, bf16[96,1536]{1,0:T(8,128)(2,1)}, u32[]{:S(2)}, u32[]{:S(2)}) collective-permute-start(bf16[96,1536]{1,0:T(8,128)(2,1)} %get-tuple-element.159), channel_id=1, source_target_pairs={{0,8},{4,12},{8,0},{12,4},{16,24},{20,28},{24,16},{28,20},{1,9},{5... | collective-permute-start | bytes 884744 | tf_op jit(solution)/shard_map/ppermute | solution.py:63
  376.0 16.5 %collective-permute-start.80 = (bf16[96,1536]{1,0:T(8,128)(2,1)}, bf16[96,1536]{1,0:T(8,128)(2,1)}, u32[]{:S(2)}, u32[]{:S(2)}) collective-permute-start(bf16[96,1536]{1,0:T(8,128)(2,1)} %get-tuple-element.160), channel_id=1, source_target_pairs={{0,24},{4,28},{8,16},{12,20},{16,8},{20,12},{24,0},{28,4},{1,25},{... | collective-permute-start | bytes 884744 | tf_op jit(solution)/shard_map/ppermute | solution.py:63
  378.2 24.5 %collective-permute-start.79 = (bf16[96,1536]{1,0:T(8,128)(2,1)}, bf16[96,1536]{1,0:T(8,128)(2,1)}, u32[]{:S(2)}, u32[]{:S(2)}) collective-permute-start(bf16[96,1536]{1,0:T(8,128)(2,1)} %get-tuple-element.161), channel_id=1, source_target_pairs={{0,16},{4,20},{8,24},{12,28},{16,0},{20,4},{24,8},{28,12},{1,17},{... | collective-permute-start | bytes 884744 | tf_op jit(solution)/shard_map/ppermute | solution.py:63
  380.4 24.7 %collective-permute-start.49 = (bf16[2,192,768]{2,1,0:T(8,128)(2,1)}, bf16[2,192,768]{2,1,0:T(8,128)(2,1)}, u32[]{:S(2)}, u32[]{:S(2)}) collective-permute-start(bf16[2,192,768]{2,1,0:T(8,128)(2,1)} %get-tuple-element.130.refs_0_), channel_id=1, source_target_pairs={{0,1},{1,0},{2,3},{3,2},{4,5},{5,4},{6,7},{7,6},{8,9},{9,8},{10,11... | collective-permute-start | bytes 1769480 | tf_op jit(solution)/shard_map/ppermute | solution.py:63
  385.7 19.4 %collective-permute-start.51 = (bf16[2,192,768]{2,1,0:T(8,128)(2,1)}, bf16[2,192,768]{2,1,0:T(8,128)(2,1)}, u32[]{:S(2)}, u32[]{:S(2)}) collective-permute-start(bf16[2,192,768]{2,1,0:T(8,128)(2,1)} %collective-permute-done.50.refs_2_), channel_id=1, source_target_pairs={{0,1},{1,0},{2,3},{3,2},{4,5},{5,4},{6,7},{7,6},{8,9},{9,8},{10,11... | collective-permute-start | bytes 1769480 | tf_op jit(solution)/shard_map/ppermute | solution.py:63
  447.0 26.3 %collective-permute-start.54 = (bf16[2,19968]{1,0:T(2,128)(2,1)S(1)}, bf16[2,19968]{1,0:T(2,128)(2,1)S(1)}, u32[]{:S(2)}, u32[]{:S(2)}) collective-permute-start(bf16[2,19968]{1,0:T(2,128)(2,1)S(1)} %constant_dynamic-update-slice_fusion.16), channel_id=1, source_target_pairs={{0,1},{1,0},{2,3},{3,2},{4,5},{5,4},{6,7},{7,6},{8,9},{9,8},{10,11... | collective-permute-start | bytes 239624 | tf_op jit(solution)/shard_map/ppermute | solution.py:63
  448.4 23.4 %collective-permute-start.59 = (bf16[192,192]{1,0:T(8,128)(2,1)S(1)}, bf16[192,192]{1,0:T(8,128)(2,1)S(1)}, u32[]{:S(2)}, u32[]{:S(2)}) collective-permute-start(bf16[192,192]{1,0:T(8,128)(2,1)S(1)} %bitcast.367), channel_id=1, source_target_pairs={{0,3},{1,2},{2,1},{3,0},{4,7},{5,6},{6,5},{7,4},{8,11},{9,10},{10,... | collective-permute-start | bytes 221192 | tf_op jit(solution)/shard_map/ppermute | solution.py:63
  449.7 23.6 %collective-permute-start.60 = (bf16[192,192]{1,0:T(8,128)(2,1)S(1)}, bf16[192,192]{1,0:T(8,128)(2,1)S(1)}, u32[]{:S(2)}, u32[]{:S(2)}) collective-permute-start(bf16[192,192]{1,0:T(8,128)(2,1)S(1)} %bitcast.364), channel_id=1, source_target_pairs={{0,2},{1,3},{2,0},{3,1},{4,6},{5,7},{6,4},{7,5},{8,10},{9,11},{10,... | collective-permute-start | bytes 221192 | tf_op jit(solution)/shard_map/ppermute | solution.py:63
  450.6 22.7 %collective-permute-start.61 = (bf16[192,192]{1,0:T(8,128)(2,1)S(1)}, bf16[192,192]{1,0:T(8,128)(2,1)S(1)}, u32[]{:S(2)}, u32[]{:S(2)}) collective-permute-start(bf16[192,192]{1,0:T(8,128)(2,1)S(1)} %bitcast.363), channel_id=1, source_target_pairs={{0,1},{1,0},{2,3},{3,2},{4,5},{5,4},{6,7},{7,6},{8,9},{9,8},{10,11... | collective-permute-start | bytes 221192 | tf_op jit(solution)/shard_map/ppermute | solution.py:63
  450.6 164.9 %collective-permute-start.52 = (bf16[2,2,192,768]{3,2,1,0:T(8,128)(2,1)}, bf16[2,2,192,768]{3,2,1,0:T(8,128)(2,1)}, u32[]{:S(2)}, u32[]{:S(2)}) collective-permute-start(bf16[2,2,192,768]{3,2,1,0:T(8,128)(2,1)} %get-tuple-element.59), channel_id=1, source_target_pairs={{0,1},{1,0},{2,3},{3,2},{4,5},{5,4},{6,7},{7,6},{8,9},{9,8},{10,11... | collective-permute-start | bytes 3538952 | tf_op jit(solution)/shard_map/ppermute | solution.py:63
  471.8 70.8 %collective-permute-start.66 = (bf16[4,96,1536]{2,1,0:T(8,128)(2,1)}, bf16[4,96,1536]{2,1,0:T(8,128)(2,1)}, u32[]{:S(2)}, u32[]{:S(2)}) collective-permute-start(bf16[4,96,1536]{2,1,0:T(8,128)(2,1)} %fusion.85), channel_id=1, source_target_pairs={{0,4},{4,0},{8,12},{12,8},{16,20},{20,16},{24,28},{28,24},{1,5},{5... | collective-permute-start | bytes 3538952 | tf_op jit(solution)/shard_map/ppermute | solution.py:63
  478.7 22.9 %collective-permute-start.56 = (bf16[2,19968]{1,0:T(2,128)(2,1)S(1)}, bf16[2,19968]{1,0:T(2,128)(2,1)S(1)}, u32[]{:S(2)}, u32[]{:S(2)}) collective-permute-start(bf16[2,19968]{1,0:T(2,128)(2,1)S(1)} %pad_maximum_fusion.11), channel_id=1, source_target_pairs={{0,4},{4,0},{8,12},{12,8},{16,20},{20,16},{24,28},{28,24},{1,5},{5... | collective-permute-start | bytes 239624 | tf_op jit(solution)/shard_map/ppermute | solution.py:63
  512.7 14.0 %collective-permute-start.62 = (bf16[4,96,768]{2,1,0:T(8,128)(2,1)S(1)}, bf16[4,96,768]{2,1,0:T(8,128)(2,1)S(1)}, u32[]{:S(2)}, u32[]{:S(2)}) collective-permute-start(bf16[4,96,768]{2,1,0:T(8,128)(2,1)S(1)} %fusion.103), channel_id=1, source_target_pairs={{0,4},{4,0},{8,12},{12,8},{16,20},{20,16},{24,28},{28,24},{1,5},{5... | collective-permute-start | bytes 1769480 | tf_op jit(solution)/shard_map/ppermute | solution.py:63
  530.1 12.3 %collective-permute-start.64 = (bf16[96,768]{1,0:T(8,128)(2,1)S(1)}, bf16[96,768]{1,0:T(8,128)(2,1)S(1)}, u32[]{:S(2)}, u32[]{:S(2)}) collective-permute-start(bf16[96,768]{1,0:T(8,128)(2,1)S(1)} %get-tuple-element.168), channel_id=1, source_target_pairs={{0,16},{4,20},{8,24},{12,28},{16,0},{20,4},{24,8},{28,12},{1,17},{... | collective-permute-start | bytes 442376 | tf_op jit(solution)/shard_map/ppermute | solution.py:63
  547.3 12.5 %collective-permute-start.67 = (bf16[96,1536]{1,0:T(8,128)(2,1)}, bf16[96,1536]{1,0:T(8,128)(2,1)S(1)}, u32[]{:S(2)}, u32[]{:S(2)}) collective-permute-start(bf16[96,1536]{1,0:T(8,128)(2,1)} %get-tuple-element.156), channel_id=1, source_target_pairs={{0,8},{4,12},{8,0},{12,4},{16,24},{20,28},{24,16},{28,20},{1,9},{5... | collective-permute-start | bytes 884744 | tf_op jit(solution)/shard_map/ppermute | solution.py:63
  547.3 16.2 %collective-permute-start.69 = (bf16[96,1536]{1,0:T(8,128)(2,1)}, bf16[96,1536]{1,0:T(8,128)(2,1)S(1)}, u32[]{:S(2)}, u32[]{:S(2)}) collective-permute-start(bf16[96,1536]{1,0:T(8,128)(2,1)} %get-tuple-element.157), channel_id=1, source_target_pairs={{0,24},{4,28},{8,16},{12,20},{16,8},{20,12},{24,0},{28,4},{1,25},{... | collective-permute-start | bytes 884744 | tf_op jit(solution)/shard_map/ppermute | solution.py:63
  548.9 25.8 %collective-permute-start.68 = (bf16[96,1536]{1,0:T(8,128)(2,1)}, bf16[96,1536]{1,0:T(8,128)(2,1)}, u32[]{:S(2)}, u32[]{:S(2)}) collective-permute-start(bf16[96,1536]{1,0:T(8,128)(2,1)} %get-tuple-element.158), channel_id=1, source_target_pairs={{0,16},{4,20},{8,24},{12,28},{16,0},{20,4},{24,8},{28,12},{1,17},{... | collective-permute-start | bytes 884744 | tf_op jit(solution)/shard_map/ppermute | solution.py:63
  621.7 13.1 %collective-permute-start.53 = (bf16[2,192,768]{2,1,0:T(8,128)(2,1)}, bf16[2,192,768]{2,1,0:T(8,128)(2,1)}, u32[]{:S(2)}, u32[]{:S(2)}) collective-permute-start(bf16[2,192,768]{2,1,0:T(8,128)(2,1)} %fusion.108), channel_id=1, source_target_pairs={{0,2},{1,3},{2,0},{3,1},{4,6},{5,7},{6,4},{7,5},{8,10},{9,11},{10,... | collective-permute-start | bytes 1769480 | tf_op jit(solution)/shard_map/ppermute | solution.py:63
  (160 other events, 1821.5 us)

commit v2 on v1

v2 whole, which is shorter than its diff:
```python
import functools

import jax
import jax.numpy as jnp
from jax import lax
from jax.experimental import pallas as pl
from jax.experimental.pallas import tpu as pltpu
from jax.sharding import PartitionSpec as P

D = 768
HEADS = 12
FF = 3072
LAYERS = 2
HEAD_DIM = 64
ROT = 16
SMALL = 9984

EPS_NORM = 1e-05
EPS_SQUARE = 1e-30
RATE = 0.5
DECAY = 0.5
NEG_LARGE = -1e30
SCORE_SCALE = HEAD_DIM ** (-0.5)
CONTRACT_LAST = (((1,), (1,)), ((), ()))
CONTRACT_FIRST = (((0,), (0,)), ((), ()))
VMEM_BYTES = 56 * 1024 * 1024
BF16 = jnp.bfloat16
F32 = jnp.float32


def unpack(vector):
    return jnp.split(vector, [D, 2 * D, 3 * D, 4 * D, 7 * D, 8 * D, 8 * D + FF], axis=-1)


def apply_layer_norm(inputs):
    centred = inputs - jnp.mean(inputs, axis=-1, keepdims=True)
    variance = jnp.mean(centred * centred, axis=-1, keepdims=True)
    inverse = lax.rsqrt(variance + EPS_NORM)
    return (centred * inverse, inverse)


def norm_back(grad_scaled, scaled, inverse):
    mean_grad = jnp.mean(grad_scaled, axis=-1, keepdims=True)
    mean_cross = jnp.mean(grad_scaled * scaled, axis=-1, keepdims=True)
    return (grad_scaled - mean_grad - scaled * mean_cross) * inverse


def rotary_tables(length):
    halfway = ROT // 2
    frequency = 10000.0 ** (-2.0 * jnp.arange(halfway, dtype=F32) / ROT)
    angles = jnp.arange(length).astype(F32)[:, None] * frequency[None, :]
    cosine, sine = jnp.cos(angles), jnp.sin(angles)
    rest = jnp.ones((length, HEAD_DIM - ROT), F32)
    none = jnp.zeros((length, halfway), F32)
    keep = jnp.concatenate([cosine, cosine, rest], axis=1)
    ahead = jnp.concatenate([-sine, none, 0.0 * rest], axis=1)
    behind = jnp.concatenate([none, sine, 0.0 * rest], axis=1)
    return tuple(jnp.concatenate([table, table], axis=1) for table in (keep, ahead, behind))


def swap(values, axis, bits):
    size = lax.axis_size(axis)
    return lax.ppermute(values, axis, [(i, i ^ bits) for i in range(size)])


def sum_pairwise(values, axis, wire=F32):
    bits = 1
    while bits < lax.axis_size(axis):
        sent = values.astype(wire)
        values = sent.astype(F32) + swap(sent, axis, bits).astype(F32)
        bits *= 2
    return values


def both_halves(own):
    return jnp.stack([own, swap(own, "seq", 2)], axis=-3)


def core_sum(keep, send):
    total = keep + swap(send, "seq", 1).astype(F32)
    return total, total.astype(BF16)


def finish_sum(total, low_total):
    return total + jnp.flip(swap(low_total, "seq", 2), axis=0).astype(F32)


def own_sum_over_seq(keep, send):
    total, low_total = core_sum(keep, send)
    return total[0] + swap(low_total[1], "seq", 2).astype(F32)


def gather_rows(rows):
    if lax.axis_size("dp") != 8:
        return [lax.all_gather(rows, "dp", axis=0, tiled=True)]
    even = [rows] + [swap(rows, "dp", 2 * k) for k in (1, 2, 3)]
    pieces = []
    for piece in even:
        pieces += [piece, swap(piece, "dp", 1)]
    return pieces


def pair_sum(keep, send, z_place):
    summed = keep + swap(send, "dp", 1).astype(F32)
    own = lax.dynamic_index_in_dim(summed, z_place, 0, keepdims=False)
    return own, [
        lax.dynamic_index_in_dim(summed, z_place ^ k, 0, keepdims=False).astype(BF16)
        for k in range(1, summed.shape[0])
    ]


def exchange_parts(parts):
    return [swap(part, "dp", 2 * (k + 1)) for k, part in enumerate(parts)]


def in_place_order(pieces, index):
    stacked = list(pieces)
    bits = 1
    while bits < len(stacked):
        flag = (index // bits) % 2 == 1
        stacked = [
            jnp.where(flag, stacked[i ^ bits], stacked[i]) for i in range(len(stacked))
        ]
        bits *= 2
    return stacked


def exchange_blocks(blocks, index):
    size = lax.axis_size("seq")
    received = []
    for k in range(size):
        block = lax.dynamic_index_in_dim(blocks, index ^ k, 0, keepdims=False)
        received.append(block if k == 0 else swap(block, "seq", k))
    return in_place_order(received, index)


def heads_together(values):
    heads = values.shape[-1] // (3 * HEAD_DIM)
    lead = values.shape[:-1]
    by_head = values.reshape(*lead, heads, 3 * HEAD_DIM)
    return jnp.concatenate(
        [
            by_head[..., : 2 * HEAD_DIM].reshape(*lead, heads * 2 * HEAD_DIM),
            by_head[..., 2 * HEAD_DIM :].reshape(*lead, heads * HEAD_DIM),
        ],
        axis=-1,
    )


def heads_apart(values):
    heads = values.shape[-1] // (3 * HEAD_DIM)
    lead = values.shape[:-1]
    pairs, last = jnp.split(values, [heads * 2 * HEAD_DIM], axis=-1)
    return jnp.concatenate(
        [
            pairs.reshape(*lead, heads, 2 * HEAD_DIM),
            last.reshape(*lead, heads, HEAD_DIM),
        ],
        axis=-1,
    ).reshape(values.shape)


def place_tokens(dst, own, near, core_bit, y_here, chunk):
    for bit in (0, 1):

        @pl.when(core_bit == bit)
        def _():
            first, second = (own, near) if bit == 0 else (near, own)
            dst[:chunk] = first[y_here]
            dst[chunk:] = second[y_here]


def spread_tokens(value, keep, send, core_bit, y_here, chunk):
    for bit in (0, 1):

        @pl.when(core_bit == bit)
        def _():
            mine = value[:chunk] if bit == 0 else value[chunk:]
            other = value[chunk:] if bit == 0 else value[:chunk]
            keep[pl.ds(y_here, 1)] = mine[None]
            send[pl.ds(y_here, 1)] = other.astype(send.dtype)[None]


def gelu_and_slope(v):
    magnitude = jnp.abs(v) * 0.7071067811865476
    t = 1.0 / (1.0 + 0.3275911 * magnitude)
    falling = jnp.exp(-0.5 * v * v)
    poly = t * (
        0.254829592
        + t * (-0.284496736 + t * (1.421413741 + t * (-1.453152027 + t * 1.061405429)))
    )
    tail = 0.5 * poly * falling
    cdf = jnp.where(v >= 0.0, 1.0 - tail, tail)
    return v * cdf, cdf + v * falling * 0.3989422804014327


def weight_copies(dp_place, sources, targets, sems):
    copies = []
    for (pieces, first), target in zip(sources, targets):
        rows, width = pieces[0].shape[0], target.shape[1]
        for k, piece in enumerate(pieces):
            offset = 0 if len(pieces) == 1 else pl.multiple_of((k ^ dp_place) * rows, 16)
            copies.append(
                pltpu.make_async_copy(
                    piece if piece.shape[1] == width else piece.at[:, pl.ds(first, width)],
                    target.at[pl.ds(offset, rows), :],
                    sems.at[len(copies)],
                )
            )
    return copies


def start_all(copies):
    for copy in copies:
        copy.start()


def wait_all(copies):
    for copy in copies:
        copy.wait()


def turn(pair, tables, sign):
    keep_tab, ahead_tab, behind_tab = tables
    ahead = pltpu.roll(pair, 2 * HEAD_DIM - ROT // 2, 1) * ahead_tab[...]
    behind = pltpu.roll(pair, ROT // 2, 1) * behind_tab[...]
    return pair * keep_tab[...] + sign * (ahead + behind)


def forward_kernel(count_a, count_b, place, *refs):
    refs = list(refs)

    def take(count):
        taken, refs[:] = refs[:count], refs[count:]
        return taken

    own, near, vec = take(3)
    tables = take(3)
    (w_out,) = take(1)
    pieces_a, pieces_b = take(count_a), take(count_b)
    keep, send, xhat, qk, val, att, lse, hid, slope = refs[-14:-5]
    whole_a, whole_b, k_all, v_all, sems = refs[-5:]
    core_bit, y_bit, dp_place = place[0], place[1], place[2]
    step = pl.program_id(0)
    wide = 3 * val.shape[1]
    source_b = (pieces_b, 0) if count_b else (pieces_a, pieces_a[0].shape[1] - whole_b.shape[1])
    copies = weight_copies(dp_place, [(pieces_a, 0), source_b], [whole_a, whole_b], sems)
    copies_a, copies_b = copies[:count_a], copies[count_a:]

    @pl.when(step == 0)
    def _():
        start_all(copies)

    chunk = own.shape[1]
    block = 2 * chunk
    y_here = step ^ y_bit
    place_tokens(xhat, own, near, core_bit, y_here, chunk)
    scaled = xhat[...].astype(F32)
    normed_one = (scaled * vec[0:1] + vec[1:2]).astype(BF16)
    normed_two = (scaled * vec[2:3] + vec[3:4]).astype(BF16)

    @pl.when(step == 0)
    def _():
        wait_all(copies_a)

    heads = val.shape[-1] // HEAD_DIM
    joined = jnp.dot(normed_one, whole_a[:, :wide], preferred_element_type=F32) + vec[5:6, :wide]
    for h in range(heads):
        at_q, at_k = 2 * HEAD_DIM * h, 2 * HEAD_DIM * h + HEAD_DIM
        turned = turn(joined[:, at_q : at_k + HEAD_DIM], tables, 1.0)
        qk[:, at_q : at_k + HEAD_DIM] = turned.astype(BF16)
        k_all[h, pl.ds(step * block, block)] = turned[:, HEAD_DIM:].astype(BF16)
        first = 2 * HEAD_DIM * heads + HEAD_DIM * h
        v_all[h, pl.ds(step * block, block)] = joined[:, first : first + HEAD_DIM].astype(BF16)
    val[...] = joined[:, 2 * HEAD_DIM * heads :].astype(BF16)
    row = lax.broadcasted_iota(jnp.int32, (block, block), 0)
    column = lax.broadcasted_iota(jnp.int32, (block, block), 1)
    lane = lax.broadcasted_iota(jnp.int32, (block, 128), 1)
    for here in range(2):

        @pl.when(step == here)
        def _():
            log_sums = jnp.zeros((block, 128), F32)
            for h in range(heads):
                at_q = 2 * HEAD_DIM * h
                query = qk[:, at_q : at_q + HEAD_DIM] * jnp.asarray(SCORE_SCALE, BF16)
                scores = []
                for j in range(here + 1):
                    part = lax.dot_general(
                        query,
                        k_all[h, block * j : block * (j + 1)],
                        CONTRACT_LAST,
                        preferred_element_type=F32,
                    )
                    if j == here:
                        part = jnp.where(column <= row, part, NEG_LARGE)
                    scores.append(part)
                largest = functools.reduce(
                    jnp.maximum, [jnp.max(part, axis=-1, keepdims=True) for part in scores]
                )
                total = 0.0
                mixed = 0.0
                for j, part in enumerate(scores):
                    exponent = jnp.exp(part - largest)
                    total = total + jnp.sum(exponent, axis=-1, keepdims=True)
                    mixed = mixed + jnp.dot(
                        exponent.astype(BF16),
                        v_all[h, block * j : block * (j + 1)],
                        preferred_element_type=F32,
                    )
                att[:, HEAD_DIM * h : HEAD_DIM * (h + 1)] = (mixed / total).astype(BF16)
                log_sums = jnp.where(lane == h, largest + jnp.log(total), log_sums)
            lse[...] = log_sums.T[:8]

    @pl.when(step == 0)
    def _():
        wait_all(copies_b)

    quarter = hid.shape[-1]
    hidden_pre = (
        jnp.dot(normed_two, whole_b[:, :quarter], preferred_element_type=F32) + vec[4:5, :quarter]
    )
    hidden, gradient = gelu_and_slope(hidden_pre)
    hid[...] = hidden.astype(BF16)
    slope[...] = gradient
    partial = jnp.dot(att[...], w_out[...], preferred_element_type=F32) + lax.dot_general(
        hid[...], whole_b[:, quarter:], CONTRACT_LAST, preferred_element_type=F32
    )
    spread_tokens(partial, keep, send, core_bit, y_here, chunk)


def add_up(sums, place_row, values):
    sums[place_row : place_row + 1, : values.shape[-1]] += jnp.sum(
        values.astype(F32), axis=0, keepdims=True
    )


def mlp_backward_kernel(count, place, *refs):
    own, near, vec, xhat, slope = refs[:5]
    pieces = refs[5 : 5 + count]
    grad, grad_pre, grad_two, sums, whole_b, sems = refs[-6:]
    core_bit, y_bit, dp_place = place[0], place[1], place[2]
    step = pl.program_id(0)
    copies = weight_copies(
        dp_place, [(pieces, pieces[0].shape[1] - whole_b.shape[1])], [whole_b], sems
    )

    @pl.when(step == 0)
    def _():
        start_all(copies)
        sums[...] = jnp.zeros_like(sums)

    chunk = own.shape[1]
    place_tokens(grad, own, near, core_bit, step ^ y_bit, chunk)

    @pl.when(step == 0)
    def _():
        wait_all(copies)

    quarter = slope.shape[-1]
    grad_hidden = jnp.dot(grad[...], whole_b[:, quarter:], preferred_element_type=F32)
    low_pre = (grad_hidden * slope[...]).astype(BF16)
    grad_pre[...] = low_pre
    normed = lax.dot_general(
        low_pre, whole_b[:, :quarter], CONTRACT_LAST, preferred_element_type=F32
    )
    grad_two[...] = normed * vec[2:3]
    add_up(sums, 0, normed * xhat[...].astype(F32))
    add_up(sums, 1, normed)
    add_up(sums, 2, low_pre)
    add_up(sums, 3, grad[...])


def attention_backward_kernel(count, place, *refs):
    refs = list(refs)

    def take(number):
        taken, refs[:] = refs[:number], refs[number:]
        return taken

    grad, vec = take(2)
    tables = take(3)
    w_out, xhat, qk, val, lse, grad_two = take(6)
    pieces = take(count)
    keep, send, grad_joined, sums, whole_a, dk_all, dv_all, dq_all, sems = refs[-9:]
    core_bit, y_bit, dp_place = place[0], place[1], place[2]
    step = 1 - pl.program_id(0)
    copies = weight_copies(dp_place, [(pieces, 0)], [whole_a], sems)

    @pl.when(step == 1)
    def _():
        start_all(copies)
        sums[...] = jnp.zeros_like(sums)

    block = grad.shape[0]
    chunk = block // 2
    heads = val.shape[-1] // HEAD_DIM
    grad_att = lax.dot_general(
        grad[...], w_out[...], CONTRACT_LAST, preferred_element_type=F32
    ).astype(BF16)
    row = lax.broadcasted_iota(jnp.int32, (block, block), 0)
    column = lax.broadcasted_iota(jnp.int32, (block, block), 1)
    for here in range(2):

        @pl.when(step == here)
        def _():
            for h in range(heads):
                at_q, at_k = 2 * HEAD_DIM * h, 2 * HEAD_DIM * h + HEAD_DIM
                query = qk[block * here : block * (here + 1), at_q:at_k]
                query = query * jnp.asarray(SCORE_SCALE, BF16)
                near_grad = grad_att[:, HEAD_DIM * h : HEAD_DIM * (h + 1)]
                log_row = lse[h : h + 1]
                probs, grad_probs, keys = [], [], []
                delta = 0.0
                for j in range(here + 1):
                    key = qk[block * j : block * (j + 1), at_k : at_k + HEAD_DIM]
                    value = val[block * j : block * (j + 1), HEAD_DIM * h : HEAD_DIM * (h + 1)]
                    scores = lax.dot_general(
                        key, query, CONTRACT_LAST, preferred_element_type=F32
                    )
                    prob = jnp.exp(scores - log_row)
                    if j == here:
                        prob = jnp.where(row <= column, prob, 0.0)
                    grad_prob = lax.dot_general(
                        value, near_grad, CONTRACT_LAST, preferred_element_type=F32
                    )
                    delta = delta + jnp.sum(prob * grad_prob, axis=0, keepdims=True)
                    probs.append(prob)
                    grad_probs.append(grad_prob)
                    keys.append(key)
                dq = 0.0
                for j in range(here + 1):
                    grad_score = (probs[j] * (grad_probs[j] - delta)).astype(BF16)
                    dk = jnp.dot(grad_score, query, preferred_element_type=F32)
                    dv = jnp.dot(probs[j].astype(BF16), near_grad, preferred_element_type=F32)
                    if here == 1:
                        dk_all[h, block * j : block * (j + 1)] = dk
                        dv_all[h, block * j : block * (j + 1)] = dv
                    else:
                        dk_all[h, block * j : block * (j + 1)] += dk
                        dv_all[h, block * j : block * (j + 1)] += dv
                    dq = dq + lax.dot_general(
                        grad_score, keys[j], CONTRACT_FIRST, preferred_element_type=F32
                    )
                dq_all[h] = dq * SCORE_SCALE

    for h in range(heads):
        pair = jnp.concatenate([dq_all[h], dk_all[h, pl.ds(step * block, block)]], axis=1)
        at_q = 2 * HEAD_DIM * h
        grad_joined[:, at_q : at_q + 2 * HEAD_DIM] = turn(pair, tables, -1.0).astype(BF16)
        first = 2 * HEAD_DIM * heads + HEAD_DIM * h
        grad_joined[:, first : first + HEAD_DIM] = dv_all[h, pl.ds(step * block, block)].astype(
            BF16
        )

    @pl.when(step == 1)
    def _():
        wait_all(copies)

    normed = lax.dot_general(
        grad_joined[...], whole_a[:, : grad_joined.shape[1]], CONTRACT_LAST, preferred_element_type=F32
    )
    spread_tokens(
        normed * vec[0:1] + grad_two[...], keep, send, core_bit, step ^ y_bit, chunk
    )
    add_up(sums, 0, normed * xhat[...].astype(F32))
    add_up(sums, 1, normed)
    add_up(sums, 2, grad_joined[...])


def outer_sum(flags, lefts, rights):
    total = 0.0
    for s, (left, right) in enumerate(zip(lefts, rights)):
        kept = jnp.where(flags[s] > 0, right, jnp.zeros_like(right))
        total = total + lax.dot_general(left, kept, CONTRACT_FIRST, preferred_element_type=F32)
    return total


def store_rows(value, outs, first, x_bit):
    columns = pl.ds(first, value.shape[1])
    if len(outs) == 1:
        outs[0][:, columns] = value.astype(BF16)
        return
    keep, send = outs
    rows = keep.shape[1]
    for bit in (0, 1):

        @pl.when(x_bit == bit)
        def _():
            for z in range(keep.shape[0]):
                at = rows * (2 * z + bit)
                to = rows * (2 * z + 1 - bit)
                keep[z, :, columns] = value[at : at + rows]
                send[z, :, columns] = value[to : to + rows].astype(BF16)


def mlp_outer_kernel(count, n_outs, scalars, vec, *refs):
    groups = [refs[count * n : count * (n + 1)] for n in range(5)]
    outs, outward = refs[-1 - n_outs : -1], refs[-1]
    xhat, grad, grad_pre, hid, att = ([ref[...] for ref in group] for group in groups)
    quarter = hid[0].shape[1]
    x_bit, flags = scalars[0], [scalars[1 + s] for s in range(count)]
    normed = [(x.astype(F32) * vec[2:3] + vec[3:4]).astype(BF16) for x in xhat]
    outward[...] = outer_sum(flags, att, grad).astype(BF16)
    store_rows(outer_sum(flags, normed, grad_pre), outs, 0, x_bit)
    store_rows(outer_sum(flags, grad, hid), outs, quarter, x_bit)


def qkv_outer_kernel(count, n_outs, scalars, vec, *refs):
    groups = [refs[count * n : count * (n + 1)] for n in range(2)]
    outward, outs = refs[2 * count], refs[-n_outs:]
    xhat, grad_joined = ([ref[...] for ref in group] for group in groups)
    wide = grad_joined[0].shape[1]
    x_bit, flags = scalars[0], [scalars[1 + s] for s in range(count)]
    normed = [(x.astype(F32) * vec[0:1] + vec[1:2]).astype(BF16) for x in xhat]
    store_rows(outer_sum(flags, normed, grad_joined), outs, 0, x_bit)
    store_rows(outward[...].astype(F32), outs, wide, x_bit)


def natural_heads(values):
    heads = values.shape[1] // (3 * HEAD_DIM)
    parts = []
    for h in range(heads):
        parts.append(values[:, 2 * HEAD_DIM * h : 2 * HEAD_DIM * (h + 1)])
        at = 2 * HEAD_DIM * heads + HEAD_DIM * h
        parts.append(values[:, at : at + HEAD_DIM])
    return parts


def matrix_cuts(width):
    unit = width // 12
    return [0, 3 * unit, 4 * unit, 8 * unit, width]


def gradient_kernel(counts, cuts, *refs):
    sources_b = refs[: counts[0]]
    sources_a = refs[counts[0] : counts[0] + counts[1]]
    grads, row_sums, col_sums = refs[-3:]
    part_b = sum(ref[...].astype(F32) for ref in sources_b)
    part_a = sum(ref[...].astype(F32) for ref in sources_a) if sources_a else None
    if part_a is None:
        part_a, part_b = part_b[:, cuts[4] - cuts[2] :], part_b[:, : cuts[4] - cuts[2]]
    at = 0
    for part in natural_heads(part_a[:, : cuts[1]]):
        grads[0, :, at : at + part.shape[1]] = part
        at += part.shape[1]
    grads[0, :, at : cuts[2]] = part_a[:, cuts[1] :]
    grads[0, :, cuts[2] :] = part_b
    whole = grads[0]
    squares = whole * whole + EPS_SQUARE
    col_sums[0] = jnp.sum(squares, axis=0, keepdims=True)
    lane = lax.broadcasted_iota(jnp.int32, (whole.shape[0], 128), 1)
    by_row = jnp.zeros((whole.shape[0], 128), F32)
    for m in range(4):
        total = jnp.sum(squares[:, cuts[m] : cuts[m + 1]], axis=1, keepdims=True)
        by_row = jnp.where(lane == m, total, by_row)
    row_sums[0] = by_row


def scaled_update(grads, row_inverse, col_inverse, cuts, m):
    columns = slice(cuts[m], cuts[m + 1])
    return grads[0, :, columns] * row_inverse[0, :, m : m + 1] * col_inverse[0, :, columns]


def square_kernel(cuts, grads, master, row_inverse, col_inverse, sums):
    row = lax.broadcasted_iota(jnp.int32, (8, 128), 0)
    lane = lax.broadcasted_iota(jnp.int32, (8, 128), 1)
    result = jnp.zeros((8, 128), F32)
    for m in range(4):
        update = scaled_update(grads, row_inverse, col_inverse, cuts, m)
        old = master[0, :, cuts[m] : cuts[m + 1]]
        for at, values in ((0, update), (1, old)):
            total = jnp.sum(jnp.sum(values * values, axis=0, keepdims=True), axis=1, keepdims=True)
            result = jnp.where((row == at) & (lane == m), total, result)
    sums[0] = result


def update_kernel(cuts, grads, master, row_inverse, col_inverse, factor, new, new_low):
    for m in range(4):
        update = scaled_update(grads, row_inverse, col_inverse, cuts, m)
        columns = slice(cuts[m], cuts[m + 1])
        fresh = master[0, :, columns] - factor[0, :, m : m + 1] * update
        new[0, :, columns] = fresh
        new_low[0, :, columns] = fresh.astype(BF16)


def whole_spec(shape):
    return pl.BlockSpec(shape, lambda *_: (0,) * len(shape))


def in_any(count):
    return [pl.BlockSpec(memory_space=pl.ANY)] * count


def cost(micros):
    return pl.CostEstimate(
        flops=int(micros * 10**9), bytes_accessed=int(micros * 10**6), transcendentals=0
    )


def rows_spec(rows, width, block_of):
    return pl.BlockSpec((rows, width), lambda t, *_: (block_of(t), 0))


def run_forward(place, chunks, vec, tables, weight, riders=()):
    w_out, pieces_a, pieces_b = weight
    chunk = chunks[0].shape[1]
    block, length = 2 * chunk, 4 * chunk
    count_a, count_b = len(pieces_a), len(pieces_b)
    out_wide = w_out.shape[0]
    heads = out_wide // HEAD_DIM
    wide = 3 * out_wide
    quarter = FF * out_wide // D

    def same(t):
        return t

    widths = [
        (D, BF16),
        (2 * out_wide, BF16),
        (out_wide, BF16),
        (out_wide, BF16),
        (quarter, BF16),
        (quarter, F32),
    ]
    shapes = [jax.ShapeDtypeStruct((length, width), kind) for width, kind in widths]
    specs = [rows_spec(block, width, same) for width, _ in widths]
    shapes.insert(4, jax.ShapeDtypeStruct((8, length), F32))
    specs.insert(4, pl.BlockSpec((8, block), lambda t, *_: (0, t)))
    return pl.pallas_call(
        functools.partial(forward_kernel, count_a, count_b),
        grid_spec=pltpu.PrefetchScalarGridSpec(
            num_scalar_prefetch=1,
            grid=(2,),
            in_specs=[
                *[whole_spec((2, chunk, D))] * 2,
                whole_spec((8, D)),
                *[rows_spec(block, 2 * HEAD_DIM, same)] * 3,
                whole_spec(w_out.shape),
                *in_any(count_a + count_b + len(riders)),
            ],
            out_specs=[whole_spec((2, chunk, D))] * 2 + specs,
            scratch_shapes=[
                pltpu.VMEM((D, wide + out_wide), BF16),
                pltpu.VMEM((D, 2 * quarter), BF16),
                pltpu.VMEM((heads, length, HEAD_DIM), BF16),
                pltpu.VMEM((heads, length, HEAD_DIM), BF16),
                pltpu.SemaphoreType.DMA((count_a + max(count_b, 1),)),
            ],
        ),
        out_shape=[
            jax.ShapeDtypeStruct((2, chunk, D), F32),
            jax.ShapeDtypeStruct((2, chunk, D), BF16),
            *shapes,
        ],
        compiler_params=pltpu.CompilerParams(vmem_limit_bytes=VMEM_BYTES),
        cost_estimate=cost(13),
        name="layer_forward",
    )(place, *chunks, vec, *tables, w_out, *pieces_a, *pieces_b, *riders)


def run_mlp_backward(place, chunks, vec, weight, xhat, slope, riders=()):
    _, pieces_a, pieces_b = weight
    pieces = pieces_b or pieces_a
    chunk = chunks[0].shape[1]
    block, length = 2 * chunk, 4 * chunk
    quarter = slope.shape[1]

    def same(t):
        return t

    return pl.pallas_call(
        functools.partial(mlp_backward_kernel, len(pieces)),
        grid_spec=pltpu.PrefetchScalarGridSpec(
            num_scalar_prefetch=1,
            grid=(2,),
            in_specs=[
                *[whole_spec((2, chunk, D))] * 2,
                whole_spec((8, D)),
                rows_spec(block, D, same),
                rows_spec(block, quarter, same),
                *in_any(len(pieces) + len(riders)),
            ],
            out_specs=[
                rows_spec(block, D, same),
                rows_spec(block, quarter, same),
                rows_spec(block, D, same),
                whole_spec((8, D)),
            ],
            scratch_shapes=[
                pltpu.VMEM((D, 2 * quarter), BF16),
                pltpu.SemaphoreType.DMA((len(pieces),)),
            ],
        ),
        out_shape=[
            jax.ShapeDtypeStruct((length, D), BF16),
            jax.ShapeDtypeStruct((length, quarter), BF16),
            jax.ShapeDtypeStruct((length, D), F32),
            jax.ShapeDtypeStruct((8, D), F32),
        ],
        compiler_params=pltpu.CompilerParams(vmem_limit_bytes=VMEM_BYTES),
        cost_estimate=cost(6),
        name="mlp_backward",
    )(place, *chunks, vec, xhat, slope, *pieces, *riders)


def run_attention_backward(
    place, grad, vec, tables, weight, xhat, qk, val, lse, grad_two, riders=()
):
    w_out, pieces, _ = weight
    length = grad.shape[0]
    block, chunk = length // 2, length // 4
    out_wide = w_out.shape[0]
    heads = out_wide // HEAD_DIM
    wide = 3 * out_wide

    def turned(t):
        return 1 - t

    return pl.pallas_call(
        functools.partial(attention_backward_kernel, len(pieces)),
        grid_spec=pltpu.PrefetchScalarGridSpec(
            num_scalar_prefetch=1,
            grid=(2,),
            in_specs=[
                rows_spec(block, D, turned),
                whole_spec((8, D)),
                *[rows_spec(block, 2 * HEAD_DIM, turned)] * 3,
                whole_spec(w_out.shape),
                rows_spec(block, D, turned),
                whole_spec(qk.shape),
                whole_spec(val.shape),
                pl.BlockSpec((8, block), lambda t, *_: (0, 1 - t)),
                rows_spec(block, D, turned),
                *in_any(len(pieces) + len(riders)),
            ],
            out_specs=[
                *[whole_spec((2, chunk, D))] * 2,
                rows_spec(block, wide, turned),
                whole_spec((8, D)),
            ],
            scratch_shapes=[
                pltpu.VMEM((D, wide + out_wide), BF16),
                pltpu.VMEM((heads, length, HEAD_DIM), F32),
                pltpu.VMEM((heads, length, HEAD_DIM), F32),
                pltpu.VMEM((heads, block, HEAD_DIM), F32),
                pltpu.SemaphoreType.DMA((len(pieces),)),
            ],
        ),
        out_shape=[
            jax.ShapeDtypeStruct((2, chunk, D), F32),
            jax.ShapeDtypeStruct((2, chunk, D), BF16),
            jax.ShapeDtypeStruct((length, wide), BF16),
            jax.ShapeDtypeStruct((8, D), F32),
        ],
        compiler_params=pltpu.CompilerParams(vmem_limit_bytes=VMEM_BYTES),
        cost_estimate=cost(11),
        name="attention_backward",
    )(place, grad, vec, *tables, w_out, xhat, qk, val, lse, grad_two, *pieces, *riders)


def outer_outputs(split, columns, total, place):
    if split:
        shape = (4, D // 8, columns)
        return [jax.ShapeDtypeStruct(shape, F32), jax.ShapeDtypeStruct(shape, BF16)], [
            whole_spec(shape)
        ] * 2
    return [jax.ShapeDtypeStruct((D, total), BF16)], [
        pl.BlockSpec((D, columns), lambda *_: (0, place))
    ]


def run_mlp_outer(scalars, vec, groups, split, total, riders=()):
    arrays = [array for group in groups for array in group]
    out_wide, quarter = groups[4][0].shape[1], groups[3][0].shape[1]
    shapes, specs = outer_outputs(split, 2 * quarter, total, 0)
    return pl.pallas_call(
        functools.partial(mlp_outer_kernel, len(groups[0]), len(shapes)),
        grid_spec=pltpu.PrefetchScalarGridSpec(
            num_scalar_prefetch=1,
            grid=(1,),
            in_specs=[
                whole_spec((8, D)),
                *[whole_spec(array.shape) for array in arrays],
                *in_any(len(riders)),
            ],
            out_specs=specs + [whole_spec((out_wide, D))],
        ),
        out_shape=shapes + [jax.ShapeDtypeStruct((out_wide, D), BF16)],
        compiler_params=pltpu.CompilerParams(vmem_limit_bytes=VMEM_BYTES),
        cost_estimate=cost(10),
        name="mlp_outer",
    )(scalars, vec, *arrays, *riders)


def run_qkv_outer(scalars, vec, groups, outward, split, both=None, riders=()):
    arrays = [array for group in groups for array in group] + [outward]
    columns = groups[1][0].shape[1] + outward.shape[1]
    total = columns if both is None else both.shape[1]
    shapes, specs = outer_outputs(split, columns, total, total // columns - 1)
    riders = list(riders) if both is None else [both, *riders]
    return pl.pallas_call(
        functools.partial(qkv_outer_kernel, len(groups[0]), len(shapes)),
        grid_spec=pltpu.PrefetchScalarGridSpec(
            num_scalar_prefetch=1,
            grid=(1,),
            in_specs=[
                whole_spec((8, D)),
                *[whole_spec(array.shape) for array in arrays],
                *in_any(len(riders)),
            ],
            out_specs=specs,
        ),
        out_shape=shapes,
        input_output_aliases={} if both is None else {2 + len(arrays): 0},
        compiler_params=pltpu.CompilerParams(vmem_limit_bytes=VMEM_BYTES),
        cost_estimate=cost(6),
        name="qkv_outer",
    )(scalars, vec, *arrays, *riders)


def run_gradient(sources_b, sources_a, layer, shape, earlier=None):
    _, rows, width = shape
    arrays = [*sources_b, *sources_a]
    riders = [] if earlier is None else [earlier]
    return pl.pallas_call(
        functools.partial(
            gradient_kernel, (len(sources_b), len(sources_a)), matrix_cuts(width)
        ),
        grid=(1,),
        in_specs=[whole_spec(array.shape) for array in arrays] + in_any(len(riders)),
        out_specs=[
            pl.BlockSpec((1, rows, width), lambda *_: (layer, 0, 0)),
            whole_spec((1, rows, 128)),
            whole_spec((1, 1, width)),
        ],
        out_shape=[
            jax.ShapeDtypeStruct(shape, F32),
            jax.ShapeDtypeStruct((1, rows, 128), F32),
            jax.ShapeDtypeStruct((1, 1, width), F32),
        ],
        input_output_aliases={len(arrays): 0} if riders else {},
        compiler_params=pltpu.CompilerParams(vmem_limit_bytes=VMEM_BYTES),
        cost_estimate=cost(2),
        name="gradient",
    )(*arrays, *riders)


def layer_spec(*shape):
    return pl.BlockSpec((1, *shape), lambda i: (i, 0, 0))


def run_squares(grads, master, row_inverse, col_inverse):
    layers, rows, width = grads.shape
    return pl.pallas_call(
        functools.partial(square_kernel, matrix_cuts(width)),
        grid=(layers,),
        in_specs=[
            layer_spec(rows, width),
            layer_spec(rows, width),
            layer_spec(rows, 4),
            layer_spec(1, width),
        ],
        out_specs=layer_spec(8, 128),
        out_shape=jax.ShapeDtypeStruct((layers, 8, 128), F32),
        compiler_params=pltpu.CompilerParams(vmem_limit_bytes=VMEM_BYTES),
        cost_estimate=cost(2),
        name="squares",
    )(grads, master, row_inverse, col_inverse)


def run_update(grads, master, row_inverse, col_inverse, factor):
    layers, rows, width = grads.shape
    return pl.pallas_call(
        functools.partial(update_kernel, matrix_cuts(width)),
        grid=(layers,),
        in_specs=[
            layer_spec(rows, width),
            layer_spec(rows, width),
            layer_spec(rows, 4),
            layer_spec(1, width),
            layer_spec(1, 4),
        ],
        out_specs=[layer_spec(rows, width)] * 2,
        out_shape=[
            jax.ShapeDtypeStruct(grads.shape, F32),
            jax.ShapeDtypeStruct(grads.shape, BF16),
        ],
        compiler_params=pltpu.CompilerParams(vmem_limit_bytes=VMEM_BYTES),
        cost_estimate=cost(2),
        name="update",
    )(grads, master, row_inverse, col_inverse, factor)


def pass_through_kernel(*refs):
    del refs


def after(values, *others):
    return pl.pallas_call(
        pass_through_kernel,
        in_specs=in_any(1 + len(others)),
        out_specs=pl.BlockSpec(memory_space=pl.ANY),
        out_shape=jax.ShapeDtypeStruct(values.shape, values.dtype),
        input_output_aliases={0: 0},
        name="after",
    )(values, *others)


def out_rows(columns, dp_place, seq_place):
    stacked = jnp.concatenate(
        in_place_order(columns, dp_place) if len(columns) > 1 else columns, axis=0
    )
    size = lax.axis_size("seq")
    blocks = stacked.reshape(size, D // size, -1)
    return jnp.concatenate(exchange_blocks(blocks, seq_place), axis=1)


def on_device(block_in, cotangent, labels, master, small_params, row_state, col_state, small_state):
    sequences, chunk = block_in.shape[:2]
    group_count = lax.axis_size("seq")
    seq_place, dp_place = lax.axis_index("seq"), lax.axis_index("dp")
    place = jnp.stack([seq_place % 2, seq_place // 2, dp_place]).astype(jnp.int32)
    length = chunk * group_count
    flags = (labels == 0).astype(jnp.int32)
    train_flag = flags.astype(F32)
    scalars = jnp.concatenate([(dp_place % 2).astype(jnp.int32)[None], flags])
    query_flag = 1.0 - train_flag
    wide, out_wide, quarter = 3 * D // group_count, D // group_count, FF // group_count
    cuts = matrix_cuts(master.shape[2])
    split = lax.axis_size("dp") == 8
    x_bit, z_place = dp_place % 2, dp_place // 2
    tables = rotary_tables(length)

    def normalise(stream):
        scaled, inverse = apply_layer_norm(stream)
        low_scaled = scaled.astype(BF16)
        return (scaled, inverse), low_scaled

    stream = both_halves(block_in).astype(F32)
    norm, low_scaled = normalise(stream)
    near = swap(low_scaled, "seq", 1)
    chunks = [(low_scaled[s], near[s]) for s in range(sequences)]

    low = master.astype(BF16)
    first_a = jnp.concatenate(
        [heads_together(low[0, :, : cuts[1]]), low[0, :, cuts[1] : cuts[2]]], axis=1
    )
    pieces_a = gather_rows(first_a)
    pieces_b = [lax.all_gather(low[0, :, cuts[2] :], "dp", axis=0, tiled=True)]
    rows_one = jnp.concatenate(
        [heads_together(low[1, :, : cuts[1]]), low[1, :, cuts[1] :]], axis=1
    )
    whole_one = lax.all_gather(
        after(rows_one, *pieces_b), "dp", axis=0, tiled=True
    )
    weights = [
        (out_rows([piece[:, wide:] for piece in pieces_a], dp_place, seq_place), pieces_a, pieces_b)
    ]
    vectors, params = [], []
    for i in range(LAYERS):
        param = unpack(small_params[i])
        params.append(param)
        bias_qkv = heads_together(lax.dynamic_slice_in_dim(param[4], seq_place * wide, wide))
        bias_up = lax.dynamic_slice_in_dim(param[6], seq_place * quarter, quarter)
        vectors.append(
            jnp.stack(
                [
                    *param[:4],
                    jnp.pad(bias_up, (0, D - quarter)),
                    jnp.pad(bias_qkv, (0, D - wide)),
                    jnp.zeros((D,), F32),
                    jnp.zeros((D,), F32),
                ]
            )
        )

    streams = [stream[s] for s in range(sequences)]
    norms, saved_all = [[(norm[0][s], norm[1][s]) for s in range(sequences)]], []
    for i in range(LAYERS):
        last = i == LAYERS - 1
        saved_all.append([])
        next_chunks, next_norms = [], []
        riders = []
        for s in range(sequences):
            keep, send, *saved = run_forward(
                place, chunks[s], vectors[i], tables, weights[i], riders
            )
            saved_all[i].append(saved)
            bias = params[i][5] + params[i][7]
            if last:
                streams[s] = streams[s][0] + own_sum_over_seq(keep, send) + bias
                continue
            total, low_total = core_sum(keep, send)
            riders = [low_total]
            streams[s] = streams[s] + finish_sum(total, low_total) + bias
            norm, low_scaled = normalise(streams[s])
            next_norms.append(norm)
            next_chunks.append((low_scaled, swap(low_scaled, "seq", 1)))
        if i == 0:
            whole_one = after(whole_one, keep)
            weights.append(
                (
                    out_rows([whole_one[:, wide : wide + out_wide]], dp_place, seq_place),
                    [whole_one],
                    [],
                )
            )
        chunks = next_chunks
        norms.append(next_norms)
    block_out = jnp.stack(streams).astype(BF16)

    low_grad = both_halves(cotangent)
    near = swap(low_grad, "seq", 1)
    chunks = [(low_grad[s], near[s]) for s in range(sequences)]
    grads = [low_grad[s].astype(F32) for s in range(sequences)]
    example_parts, sources = [None] * LAYERS, [None] * LAYERS
    only_one = jnp.where(seq_place == 0, 1.0, 0.0)
    for i in reversed(range(LAYERS)):
        last = i == 0
        xhats, qks, vals, atts, lses, hids, slopes = zip(*saved_all[i])
        mlp, attention, next_chunks = [], [], []
        riders = []

        def attention_part(s, riders=()):
            out = run_attention_backward(
                place,
                mlp[s][0],
                vectors[i],
                tables,
                weights[i],
                xhats[s],
                qks[s],
                vals[s],
                lses[s],
                mlp[s][2],
                riders,
            )
            attention.append(out)
            norm = norms[i][s]
            if last:
                grad_scaled = own_sum_over_seq(out[0], out[1])
                grads[s] = grads[s][0] + norm_back(grad_scaled, norm[0][0], norm[1][0])
                return []
            total, low_total = core_sum(out[0], out[1])
            grads[s] = grads[s] + norm_back(finish_sum(total, low_total), *norm)
            low_grad = grads[s].astype(BF16)
            next_chunks.append((low_grad, swap(low_grad, "seq", 1)))
            return [low_total]

        for s in range(sequences):
            mlp.append(
                run_mlp_backward(
                    place, chunks[s], vectors[i], weights[i], xhats[s], slopes[s], riders
                )
            )
            if not last:
                riders = attention_part(s)
        *both, outward = run_mlp_outer(
            scalars,
            vectors[i],
            [xhats, [out[0] for out in mlp], [out[1] for out in mlp], hids, atts],
            split and last,
            2 * quarter if last else master.shape[2],
            riders,
        )
        blocks = outward.reshape(out_wide, group_count, out_wide).transpose(1, 0, 2)
        outward = jnp.concatenate(exchange_blocks(blocks, seq_place), axis=0)
        if last:
            riders = both[-1:]
            for s in range(sequences):
                attention_part(s, riders)
                if split and s == 0:
                    own_b, parts_b = pair_sum(*both, z_place)
                    riders = parts_b
        groups = [xhats, [out[2] for out in attention]]
        if not last:
            (both,) = run_qkv_outer(scalars, vectors[i], groups, outward, False, both[0])
            parts = lax.psum_scatter(both, "dp", scatter_dimension=0, tiled=True)
            sources[i] = ([parts], [])
        else:
            rest = run_qkv_outer(scalars, vectors[i], groups, outward, split)
            if split:
                own_a, parts_a = pair_sum(*rest, z_place)
                sources[i] = (
                    [own_b, *exchange_parts(parts_b)],
                    [own_a, *exchange_parts(parts_a)],
                )
            else:
                sources[i] = tuple(
                    [lax.psum_scatter(part[0], "dp", scatter_dimension=0, tiled=True)]
                    for part in (both, rest)
                )
        chunks = next_chunks
        def spread(values, width):
            return lax.dynamic_update_slice(
                jnp.zeros((sequences, group_count * width), F32), values, (0, seq_place * width)
            )

        sums_m = jnp.stack([out[3] for out in mlp])
        sums_t = jnp.stack([out[3] for out in attention])
        grad_sum = sums_m[:, 3] * only_one
        example_parts[i] = jnp.concatenate(
            [
                sums_t[:, 0],
                sums_t[:, 1],
                sums_m[:, 0],
                sums_m[:, 1],
                spread(heads_apart(sums_t[:, 2, :wide]), wide),
                grad_sum,
                spread(sums_m[:, 2, :quarter], quarter),
                grad_sum,
            ],
            axis=1,
        )
    grad_stream = jnp.stack(grads)

    examples = sum_pairwise(jnp.concatenate(example_parts, axis=1), "seq", BF16)
    totals = sum_pairwise(
        jnp.stack(
            [
                jnp.sum(train_flag[:, None] * examples, axis=0),
                jnp.sum(query_flag[:, None] * examples, axis=0),
            ]
        ),
        "dp",
        BF16,
    )
    small_flat, query_total = totals[0], totals[1]
    example_norms = jnp.sum(examples * examples, axis=1) / (LAYERS * SMALL * length)
    influence = jnp.sum(examples * query_total, axis=1) / jnp.sqrt(
        length * LAYERS * SMALL * (jnp.mean(query_total * query_total) + 1e-06)
    )

    reduced_all, row_sums, col_sums = None, [None] * LAYERS, [None] * LAYERS
    for i in reversed(range(LAYERS)):
        reduced_all, row_sums[i], col_sums[i] = run_gradient(
            *sources[i], i, master.shape, reduced_all
        )
    matrix_width = jnp.array([3 * D, D, FF, FF], F32)
    row_part = jnp.concatenate(row_sums, axis=0)[:, :, :4].transpose(0, 2, 1)
    col_part = jnp.concatenate(col_sums, axis=0)[:, 0]
    row_total = sum_pairwise(row_part, "seq")
    fresh_row_moments = DECAY * row_state + (1.0 - DECAY) * (
        row_total / matrix_width[None, :, None]
    )
    packed = sum_pairwise(
        jnp.concatenate(
            [col_part, jnp.sum(row_part, axis=2), jnp.sum(row_state, axis=2)], axis=1
        ),
        "dp",
    )
    col_stats = DECAY * col_state + (1.0 - DECAY) * (packed[:, : cuts[4]] / D)
    square_part, state_sum = packed[:, cuts[4] : cuts[4] + 4], packed[:, cuts[4] + 4 :]
    row_inverse = lax.rsqrt(fresh_row_moments).transpose(0, 2, 1)
    col_inverse = lax.rsqrt(col_stats)[:, None]
    square_sums = run_squares(reduced_all, master, row_inverse, col_inverse)
    group_sums = sum_pairwise(
        jnp.concatenate([square_sums[:, :2, :4], square_part[:, None]], axis=1), "seq"
    )
    square_totals = sum_pairwise(group_sums[:, :2], "dp")
    row_mean = (
        DECAY * state_sum + (1.0 - DECAY) * (group_sums[:, 2] / matrix_width[None, :])
    ) / D
    entry_count = D * matrix_width
    update_rms = jnp.sqrt(row_mean * square_totals[:, 0] / entry_count[None, :])
    weight_rms = jnp.sqrt(square_totals[:, 1] / entry_count[None, :])
    factor = RATE * weight_rms * jnp.sqrt(row_mean) / jnp.maximum(1.0, update_rms)
    new_master, new_low = run_update(
        reduced_all, master, row_inverse, col_inverse, factor[:, None]
    )
    small_grads = small_flat.reshape(LAYERS, SMALL)
    small_moments = DECAY * small_state + (1.0 - DECAY) * (small_grads * small_grads + EPS_SQUARE)
    small_update = small_grads * lax.rsqrt(small_moments)
    new_pieces = []
    for update_piece, param_piece in zip(unpack(small_update), unpack(small_params)):
        piece_rms = jnp.sqrt(jnp.mean(update_piece * update_piece, axis=-1, keepdims=True))
        param_rms = jnp.sqrt(jnp.mean(param_piece * param_piece, axis=-1, keepdims=True))
        new_pieces.append(
            param_piece - RATE * param_rms * (update_piece / jnp.maximum(1.0, piece_rms))
        )
    small_new = jnp.concatenate(new_pieces, axis=-1)
    return (
        block_out,
        grad_stream,
        example_norms,
        influence,
        reduced_all,
        fresh_row_moments,
        col_stats,
        new_master,
        new_low,
        small_grads,
        small_moments,
        small_new,
    )


def solution(mesh):
    placed = (
        P("dp", "seq", None),
        P("dp", "seq", None),
        P("dp"),
        P(None, "dp", "seq"),
        P(),
        P(None, None, "dp"),
        P(None, "seq"),
        P(),
    )
    return jax.shard_map(
        on_device,
        mesh=mesh,
        in_specs=placed,
        out_specs=(
            P("dp", "seq", None),
            P("dp", "seq", None),
            P("dp"),
            P("dp"),
            P(None, "dp", "seq"),
            P(None, None, "dp"),
            P(None, "seq"),
            P(None, "dp", "seq"),
            P(None, "dp", "seq"),
            P(),
            P(),
            P(),
        ),
        check_vma=False,
    )
```

time: 647 us -> 518 us (0.80)
  waiting for transfers between devices: 222 us -> 96.4 us
  Pallas kernels: 117 us -> 199 us
  local copies, waits for them, and re-layouts: 88.6 us -> 52.3 us
  starting transfers between devices: 90 us -> 59.8 us
  matrix products: 28 us -> 0 us
  between operations: 3.99 us -> 16.6 us
    ppermute x91 -> x66, waiting for transfers between devices: 222 us -> 88.8 us  [swap(): return lax.ppermute(values, axis, [(i, i ^ bits) for i in range(size)])]
    pallas_call x4 -> x22, Pallas kernels: 117 us -> 199 us  [the longest x4 64 us: run_forward(): pl.pallas_call(functools.partial(forward_kernel, count_a, count_b), grid_...]
    ppermute x91 -> x66, starting transfers between devices: 90 us -> 59.5 us  [swap(): return lax.ppermute(values, axis, [(i, i ^ bits) for i in range(size)])]
    dot_general x8 -> x0, matrix products: 28 us -> none  [outer(): lax.dot_general(tokens(left), tokens(right), CONTRACT_FIRST, preferred_el...]
    concatenate x10 -> x2, local copies, waits for them, and re-layouts: 25.7 us -> 3.48 us  [the longest x1 2.07 us: on_device(): jnp.concatenate([heads_together(low[1, :, :cuts[1]]), low[1, :, cuts[1]:]...]
    add x14 -> x7, other arithmetic: 20.4 us -> 7.15 us  [the longest x4 2.98 us: core_sum(): total = keep + swap(send, 'seq', 1).astype(F32)]
    concatenate x7 -> x5, other arithmetic: 13.6 us -> 2.97 us  [the longest x2 1.63 us: on_device(): outward = jnp.concatenate(exchange_blocks(blocks, seq_place), axis=0)]
    convert_element_type x14 -> x2, local copies, waits for them, and re-layouts: 11.3 us -> 1.78 us  [pair_sum(): lax.dynamic_index_in_dim(summed, z_place ^ k, 0, keepdims=False)]
  transfers between devices with their start and end apart: 91 -> 69, of which waited for: 42 -> 27; matrix products, arithmetic and copies ran while one was open for 26% -> 22% of each run, Pallas kernels for 4% -> 37%
where the time goes in v2:
time: 518 us; the launch traced here: 510 us
  Pallas kernels  199 us (38%)
  waiting for transfers between devices  96.4 us (19%)
  other arithmetic  86.1 us (17%)
  starting transfers between devices  59.8 us (12%)
  local copies, waits for them, and re-layouts  52.3 us (10%)
  between operations  16.6 us (3%)
    ppermute x66, waiting for transfers between devices, swap(): return lax.ppermute(values, axis, [(i, i ^ bits) for i in range(size)])  88.8 us
    pallas_call x4, Pallas kernels, run_forward(): pl.pallas_call(functools.partial(forward_kernel, count_a, count_b), grid_...  64 us
    ppermute x66, starting transfers between devices, swap(): return lax.ppermute(values, axis, [(i, i ^ bits) for i in range(size)])  59.5 us
    pallas_call x4, Pallas kernels, run_attention_backward(): pl.pallas_call(functools.partial(attention_backward_kernel, len(pieces)),...  55.4 us
    pallas_call x4, Pallas kernels, run_mlp_backward(): pl.pallas_call(functools.partial(mlp_backward_kernel, len(pieces)), grid_...  32 us
    pallas_call x2, Pallas kernels, run_mlp_outer(): pl.pallas_call(functools.partial(mlp_outer_kernel, len(groups[0]), len(sh...  23.2 us
    pallas_call x2, Pallas kernels, run_qkv_outer(): pl.pallas_call(functools.partial(qkv_outer_kernel, len(groups[0]), len(sh...  12.8 us
  transfers between devices with their start and end apart: 69, of which 27 were waited for; matrix products, arithmetic and copies ran while one was open for 22% of the time, Pallas kernels for 37%

profile of v2, /device:TPU:0, one launch (start us, length us, event | category | flops | bytes accessed | tf_op | source)
XLA Modules:
  0.0 510.0 jit_solution(8558601900829844848)
XLA Ops:
  10.1 2.9 collective-permute-start.8
  14.6 2.6 collective-permute-start.4
  26.0 2.5 multiply_sine_fusion
  33.2 2.4 concatenate.72.refs_4_.refs_3_
  35.6 2.5 concatenate.73.refs_5_.refs_4_
  41.1 2.1 concatenate.78.refs_0_
  49.1 1.8 subtract_multiply_fusion
  51.1 1.6 collective-permute-start.9
  53.8 5.6 %collective-permute-done.9 = bf16[192,192]{1,0:T(8,128)(2,1)S(1)} collective-permute-done((bf16[192,192]{1,0:T(8,128)(2,1)S(1)}, bf16[192,192]{1,0:T(8,128)(2,1)S(1)}, u32[]{:S(2)}, u32[]{:S(2)}) %collective-permute-start.9) | collective-permute-done | bytes 73760 | tf_op jit(solution)/shard_map/ppermute | solution.py:63
  59.4 3.0 collective-permute-done.10
  65.5 7.5 %all-gather.6.cloned.1.call-done = bf16[1,768,1536]{2,1,0:T(8,128)(2,1)} async-done(((bf16[1,96,1536]{2,1,0:T(8,128)(2,1)}), bf16[1,768,1536]{2,1,0:T(8,128)(2,1)}) %all-gather.6.cloned.1.call-update) | async-done | bytes 2359312 | tf_op jit(solution)/shard_map/all_gather | solution.py:950
  73.4 15.8 %layer_forward.4 = (f32[2,192,768]{2,1,0:T(8,128)}, bf16[2,192,768]{2,1,0:T(8,128)(2,1)}, bf16[768,768]{1,0:T(8,128)(2,1)}, bf16[768,384]{1,0:T(8,128)(2,1)}, bf...) custom-call(s32[3]{0:T(128)} %pad_add_fusion.place, ...), custom_call_target="tpu_custom_call" | custom-call | flops 12999999488 | bytes 13000000 | tf_op jit(solution)/shard_map/layer_forward/pallas_call | solution.py:630
  93.2 16.1 %layer_forward.5 = (f32[2,192,768]{2,1,0:T(8,128)}, bf16[2,192,768]{2,1,0:T(8,128)(2,1)}, bf16[768,768]{1,0:T(8,128)(2,1)}, bf16[768,384]{1,0:T(8,128)(2,1)}, bf...) custom-call(s32[3]{0:T(128)} %pad_add_fusion.place, ...), custom_call_target="tpu_custom_call" | custom-call | flops 12999999488 | bytes 13000000 | tf_op jit(solution)/shard_map/layer_forward/pallas_call | solution.py:630
  117.4 2.5 slice_bitcast_fusion.9
  119.9 9.1 %collective-permute-done.13 = bf16[2,192,768]{2,1,0:T(8,128)(2,1)S(1)} collective-permute-done((bf16[2,192,768]{2,1,0:T(8,128)(2,1)S(1)}, bf16[2,192,768]{2,1,0:T(8,128)(2,1)S(1)}, u32[]{:S(2)}, u32[]{:S(2)}) %collective-permute-start.13) | collective-permute-done | bytes 589856 | tf_op jit(solution)/shard_map/ppermute | solution.py:63
  128.9 11.8 %collective-permute-done.21 = bf16[2,192,768]{2,1,0:T(8,128)(2,1)S(1)} collective-permute-done((bf16[2,192,768]{2,1,0:T(8,128)(2,1)S(1)}, bf16[2,192,768]{2,1,0:T(8,128)(2,1)S(1)}, u32[]{:S(2)}, u32[]{:S(2)}) %collective-permute-start.21) | collective-permute-done | bytes 589856 | tf_op jit(solution)/shard_map/ppermute | solution.py:63
  146.6 2.2 collective-permute-done.15
  148.8 2.4 collective-permute-done.16
  152.1 16.2 %layer_forward.6 = (f32[2,192,768]{2,1,0:T(8,128)}, bf16[2,192,768]{2,1,0:T(8,128)(2,1)}, bf16[768,768]{1,0:T(8,128)(2,1)}, bf16[768,384]{1,0:T(8,128)(2,1)}, bf...) custom-call(s32[3]{0:T(128)} %pad_add_fusion.place, ...), custom_call_target="tpu_custom_call" | custom-call | flops 12999999488 | bytes 13000000 | tf_op jit(solution)/shard_map/layer_forward/pallas_call | solution.py:630
  168.4 7.9 %mlp_backward.4 = (bf16[768,768]{1,0:T(8,128)(2,1)}, bf16[768,768]{1,0:T(8,128)(2,1)}, f32[768,768]{1,0:T(8,128)}, f32[8,768]{1,0:T(8,128)}) custom-call(s32[3]{0:T(128)} %pad_add_fusion.place, bf16[2,192,768]{2,1,0:T(8,128)(2,1)} %get-tuple-element.286.refs_0_, bf16[2,192,768]{2,1,0:T(8,128)(2,1)} %get-tuple-element.284.refs_1_, ...), custom_call_target="tpu_custom_call" | custom-call | flops 6000000000 | bytes 6000000 | tf_op jit(solution)/shard_map/mlp_backward/pallas_call | solution.py:672
  176.4 13.7 %attention_backward.4 = (f32[2,192,768]{2,1,0:T(8,128)}, bf16[2,192,768]{2,1,0:T(8,128)(2,1)}, bf16[768,576]{1,0:T(8,128)(2,1)}, f32[8,768]{1,0:T(8,128)}) custom-call(s32[3]{0:T(128)} %pad_add_fusion.place, bf16[768,768]{1,0:T(8,128)(2,1)} %get-tuple-element.105.refs_0_.refs_2_, f32[8,768]{1,0:T(8,128)} %stack.131.refs_2_.refs_1_.vec, ...), custom_call_target="tpu_custom_call" | custom-call | flops 11000000512 | bytes 11000000 | tf_op jit(solution)/shard_map/attention_backward/pallas_call | solution.py:720
  191.4 15.9 %layer_forward.7 = (f32[2,192,768]{2,1,0:T(8,128)}, bf16[2,192,768]{2,1,0:T(8,128)(2,1)}, bf16[768,768]{1,0:T(8,128)(2,1)}, bf16[768,384]{1,0:T(8,128)(2,1)}, bf...) custom-call(s32[3]{0:T(128)} %pad_add_fusion.place, ...), custom_call_target="tpu_custom_call" | custom-call | flops 12999999488 | bytes 13000000 | tf_op jit(solution)/shard_map/layer_forward/pallas_call | solution.py:630
  211.7 8.0 %mlp_backward.6 = (bf16[768,768]{1,0:T(8,128)(2,1)}, bf16[768,768]{1,0:T(8,128)(2,1)}, f32[768,768]{1,0:T(8,128)}, f32[8,768]{1,0:T(8,128)}) custom-call(s32[3]{0:T(128)} %pad_add_fusion.place, bf16[2,192,768]{2,1,0:T(8,128)(2,1)} %get-tuple-element.287.refs_0_, bf16[2,192,768]{2,1,0:T(8,128)(2,1)} %get-tuple-element.285.refs_1_, ...), custom_call_target="tpu_custom_call" | custom-call | flops 6000000000 | bytes 6000000 | tf_op jit(solution)/shard_map/mlp_backward/pallas_call | solution.py:672
  224.3 13.8 %attention_backward.5 = (f32[2,192,768]{2,1,0:T(8,128)}, bf16[2,192,768]{2,1,0:T(8,128)(2,1)}, bf16[768,576]{1,0:T(8,128)(2,1)}, f32[8,768]{1,0:T(8,128)}) custom-call(s32[3]{0:T(128)} %pad_add_fusion.place, bf16[768,768]{1,0:T(8,128)(2,1)} %get-tuple-element.122.refs_0_.refs_3_, f32[8,768]{1,0:T(8,128)} %stack.131.refs_2_.refs_1_.vec, ...), custom_call_target="tpu_custom_call" | custom-call | flops 11000000512 | bytes 11000000 | tf_op jit(solution)/shard_map/attention_backward/pallas_call | solution.py:720
  243.1 1.8 dynamic_update_slice.14
  251.2 2.1 fusion.9.refs_10_
  254.1 10.3 %mlp_outer.3 = (bf16[768,2304]{1,0:T(8,128)(2,1)}, bf16[192,768]{1,0:T(8,128)(2,1)}) custom-call(s32[3]{0:T(128)} %pad_add_fusion.1.scalars, f32[8,768]{1,0:T(8,128)} %stack.131.refs_2_.refs_1_.vec, bf16[768,768]{1,0:T(8,128)(2,1)} %get-tuple-element.103.refs_3_.refs_6_.refs_0_, bf16[768,768]{1,0:T(8,128)(2,1)} %get-tuple-element.120.refs_3_.refs_6_.refs_1_, ...), custom_call_target="tpu_custom_call" | custom-call | flops 10000000000 | bytes 10000000 | tf_op jit(solution)/shard_map/mlp_outer/pallas_call | solution.py:777
  264.5 2.1 reshape.404
  266.6 2.4 constant_dynamic-slice_fusion
  271.2 2.8 fusion.74
  274.5 1.8 collective-permute-done.54
  277.2 1.8 fusion.69
  279.1 2.9 fusion.73
  282.0 6.0 %qkv_outer.3 = bf16[768,2304]{1,0:T(8,128)(2,1)} custom-call(s32[3]{0:T(128)} %pad_add_fusion.1.scalars, f32[8,768]{1,0:T(8,128)} %stack.131.refs_2_.refs_1_.vec, bf16[768,768]{1,0:T(8,128)(2,1)} %get-tuple-element.103.refs_3_.refs_6_.refs_0_, bf16[768,768]{1,0:T(8,128)(2,1)} %get-tuple-element.120.refs_3_.refs_6_.refs_1_, ...), custom_call_target="tpu_custom_call", output_to_operand_aliasing={{}: (7, {})} | custom-call | flops 6000000000 | bytes 6000000 | tf_op jit(solution)/shard_map/qkv_outer/pallas_call | solution.py:802
  288.9 7.9 %mlp_backward.5 = (bf16[768,768]{1,0:T(8,128)(2,1)}, bf16[768,768]{1,0:T(8,128)(2,1)}, f32[768,768]{1,0:T(8,128)}, f32[8,768]{1,0:T(8,128)}) custom-call(s32[3]{0:T(128)} %pad_add_fusion.place, bf16[2,192,768]{2,1,0:T(8,128)(2,1)} %get-tuple-element.256.refs_0_, bf16[2,192,768]{2,1,0:T(8,128)(2,1)} %copy-done.85, f32[8,768]{1,0:T(8,128)} %stack.129.refs_2_.vec.refs_1_, ...), custom_call_target="tpu_custom_call" | custom-call | flops 6000000000 | bytes 6000000 | tf_op jit(solution)/shard_map/mlp_backward/pallas_call | solution.py:672
  297.6 8.1 %mlp_backward.7 = (bf16[768,768]{1,0:T(8,128)(2,1)}, bf16[768,768]{1,0:T(8,128)(2,1)}, f32[768,768]{1,0:T(8,128)}, f32[8,768]{1,0:T(8,128)}) custom-call(s32[3]{0:T(128)} %pad_add_fusion.place, bf16[2,192,768]{2,1,0:T(8,128)(2,1)} %copy-done.33, bf16[2,192,768]{2,1,0:T(8,128)(2,1)} %copy-done.87, f32[8,768]{1,0:T(8,128)} %stack.129.refs_2_.vec.refs_1_, ...), custom_call_target="tpu_custom_call" | custom-call | flops 6000000000 | bytes 6000000 | tf_op jit(solution)/shard_map/mlp_backward/pallas_call | solution.py:672
  305.7 12.8 %mlp_outer.2 = (f32[4,96,1536]{2,1,0:T(8,128)}, bf16[4,96,1536]{2,1,0:T(8,128)(2,1)}, bf16[192,768]{1,0:T(8,128)(2,1)}) custom-call(s32[3]{0:T(128)} %pad_add_fusion.1.scalars, f32[8,768]{1,0:T(8,128)} %stack.129.refs_2_.vec.refs_1_, bf16[768,768]{1,0:T(8,128)(2,1)} %get-tuple-element.112.refs_3_.refs_0_.refs_6_, ...), custom_call_target="tpu_custom_call" | custom-call | flops 10000000000 | bytes 10000000 | tf_op jit(solution)/shard_map/mlp_outer/pallas_call | solution.py:777
  319.2 13.9 %attention_backward.6 = (f32[2,192,768]{2,1,0:T(8,128)}, bf16[2,192,768]{2,1,0:T(8,128)(2,1)}, bf16[768,576]{1,0:T(8,128)(2,1)}, f32[8,768]{1,0:T(8,128)}) custom-call(s32[3]{0:T(128)} %pad_add_fusion.place, bf16[768,768]{1,0:T(8,128)(2,1)} %get-tuple-element.114.refs_2_.refs_0_, f32[8,768]{1,0:T(8,128)} %stack.129.refs_2_.vec.refs_1_, ...), custom_call_target="tpu_custom_call" | custom-call | flops 11000000512 | bytes 11000000 | tf_op jit(solution)/shard_map/attention_backward/pallas_call | solution.py:720
  336.9 2.7 collective-permute-done.46
  339.6 2.4 collective-permute-done.47
  342.1 14.7 %collective-permute-done.35 = bf16[4,96,1536]{2,1,0:T(8,128)(2,1)S(1)} collective-permute-done((bf16[4,96,1536]{2,1,0:T(8,128)(2,1)}, bf16[4,96,1536]{2,1,0:T(8,128)(2,1)S(1)}, u32[]{:S(2)}, u32[]{:S(2)}) %collective-permute-start.35) | collective-permute-done | bytes 1179680 | tf_op jit(solution)/shard_map/ppermute | solution.py:63
  357.8 1.6 convert_add_fusion
  360.5 14.0 %attention_backward.7 = (f32[2,192,768]{2,1,0:T(8,128)}, bf16[2,192,768]{2,1,0:T(8,128)(2,1)}, bf16[768,576]{1,0:T(8,128)(2,1)}, f32[8,768]{1,0:T(8,128)}) custom-call(s32[3]{0:T(128)} %pad_add_fusion.place, bf16[768,768]{1,0:T(8,128)(2,1)} %get-tuple-element.130.refs_3_.refs_0_, f32[8,768]{1,0:T(8,128)} %stack.129.refs_2_.vec.refs_1_, ...), custom_call_target="tpu_custom_call" | custom-call | flops 11000000512 | bytes 11000000 | tf_op jit(solution)/shard_map/attention_backward/pallas_call | solution.py:720
  390.2 6.8 %qkv_outer.2 = (f32[4,96,768]{2,1,0:T(8,128)}, bf16[4,96,768]{2,1,0:T(8,128)(2,1)}) custom-call(s32[3]{0:T(128)} %pad_add_fusion.1.scalars, f32[8,768]{1,0:T(8,128)} %stack.129.refs_2_.vec.refs_1_, bf16[768,768]{1,0:T(8,128)(2,1)} %get-tuple-element.112.refs_3_.refs_0_.refs_6_, bf16[768,768]{1,0:T(8,128)(2,1)} %get-tuple-element.119.refs_3_.refs_1_.refs_6_, ...), custom_call_target="tpu_custom_call" | custom-call | flops 6000000000 | bytes 6000000 | tf_op jit(solution)/shard_map/qkv_outer/pallas_call | solution.py:802
  397.0 5.0 collective-permute-done.41
  402.1 1.9 collective-permute-start.42
  404.9 2.6 collective-permute-done.42
  409.5 1.6 rsqrt_multiply_fusion
  421.7 1.9 collective-permute-start.45
  429.4 2.3 collective-permute-done.37
  433.1 1.9 multiply_reduce_fusion.6
  436.5 2.1 gradient.2
  438.6 7.2 %collective-permute-done.51.refs_6_ = bf16[96,768]{1,0:T(8,128)(2,1)} collective-permute-done((bf16[96,768]{1,0:T(8,128)(2,1)}, bf16[96,768]{1,0:T(8,128)(2,1)}, u32[]{:S(2)}, u32[]{:S(2)}) %collective-permute-start.51) | collective-permute-done | bytes 147488 | tf_op jit(solution)/shard_map/ppermute | solution.py:63
  445.8 2.8 gradient.3
  453.7 2.8 collective-permute-done.57
  462.3 2.5 collective-permute-done.58
  466.1 2.2 collective-permute-start.59
  471.1 2.4 collective-permute-start.60
  477.9 3.1 squares.1
  488.3 2.0 collective-permute-done.63
  490.2 2.0 collective-permute-start.64
  493.8 2.3 collective-permute-start.65
  496.1 2.2 collective-permute-done.65
  499.7 3.3 update.1
  (540 shorter events, 150.5 us)
Async XLA Ops:
  7.2 65.9 %all-gather.6.cloned.1.call-start = ((), (), s32[]{:S(2)}) async-start(), calls=%async_computation.3 | async-start | bytes 2654208 | tf_op jit(solution)/shard_map/all_gather | solution.py:950
  10.1 35.1 %collective-permute-start.8 = (bf16[96,768]{1,0:T(8,128)(2,1)}, bf16[96,768]{1,0:T(8,128)(2,1)}, u32[]{:S(2)}, u32[]{:S(2)}) collective-permute-start(bf16[96,768]{1,0:T(8,128)(2,1)} %pad_maximum_fusion.8.refs_7_.refs_11_), channel_id=1, source_target_pairs={{0,4},{4,0},{8,12},{12,8},{16,20},{20,16},{24,28},{28,24},{1,5},{5... | collective-permute-start | bytes 442376 | tf_op jit(solution)/shard_map/ppermute | solution.py:63
  13.0 16.1 %collective-permute-start.6 = (bf16[96,768]{1,0:T(8,128)(2,1)}, bf16[96,768]{1,0:T(8,128)(2,1)}, u32[]{:S(2)}, u32[]{:S(2)}) collective-permute-start(bf16[96,768]{1,0:T(8,128)(2,1)} %pad_maximum_fusion.8.refs_7_.refs_11_), channel_id=1, source_target_pairs={{0,8},{4,12},{8,0},{12,4},{16,24},{20,28},{24,16},{28,20},{1,9},{5... | collective-permute-start | bytes 442376 | tf_op jit(solution)/shard_map/ppermute | solution.py:63
  14.6 15.1 %collective-permute-start.4 = (bf16[96,768]{1,0:T(8,128)(2,1)}, bf16[96,768]{1,0:T(8,128)(2,1)}, u32[]{:S(2)}, u32[]{:S(2)}) collective-permute-start(bf16[96,768]{1,0:T(8,128)(2,1)} %pad_maximum_fusion.8.refs_7_.refs_11_), channel_id=1, source_target_pairs={{0,16},{4,20},{8,24},{12,28},{16,0},{20,4},{24,8},{28,12},{1,17},{... | collective-permute-start | bytes 442376 | tf_op jit(solution)/shard_map/ppermute | solution.py:63
  17.2 14.0 %collective-permute-start.2 = (bf16[96,768]{1,0:T(8,128)(2,1)}, bf16[96,768]{1,0:T(8,128)(2,1)}, u32[]{:S(2)}, u32[]{:S(2)}) collective-permute-start(bf16[96,768]{1,0:T(8,128)(2,1)} %pad_maximum_fusion.8.refs_7_.refs_11_), channel_id=1, source_target_pairs={{0,24},{4,28},{8,16},{12,20},{16,8},{20,12},{24,0},{28,4},{1,25},{... | collective-permute-start | bytes 442376 | tf_op jit(solution)/shard_map/ppermute | solution.py:63
  17.4 30.9 %collective-permute-start = (bf16[2,192,768]{2,1,0:T(8,128)(2,1)S(1)}, bf16[2,192,768]{2,1,0:T(8,128)(2,1)S(1)}, u32[]{:S(2)}, u32[]{:S(2)}) collective-permute-start(bf16[2,192,768]{2,1,0:T(8,128)(2,1)S(1)} %copy-done.4), channel_id=1, source_target_pairs={{0,2},{1,3},{2,0},{3,1},{4,6},{5,7},{6,4},{7,5},{8,10},{9,11},{10,... | collective-permute-start | bytes 1769480 | tf_op jit(solution)/shard_map/ppermute | solution.py:63
  19.7 122.8 %all-gather.4.cloned.1.call-start = ((), (), s32[]{:S(2)}) async-start(), calls=%async_computation.1 | async-start | bytes 3981312 | tf_op jit(solution)/shard_map/all_gather | solution.py:954
  29.1 16.7 %collective-permute-start.7 = (bf16[96,768]{1,0:T(8,128)(2,1)}, bf16[96,768]{1,0:T(8,128)(2,1)}, u32[]{:S(2)}, u32[]{:S(2)}) collective-permute-start(bf16[96,768]{1,0:T(8,128)(2,1)} %collective-permute-done.6.refs_9_.refs_13_), channel_id=1, source_target_pairs={{0,4},{4,0},{8,12},{12,8},{16,20},{20,16},{24,28},{28,24},{1,5},{5... | collective-permute-start | bytes 442376 | tf_op jit(solution)/shard_map/ppermute | solution.py:63
  29.7 16.1 %collective-permute-start.5 = (bf16[96,768]{1,0:T(8,128)(2,1)}, bf16[96,768]{1,0:T(8,128)(2,1)}, u32[]{:S(2)}, u32[]{:S(2)}) collective-permute-start(bf16[96,768]{1,0:T(8,128)(2,1)} %collective-permute-done.4.refs_11_.refs_15_), channel_id=1, source_target_pairs={{0,4},{4,0},{8,12},{12,8},{16,20},{20,16},{24,28},{28,24},{1,5},{5... | collective-permute-start | bytes 442376 | tf_op jit(solution)/shard_map/ppermute | solution.py:63
  31.2 14.7 %collective-permute-start.3 = (bf16[96,768]{1,0:T(8,128)(2,1)}, bf16[96,768]{1,0:T(8,128)(2,1)}, u32[]{:S(2)}, u32[]{:S(2)}) collective-permute-start(bf16[96,768]{1,0:T(8,128)(2,1)} %collective-permute-done.2.refs_13_.refs_17_), channel_id=1, source_target_pairs={{0,4},{4,0},{8,12},{12,8},{16,20},{20,16},{24,28},{28,24},{1,5},{5... | collective-permute-start | bytes 442376 | tf_op jit(solution)/shard_map/ppermute | solution.py:63
  45.2 45.3 %collective-permute-start.25 = (bf16[2,192,768]{2,1,0:T(8,128)(2,1)S(1)}, bf16[2,192,768]{2,1,0:T(8,128)(2,1)S(1)}, u32[]{:S(2)}, u32[]{:S(2)}) collective-permute-start(bf16[2,192,768]{2,1,0:T(8,128)(2,1)S(1)} %copy-done.20), channel_id=1, source_target_pairs={{0,2},{1,3},{2,0},{3,1},{4,6},{5,7},{6,4},{7,5},{8,10},{9,11},{10,... | collective-permute-start | bytes 1769480 | tf_op jit(solution)/shard_map/ppermute | solution.py:63
  50.9 13.5 %collective-permute-start.1 = (bf16[2,2,192,768]{3,2,1,0:T(8,128)(2,1)S(1)}, bf16[2,2,192,768]{3,2,1,0:T(8,128)(2,1)S(1)}, u32[]{:S(2)}, u32[]{:S(2)}) collective-permute-start(bf16[2,2,192,768]{3,2,1,0:T(8,128)(2,1)S(1)} %get-tuple-element.280), channel_id=1, source_target_pairs={{0,1},{1,0},{2,3},{3,2},{4,5},{5,4},{6,7},{7,6},{8,9},{9,8},{10,11... | collective-permute-start | bytes 3538952 | tf_op jit(solution)/shard_map/ppermute | solution.py:63
  51.1 8.3 %collective-permute-start.9 = (bf16[192,192]{1,0:T(8,128)(2,1)S(1)}, bf16[192,192]{1,0:T(8,128)(2,1)S(1)}, u32[]{:S(2)}, u32[]{:S(2)}) collective-permute-start(bf16[192,192]{1,0:T(8,128)(2,1)S(1)} %get-tuple-element.319), channel_id=1, source_target_pairs={{0,3},{1,2},{2,1},{3,0},{4,7},{5,6},{6,5},{7,4},{8,11},{9,10},{10,... | collective-permute-start | bytes 221192 | tf_op jit(solution)/shard_map/ppermute | solution.py:63
  52.7 9.7 %collective-permute-start.10 = (bf16[192,192]{1,0:T(8,128)(2,1)S(1)}, bf16[192,192]{1,0:T(8,128)(2,1)S(1)}, u32[]{:S(2)}, u32[]{:S(2)}) collective-permute-start(bf16[192,192]{1,0:T(8,128)(2,1)S(1)} %get-tuple-element.318), channel_id=1, source_target_pairs={{0,2},{1,3},{2,0},{3,1},{4,6},{5,7},{6,4},{7,5},{8,10},{9,11},{10,... | collective-permute-start | bytes 221192 | tf_op jit(solution)/shard_map/ppermute | solution.py:63
  53.3 9.2 %collective-permute-start.11 = (bf16[192,192]{1,0:T(8,128)(2,1)S(1)}, bf16[192,192]{1,0:T(8,128)(2,1)S(1)}, u32[]{:S(2)}, u32[]{:S(2)}) collective-permute-start(bf16[192,192]{1,0:T(8,128)(2,1)S(1)} %get-tuple-element.317), channel_id=1, source_target_pairs={{0,1},{1,0},{2,3},{3,2},{4,5},{5,4},{6,7},{7,6},{8,9},{9,8},{10,11... | collective-permute-start | bytes 221192 | tf_op jit(solution)/shard_map/ppermute | solution.py:63
  73.1 363.4 %reduce-scatter.2.cloned.1.call-start = ((), (), s32[]{:S(2)}) async-start(), calls=%async_computation.2 | async-start | bytes 3981312 | tf_op jit(solution)/shard_map/reduce_scatter | solution.py:1079
  91.7 25.7 %collective-permute-start.26 = (bf16[2,2,192,768]{3,2,1,0:T(8,128)(2,1)}, bf16[2,2,192,768]{3,2,1,0:T(8,128)(2,1)}, u32[]{:S(2)}, u32[]{:S(2)}) collective-permute-start(bf16[2,2,192,768]{3,2,1,0:T(8,128)(2,1)} %pad_maximum_fusion), channel_id=1, source_target_pairs={{0,1},{1,0},{2,3},{3,2},{4,5},{5,4},{6,7},{7,6},{8,9},{9,8},{10,11... | collective-permute-start | bytes 3538952 | tf_op jit(solution)/shard_map/ppermute | solution.py:63
  109.3 4.9 collective-permute-start.20
  112.8 16.2 %collective-permute-start.13 = (bf16[2,192,768]{2,1,0:T(8,128)(2,1)S(1)}, bf16[2,192,768]{2,1,0:T(8,128)(2,1)S(1)}, u32[]{:S(2)}, u32[]{:S(2)}) collective-permute-start(bf16[2,192,768]{2,1,0:T(8,128)(2,1)S(1)} %copy-done.37), channel_id=1, source_target_pairs={{0,2},{1,3},{2,0},{3,1},{4,6},{5,7},{6,4},{7,5},{8,10},{9,11},{10,... | collective-permute-start | bytes 1769480 | tf_op jit(solution)/shard_map/ppermute | solution.py:63
  115.1 25.7 %collective-permute-start.21 = (bf16[2,192,768]{2,1,0:T(8,128)(2,1)S(1)}, bf16[2,192,768]{2,1,0:T(8,128)(2,1)S(1)}, u32[]{:S(2)}, u32[]{:S(2)}) collective-permute-start(bf16[2,192,768]{2,1,0:T(8,128)(2,1)S(1)} %fusion.7), channel_id=1, source_target_pairs={{0,2},{1,3},{2,0},{3,1},{4,6},{5,7},{6,4},{7,5},{8,10},{9,11},{10,... | collective-permute-start | bytes 1769480 | tf_op jit(solution)/shard_map/ppermute | solution.py:63
  141.9 10.3 %collective-permute-start.14 = (bf16[2,192,768]{2,1,0:T(8,128)(2,1)S(1)}, bf16[2,192,768]{2,1,0:T(8,128)(2,1)}, u32[]{:S(2)}, u32[]{:S(2)}) collective-permute-start(bf16[2,192,768]{2,1,0:T(8,128)(2,1)S(1)} %fusion.4.refs_0_), channel_id=1, source_target_pairs={{0,1},{1,0},{2,3},{3,2},{4,5},{5,4},{6,7},{7,6},{8,9},{9,8},{10,11... | collective-permute-start | bytes 1769480 | tf_op jit(solution)/shard_map/ppermute | solution.py:63
  143.9 4.9 collective-permute-start.15
  145.2 6.0 %collective-permute-start.16 = (bf16[192,192]{1,0:T(8,128)(2,1)S(1)}, bf16[192,192]{1,0:T(8,128)(2,1)S(1)}, u32[]{:S(2)}, u32[]{:S(2)}) collective-permute-start(bf16[192,192]{1,0:T(8,128)(2,1)S(1)} %get-tuple-element.315), channel_id=1, source_target_pairs={{0,2},{1,3},{2,0},{3,1},{4,6},{5,7},{6,4},{7,5},{8,10},{9,11},{10,... | collective-permute-start | bytes 221192 | tf_op jit(solution)/shard_map/ppermute | solution.py:63
  145.8 5.4 %collective-permute-start.17 = (bf16[192,192]{1,0:T(8,128)(2,1)S(1)}, bf16[192,192]{1,0:T(8,128)(2,1)S(1)}, u32[]{:S(2)}, u32[]{:S(2)}) collective-permute-start(bf16[192,192]{1,0:T(8,128)(2,1)S(1)} %get-tuple-element.314), channel_id=1, source_target_pairs={{0,1},{1,0},{2,3},{3,2},{4,5},{5,4},{6,7},{7,6},{8,9},{9,8},{10,11... | collective-permute-start | bytes 221192 | tf_op jit(solution)/shard_map/ppermute | solution.py:63
  146.1 44.5 %collective-permute-start.22 = (bf16[2,192,768]{2,1,0:T(8,128)(2,1)S(1)}, bf16[2,192,768]{2,1,0:T(8,128)(2,1)S(1)}, u32[]{:S(2)}, u32[]{:S(2)}) collective-permute-start(bf16[2,192,768]{2,1,0:T(8,128)(2,1)S(1)} %fusion.5.refs_0_), channel_id=1, source_target_pairs={{0,1},{1,0},{2,3},{3,2},{4,5},{5,4},{6,7},{7,6},{8,9},{9,8},{10,11... | collective-permute-start | bytes 1769480 | tf_op jit(solution)/shard_map/ppermute | solution.py:63
  168.4 39.1 %collective-permute-start.18 = (bf16[2,192,768]{2,1,0:T(8,128)(2,1)}, bf16[2,192,768]{2,1,0:T(8,128)(2,1)S(1)}, u32[]{:S(2)}, u32[]{:S(2)}) collective-permute-start(bf16[2,192,768]{2,1,0:T(8,128)(2,1)} %get-tuple-element.99), channel_id=1, source_target_pairs={{0,1},{1,0},{2,3},{3,2},{4,5},{5,4},{6,7},{7,6},{8,9},{9,8},{10,11... | collective-permute-start | bytes 1769480 | tf_op jit(solution)/shard_map/ppermute | solution.py:63
  190.0 19.8 %collective-permute-start.27 = (bf16[2,192,768]{2,1,0:T(8,128)(2,1)}, bf16[2,192,768]{2,1,0:T(8,128)(2,1)S(1)}, u32[]{:S(2)}, u32[]{:S(2)}) collective-permute-start(bf16[2,192,768]{2,1,0:T(8,128)(2,1)} %get-tuple-element.111), channel_id=1, source_target_pairs={{0,1},{1,0},{2,3},{3,2},{4,5},{5,4},{6,7},{7,6},{8,9},{9,8},{10,11... | collective-permute-start | bytes 1769480 | tf_op jit(solution)/shard_map/ppermute | solution.py:63
  207.3 13.9 %collective-permute-start.23 = (bf16[2,192,768]{2,1,0:T(8,128)(2,1)}, bf16[2,192,768]{2,1,0:T(8,128)(2,1)S(1)}, u32[]{:S(2)}, u32[]{:S(2)}) collective-permute-start(bf16[2,192,768]{2,1,0:T(8,128)(2,1)} %get-tuple-element.102), channel_id=1, source_target_pairs={{0,1},{1,0},{2,3},{3,2},{4,5},{5,4},{6,7},{7,6},{8,9},{9,8},{10,11... | collective-permute-start | bytes 1769480 | tf_op jit(solution)/shard_map/ppermute | solution.py:63
  208.3 37.3 %collective-permute-start.19 = (bf16[192,768]{1,0:T(8,128)(2,1)}, bf16[192,768]{1,0:T(8,128)(2,1)}, u32[]{:S(2)}, u32[]{:S(2)}) collective-permute-start(bf16[192,768]{1,0:T(8,128)(2,1)} %fusion.33), channel_id=1, source_target_pairs={{0,2},{1,3},{2,0},{3,1},{4,6},{5,7},{6,4},{7,5},{8,10},{9,11},{10,... | collective-permute-start | bytes 884744 | tf_op jit(solution)/shard_map/ppermute | solution.py:63
  210.8 37.3 %collective-permute-start.28 = (bf16[2,192,768]{2,1,0:T(8,128)(2,1)}, bf16[2,192,768]{2,1,0:T(8,128)(2,1)}, u32[]{:S(2)}, u32[]{:S(2)}) collective-permute-start(bf16[2,192,768]{2,1,0:T(8,128)(2,1)} %fusion.8.refs_6_), channel_id=1, source_target_pairs={{0,2},{1,3},{2,0},{3,1},{4,6},{5,7},{6,4},{7,5},{8,10},{9,11},{10,... | collective-permute-start | bytes 1769480 | tf_op jit(solution)/shard_map/ppermute | solution.py:63
  223.1 22.5 %collective-permute-start.24 = (bf16[192,768]{1,0:T(8,128)(2,1)}, bf16[192,768]{1,0:T(8,128)(2,1)}, u32[]{:S(2)}, u32[]{:S(2)}) collective-permute-start(bf16[192,768]{1,0:T(8,128)(2,1)} %fusion.35), channel_id=1, source_target_pairs={{0,2},{1,3},{2,0},{3,1},{4,6},{5,7},{6,4},{7,5},{8,10},{9,11},{10,... | collective-permute-start | bytes 884744 | tf_op jit(solution)/shard_map/ppermute | solution.py:63
  238.1 13.1 %collective-permute-start.30 = (bf16[2,192,768]{2,1,0:T(8,128)(2,1)}, bf16[2,192,768]{2,1,0:T(8,128)(2,1)}, u32[]{:S(2)}, u32[]{:S(2)}) collective-permute-start(bf16[2,192,768]{2,1,0:T(8,128)(2,1)} %get-tuple-element.128), channel_id=1, source_target_pairs={{0,1},{1,0},{2,3},{3,2},{4,5},{5,4},{6,7},{7,6},{8,9},{9,8},{10,11... | collective-permute-start | bytes 1769480 | tf_op jit(solution)/shard_map/ppermute | solution.py:63
  253.3 23.9 %collective-permute-start.31 = (bf16[2,192,768]{2,1,0:T(8,128)(2,1)}, bf16[2,192,768]{2,1,0:T(8,128)(2,1)}, u32[]{:S(2)}, u32[]{:S(2)}) collective-permute-start(bf16[2,192,768]{2,1,0:T(8,128)(2,1)} %fusion.9.refs_10_), channel_id=1, source_target_pairs={{0,2},{1,3},{2,0},{3,1},{4,6},{5,7},{6,4},{7,5},{8,10},{9,11},{10,... | collective-permute-start | bytes 1769480 | tf_op jit(solution)/shard_map/ppermute | solution.py:63
  269.1 5.5 %collective-permute-start.53 = (bf16[192,192]{1,0:T(8,128)(2,1)S(1)}, bf16[192,192]{1,0:T(8,128)(2,1)S(1)}, u32[]{:S(2)}, u32[]{:S(2)}) collective-permute-start(bf16[192,192]{1,0:T(8,128)(2,1)S(1)} %bitcast.355), channel_id=1, source_target_pairs={{0,3},{1,2},{2,1},{3,0},{4,7},{5,6},{6,5},{7,4},{8,11},{9,10},{10,... | collective-permute-start | bytes 221192 | tf_op jit(solution)/shard_map/ppermute | solution.py:63
  270.3 6.1 %collective-permute-start.54 = (bf16[192,192]{1,0:T(8,128)(2,1)S(1)}, bf16[192,192]{1,0:T(8,128)(2,1)S(1)}, u32[]{:S(2)}, u32[]{:S(2)}) collective-permute-start(bf16[192,192]{1,0:T(8,128)(2,1)S(1)} %bitcast.357), channel_id=1, source_target_pairs={{0,2},{1,3},{2,0},{3,1},{4,6},{5,7},{6,4},{7,5},{8,10},{9,11},{10,... | collective-permute-start | bytes 221192 | tf_op jit(solution)/shard_map/ppermute | solution.py:63
  271.1 5.2 %collective-permute-start.55 = (bf16[192,192]{1,0:T(8,128)(2,1)S(1)}, bf16[192,192]{1,0:T(8,128)(2,1)S(1)}, u32[]{:S(2)}, u32[]{:S(2)}) collective-permute-start(bf16[192,192]{1,0:T(8,128)(2,1)S(1)} %bitcast.359), channel_id=1, source_target_pairs={{0,1},{1,0},{2,3},{3,2},{4,5},{5,4},{6,7},{7,6},{8,9},{9,8},{10,11... | collective-permute-start | bytes 221192 | tf_op jit(solution)/shard_map/ppermute | solution.py:63
  274.1 14.0 %collective-permute-start.29 = (bf16[2,192,768]{2,1,0:T(8,128)(2,1)}, bf16[2,192,768]{2,1,0:T(8,128)(2,1)S(1)}, u32[]{:S(2)}, u32[]{:S(2)}) collective-permute-start(bf16[2,192,768]{2,1,0:T(8,128)(2,1)} %get-tuple-element.256.refs_0_), channel_id=1, source_target_pairs={{0,1},{1,0},{2,3},{3,2},{4,5},{5,4},{6,7},{7,6},{8,9},{9,8},{10,11... | collective-permute-start | bytes 1769480 | tf_op jit(solution)/shard_map/ppermute | solution.py:63
  282.0 14.8 %collective-permute-start.32 = (bf16[2,192,768]{2,1,0:T(8,128)(2,1)S(1)}, bf16[2,192,768]{2,1,0:T(8,128)(2,1)S(1)}, u32[]{:S(2)}, u32[]{:S(2)}) collective-permute-start(bf16[2,192,768]{2,1,0:T(8,128)(2,1)S(1)} %get-tuple-element.254.refs_0_), channel_id=1, source_target_pairs={{0,1},{1,0},{2,3},{3,2},{4,5},{5,4},{6,7},{7,6},{8,9},{9,8},{10,11... | collective-permute-start | bytes 1769480 | tf_op jit(solution)/shard_map/ppermute | solution.py:63
  318.6 38.2 %collective-permute-start.35 = (bf16[4,96,1536]{2,1,0:T(8,128)(2,1)}, bf16[4,96,1536]{2,1,0:T(8,128)(2,1)S(1)}, u32[]{:S(2)}, u32[]{:S(2)}) collective-permute-start(bf16[4,96,1536]{2,1,0:T(8,128)(2,1)} %get-tuple-element.137.refs_19_), channel_id=1, source_target_pairs={{0,4},{4,0},{8,12},{12,8},{16,20},{20,16},{24,28},{28,24},{1,5},{5... | collective-permute-start | bytes 3538952 | tf_op jit(solution)/shard_map/ppermute | solution.py:63
  333.1 46.6 %collective-permute-start.33 = (bf16[2,192,768]{2,1,0:T(8,128)(2,1)}, bf16[2,192,768]{2,1,0:T(8,128)(2,1)}, u32[]{:S(2)}, u32[]{:S(2)}) collective-permute-start(bf16[2,192,768]{2,1,0:T(8,128)(2,1)} %get-tuple-element.139), channel_id=1, source_target_pairs={{0,1},{1,0},{2,3},{3,2},{4,5},{5,4},{6,7},{7,6},{8,9},{9,8},{10,11... | collective-permute-start | bytes 1769480 | tf_op jit(solution)/shard_map/ppermute | solution.py:63
  334.7 4.9 collective-permute-start.46
  335.7 6.3 %collective-permute-start.47 = (bf16[192,192]{1,0:T(8,128)(2,1)S(1)}, bf16[192,192]{1,0:T(8,128)(2,1)S(1)}, u32[]{:S(2)}, u32[]{:S(2)}) collective-permute-start(bf16[192,192]{1,0:T(8,128)(2,1)S(1)} %bitcast.358), channel_id=1, source_target_pairs={{0,2},{1,3},{2,0},{3,1},{4,6},{5,7},{6,4},{7,5},{8,10},{9,11},{10,... | collective-permute-start | bytes 221192 | tf_op jit(solution)/shard_map/ppermute | solution.py:63
  336.7 5.3 %collective-permute-start.48 = (bf16[192,192]{1,0:T(8,128)(2,1)S(1)}, bf16[192,192]{1,0:T(8,128)(2,1)S(1)}, u32[]{:S(2)}, u32[]{:S(2)}) collective-permute-start(bf16[192,192]{1,0:T(8,128)(2,1)S(1)} %bitcast.360), channel_id=1, source_target_pairs={{0,1},{1,0},{2,3},{3,2},{4,5},{5,4},{6,7},{7,6},{8,9},{9,8},{10,11... | collective-permute-start | bytes 221192 | tf_op jit(solution)/shard_map/ppermute | solution.py:63
  378.2 4.6 collective-permute-start.39
  383.5 4.9 collective-permute-start.40
  384.8 43.9 %collective-permute-start.34 = (bf16[192,768]{1,0:T(8,128)(2,1)}, bf16[192,768]{1,0:T(8,128)(2,1)}, u32[]{:S(2)}, u32[]{:S(2)}) collective-permute-start(bf16[192,768]{1,0:T(8,128)(2,1)} %fusion.36), channel_id=1, source_target_pairs={{0,2},{1,3},{2,0},{3,1},{4,6},{5,7},{6,4},{7,5},{8,10},{9,11},{10,... | collective-permute-start | bytes 884744 | tf_op jit(solution)/shard_map/ppermute | solution.py:63
  386.0 48.9 %collective-permute-start.43 = (bf16[96,1536]{1,0:T(8,128)(2,1)}, bf16[96,1536]{1,0:T(8,128)(2,1)}, u32[]{:S(2)}, u32[]{:S(2)}) collective-permute-start(bf16[96,1536]{1,0:T(8,128)(2,1)} %get-tuple-element.278.refs_19_), channel_id=1, source_target_pairs={{0,8},{4,12},{8,0},{12,4},{16,24},{20,28},{24,16},{28,20},{1,9},{5... | collective-permute-start | bytes 884744 | tf_op jit(solution)/shard_map/ppermute | solution.py:63
  387.5 51.1 %collective-permute-start.44 = (bf16[96,1536]{1,0:T(8,128)(2,1)}, bf16[96,1536]{1,0:T(8,128)(2,1)}, u32[]{:S(2)}, u32[]{:S(2)}) collective-permute-start(bf16[96,1536]{1,0:T(8,128)(2,1)} %get-tuple-element.277.refs_20_), channel_id=1, source_target_pairs={{0,16},{4,20},{8,24},{12,28},{16,0},{20,4},{24,8},{28,12},{1,17},{... | collective-permute-start | bytes 884744 | tf_op jit(solution)/shard_map/ppermute | solution.py:63
  388.4 33.3 %collective-permute-start.36 = (bf16[2,192,768]{2,1,0:T(8,128)(2,1)}, bf16[2,192,768]{2,1,0:T(8,128)(2,1)}, u32[]{:S(2)}, u32[]{:S(2)}) collective-permute-start(bf16[2,192,768]{2,1,0:T(8,128)(2,1)} %get-tuple-element.146), channel_id=1, source_target_pairs={{0,1},{1,0},{2,3},{3,2},{4,5},{5,4},{6,7},{7,6},{8,9},{9,8},{10,11... | collective-permute-start | bytes 1769480 | tf_op jit(solution)/shard_map/ppermute | solution.py:63
  388.7 13.3 %collective-permute-start.41 = (bf16[2,19968]{1,0:T(2,128)(2,1)S(1)}, bf16[2,19968]{1,0:T(2,128)(2,1)S(1)}, u32[]{:S(2)}, u32[]{:S(2)}) collective-permute-start(bf16[2,19968]{1,0:T(2,128)(2,1)S(1)} %add_convert_fusion.1), channel_id=1, source_target_pairs={{0,8},{4,12},{8,0},{12,4},{16,24},{20,28},{24,16},{28,20},{1,9},{5... | collective-permute-start | bytes 239624 | tf_op jit(solution)/shard_map/ppermute | solution.py:63
  402.1 5.4 %collective-permute-start.42 = (bf16[2,19968]{1,0:T(2,128)(2,1)S(1)}, bf16[2,19968]{1,0:T(2,128)(2,1)S(1)}, u32[]{:S(2)}, u32[]{:S(2)}) collective-permute-start(bf16[2,19968]{1,0:T(2,128)(2,1)S(1)} %add_convert_fusion), channel_id=1, source_target_pairs={{0,16},{4,20},{8,24},{12,28},{16,0},{20,4},{24,8},{28,12},{1,17},{... | collective-permute-start | bytes 239624 | tf_op jit(solution)/shard_map/ppermute | solution.py:63
  407.5 17.4 %collective-permute-start.49 = (bf16[4,96,768]{2,1,0:T(8,128)(2,1)}, bf16[4,96,768]{2,1,0:T(8,128)(2,1)S(1)}, u32[]{:S(2)}, u32[]{:S(2)}) collective-permute-start(bf16[4,96,768]{2,1,0:T(8,128)(2,1)} %get-tuple-element.159), channel_id=1, source_target_pairs={{0,4},{4,0},{8,12},{12,8},{16,20},{20,16},{24,28},{28,24},{1,5},{5... | collective-permute-start | bytes 1769480 | tf_op jit(solution)/shard_map/ppermute | solution.py:63
  421.7 16.9 %collective-permute-start.45 = (bf16[96,1536]{1,0:T(8,128)(2,1)}, bf16[96,1536]{1,0:T(8,128)(2,1)}, u32[]{:S(2)}, u32[]{:S(2)}) collective-permute-start(bf16[96,1536]{1,0:T(8,128)(2,1)} %get-tuple-element.276.refs_21_), channel_id=1, source_target_pairs={{0,24},{4,28},{8,16},{12,20},{16,8},{20,12},{24,0},{28,4},{1,25},{... | collective-permute-start | bytes 884744 | tf_op jit(solution)/shard_map/ppermute | solution.py:63
  424.9 6.8 %collective-permute-start.37 = (bf16[192,768]{1,0:T(8,128)(2,1)S(1)}, bf16[192,768]{1,0:T(8,128)(2,1)S(1)}, u32[]{:S(2)}, u32[]{:S(2)}) collective-permute-start(bf16[192,768]{1,0:T(8,128)(2,1)S(1)} %fusion.37), channel_id=1, source_target_pairs={{0,2},{1,3},{2,0},{3,1},{4,6},{5,7},{6,4},{7,5},{8,10},{9,11},{10,... | collective-permute-start | bytes 884744 | tf_op jit(solution)/shard_map/ppermute | solution.py:63
  428.7 9.9 %collective-permute-start.50 = (bf16[96,768]{1,0:T(8,128)(2,1)}, bf16[96,768]{1,0:T(8,128)(2,1)}, u32[]{:S(2)}, u32[]{:S(2)}) collective-permute-start(bf16[96,768]{1,0:T(8,128)(2,1)} %get-tuple-element.283), channel_id=1, source_target_pairs={{0,8},{4,12},{8,0},{12,4},{16,24},{20,28},{24,16},{28,20},{1,9},{5... | collective-permute-start | bytes 442376 | tf_op jit(solution)/shard_map/ppermute | solution.py:63
  431.7 14.1 %collective-permute-start.51 = (bf16[96,768]{1,0:T(8,128)(2,1)}, bf16[96,768]{1,0:T(8,128)(2,1)}, u32[]{:S(2)}, u32[]{:S(2)}) collective-permute-start(bf16[96,768]{1,0:T(8,128)(2,1)} %get-tuple-element.282), channel_id=1, source_target_pairs={{0,16},{4,20},{8,24},{12,28},{16,0},{20,4},{24,8},{28,12},{1,17},{... | collective-permute-start | bytes 442376 | tf_op jit(solution)/shard_map/ppermute | solution.py:63
  435.0 10.9 %collective-permute-start.52 = (bf16[96,768]{1,0:T(8,128)(2,1)}, bf16[96,768]{1,0:T(8,128)(2,1)}, u32[]{:S(2)}, u32[]{:S(2)}) collective-permute-start(bf16[96,768]{1,0:T(8,128)(2,1)} %get-tuple-element.281), channel_id=1, source_target_pairs={{0,24},{4,28},{8,16},{12,20},{16,8},{20,12},{24,0},{28,4},{1,25},{... | collective-permute-start | bytes 442376 | tf_op jit(solution)/shard_map/ppermute | solution.py:63
  451.5 4.9 collective-permute-start.57
  460.8 4.0 collective-permute-start.58
  466.1 4.2 collective-permute-start.59
  471.1 4.7 collective-permute-start.60
  482.9 3.7 collective-permute-start.62
  490.2 3.6 collective-permute-start.64
  493.8 4.5 collective-permute-start.65
  (96 other events, 763.6 us)
Sparse Core Ops, SparseCore 0:
  19.8 53.2 all-gather.5
  75.3 63.7 all-gather.3
  288.2 87.5 reduce-scatter.1
